TPU v7x, 32 devices: a whole 2x2x4 slice. The times are simulated.
32 devices in a mesh: grp: 2 (over x), blk: 16 (over z, y, core).
Axes of the slice: x: 2, y: 2, z: 4, core: 2. Of those that a mesh axis runs over, the one named last changes fastest.
Arguments:
- features: bfloat16 [4096, 256], P(('grp', 'blk')), may hold values from -6 to 6
- dest: int32 [4096, 1], P(('grp', 'blk')), may hold values from 0 to 15; in each aligned block of 128 rows (0 to 127, 128 to 255, ...) at most 16 rows name the same one
- placement: int32 [32, 256], P(('grp', 'blk')), may hold values from 0 to 255, each once within a row
- weight: bfloat16 [27, 256, 128], replicated, may hold values from -0.078125 to 0.078125
- grad_out: bfloat16 [16, 128, 4, 128], P('grp', 'blk'), may hold values from -6 to 6
Outputs:
- output: bfloat16 [16, 128, 4, 128], P('grp', 'blk')
- grad_rows: bfloat16 [4096, 256], P(('grp', 'blk'))
- weight_grad: bfloat16 [27, 256, 128], replicated
Inputs may be any that keep to these rules, and one draw needn't show every extreme that they name: `dest`: among the rows of one device no value is named by more than 16 rows, a bound that some block reaches. `placement`: each row is a permutation of 0 to 255.
All inputs are finite; a program needn't handle non-finite values.
Results may differ from a plain program's by a relative error of at most 0.0013.
Values may be sent and summed in bfloat16 or wider, within the bound.
No kernel may reach another device: no remote copies, remote signals or barrier semaphores. Data moves between devices by JAX's collectives and lax.ppermute only.
A program may use at most 64 MiB of HBM per device.

v0:
```python
import math

import jax
import jax.numpy as jnp
from jax import lax
from jax.sharding import PartitionSpec as P


def extended(cells, sides, width):
    for axis, dim in sides:
        count = lax.axis_size(axis)
        ends = count - 1
        head = lax.slice_in_dim(cells, 0, width, axis=dim)
        tail = lax.slice_in_dim(cells, cells.shape[dim] - width, cells.shape[dim], axis=dim)
        cells = jnp.concatenate(
            [
                lax.ppermute(tail, axis, [(i, (i + 1) % count) for i in range(ends)]),
                cells,
                lax.ppermute(head, axis, [((i + 1) % count, i) for i in range(ends)]),
            ],
            axis=dim,
        )
    return cells


def shards(features, dest, placement, weight, grad_out):
    row_count, channels = features.shape
    blk_count = lax.axis_size("blk")
    grp_count = lax.axis_size("grp")
    voxel_of_slot = placement[0]
    voxel_count = voxel_of_slot.shape[0]
    capacity = voxel_count // blk_count
    size_x, size_y, size_z, out_channels = grad_out.shape
    target = dest[:, 0]
    owners = jnp.arange(blk_count, dtype=jnp.int32)
    one_hot = (target[:, None] == owners[None, :]).astype(jnp.int32)
    slot_rank = jnp.sum((jnp.cumsum(one_hot, axis=0) - one_hot) * one_hot, axis=1)
    send_counts = jnp.sum(one_hot, axis=0).reshape(blk_count, 1)
    slot_index = target * capacity + slot_rank
    outgoing = jnp.zeros((voxel_count, channels), jnp.bfloat16).at[slot_index].set(features)
    incoming, recv_counts = (
        lax.all_to_all(
            outgoing.reshape(blk_count, capacity, channels),
            "blk",
            split_axis=0,
            concat_axis=0,
            tiled=True,
        ),
        lax.all_to_all(send_counts, "blk", split_axis=0, concat_axis=0, tiled=True),
    )
    filled = (
        (jnp.arange(capacity, dtype=jnp.int32)[None, :] < recv_counts)
        .reshape(-1)
        .astype(jnp.float32)
    )
    voxel_rows = (
        jnp.zeros((voxel_count, channels), jnp.bfloat16)
        .at[voxel_of_slot]
        .set(incoming.reshape(voxel_count, channels))
    )
    occupied = jnp.zeros((voxel_count,), jnp.float32).at[voxel_of_slot].set(filled)[:, None]
    voxel_grid = voxel_rows.reshape(size_x, size_y, size_z, channels)
    padded = extended(voxel_grid, (("grp", 0), ("blk", 1)), 1)
    padded = jnp.pad(padded, ((0, 0), (0, 0), (1, 1), (0, 0)))
    shifted = []
    total = jnp.zeros((voxel_count, out_channels), jnp.float32)
    for offset in range(27):
        shift_x, shift_y, shift_z = (offset // 9, offset // 3 % 3, offset % 3)
        window = padded[
            shift_x : shift_x + size_x, shift_y : shift_y + size_y, shift_z : shift_z + size_z
        ].reshape(voxel_count, channels)
        shifted.append(window)
        total = total + jnp.dot(window, weight[offset], preferred_element_type=jnp.float32)
    output = (total * occupied).astype(jnp.bfloat16).reshape(size_x, size_y, size_z, out_channels)
    masked_grad = (
        grad_out.reshape(voxel_count, out_channels).astype(jnp.float32) * occupied
    ).astype(jnp.bfloat16)
    grad_padded = extended(
        masked_grad.reshape(size_x, size_y, size_z, out_channels), (("grp", 0), ("blk", 1)), 1
    )
    grad_padded = jnp.pad(grad_padded, ((0, 0), (0, 0), (1, 1), (0, 0)))
    back_total = jnp.zeros((voxel_count, channels), jnp.float32)
    partials = []
    for offset in range(27):
        shift_x, shift_y, shift_z = (offset // 9, offset // 3 % 3, offset % 3)
        window = grad_padded[
            2 - shift_x : 2 - shift_x + size_x,
            2 - shift_y : 2 - shift_y + size_y,
            2 - shift_z : 2 - shift_z + size_z,
        ].reshape(voxel_count, out_channels)
        back_total = back_total + lax.dot_general(
            window, weight[offset], (((1,), (1,)), ((), ())), preferred_element_type=jnp.float32
        )
        partials.append(
            lax.dot_general(
                shifted[offset],
                masked_grad,
                (((0,), (0,)), ((), ())),
                preferred_element_type=jnp.float32,
            )
        )
    grad_grid = (back_total * occupied).astype(jnp.bfloat16)
    weight_terms = jnp.stack(partials).reshape(27 * channels, out_channels)
    grad_scale = 1.0 / math.sqrt(row_count * blk_count * grp_count)
    weight_grad = (lax.psum(weight_terms, ("grp", "blk")) * grad_scale).astype(jnp.bfloat16)
    weight_grad = weight_grad.reshape(27, channels, out_channels)
    returning = grad_grid[voxel_of_slot].reshape(blk_count, capacity, channels)
    returned = lax.all_to_all(returning, "blk", split_axis=0, concat_axis=0, tiled=True)
    grad_rows = returned.reshape(voxel_count, channels)[slot_index]
    return (output, grad_rows, weight_grad)


def solution(mesh):
    in_specs = (
        P(("grp", "blk"), None),
        P(("grp", "blk"), None),
        P(("grp", "blk"), None),
        P(),
        P("grp", "blk", None, None),
    )
    out_specs = (P("grp", "blk", None, None), P(("grp", "blk"), None), P())
    return jax.shard_map(shards, mesh=mesh, in_specs=in_specs, out_specs=out_specs, check_vma=False)
```

profile of v0, /device:TPU:0, one launch (start us, length us, event | category | flops | bytes accessed | tf_op | source)
XLA Modules:
  0.0 311.8 jit_solution(5456722468034964877)
XLA Ops:
  9.6 7.4 %all-to-all-start.1 = ((s32[16,1,1]{2,1,0:T(1,128)}), s32[16,1,1]{2,1,0:T(1,128)S(1)}, u32[]{:S(2)}, u32[]{:S(2)}) async-start(s32[16,1,1]{2,1,0:T(1,128)} %copy.183), calls=%async_computation.1 | async-start | bytes 16384 | tf_op jit(solution)/shard_map/all_to_all | solution.py:49
  18.3 2.0 scatter_custom_fusion
  20.3 3.0 all-to-all-done.1
  23.3 3.6 %all-to-all-start = ((bf16[16,16,256]{2,1,0:T(8,128)(2,1)}), bf16[16,16,256]{2,1,0:T(8,128)(2,1)S(1)}, u32[]{:S(2)}, u32[]{:S(2)}) async-start(bf16[16,16,256]{2,1,0:T(8,128)(2,1)} %bitcast.5), calls=%async_computation | async-start | bytes 262144 | tf_op jit(solution)/shard_map/all_to_all | solution.py:42
  31.3 4.5 %collective-permute-start.4 = (bf16[1,8,4,128]{3,2,1,0:T(4,128)(2,1)S(1)}, bf16[1,8,4,128]{3,2,1,0:T(4,128)(2,1)S(1)}, u32[]{:S(2)}, u32[]{:S(2)}) collective-permute-start(bf16[1,8,4,128]{3,2,1,0:T(4,128)(2,1)S(1)} %bitcast.500), channel_id=1, source_target_pairs={{0,16},{1,17},{2,18},{3,19},{4,20},{5,21},{6,22},{7,23},{8,24},{9,... | collective-permute-start | bytes 24584 | tf_op jit(solution)/shard_map/ppermute | solution.py:17
  39.9 3.7 %collective-permute-done.7 = bf16[10,1,4,128]{3,2,1,0:T(4,128)(2,1)S(1)} collective-permute-done((bf16[10,1,4,128]{3,2,1,0:T(4,128)(2,1)S(1)}, bf16[10,1,4,128]{3,2,1,0:T(4,128)(2,1)S(1)}, u32[]{:S(2)}, u32[]{:S(2)}) %collective-permute-start.7) | collective-permute-done | bytes 10272 | tf_op jit(solution)/shard_map/ppermute | solution.py:19
  51.1 4.2 %collective-permute-start = (bf16[1,8,4,256]{3,1,2,0:T(8,128)(2,1)S(1)}, bf16[1,8,4,256]{3,1,2,0:T(8,128)(2,1)S(1)}, u32[]{:S(2)}, u32[]{:S(2)}) collective-permute-start(bf16[1,8,4,256]{3,1,2,0:T(8,128)(2,1)S(1)} %copy.152), channel_id=1, source_target_pairs={{0,16},{1,17},{2,18},{3,19},{4,20},{5,21},{6,22},{7,23},{8,24},{9,... | collective-permute-start | bytes 49160 | tf_op jit(solution)/shard_map/ppermute | solution.py:17
  55.5 1.8 gather_fusion
  57.2 7.3 %all-to-all-start.2 = ((bf16[16,16,256]{2,1,0:T(8,128)(2,1)}), bf16[16,16,256]{2,1,0:T(8,128)(2,1)S(1)}, u32[]{:S(2)}, u32[]{:S(2)}) async-start(bf16[16,16,256]{2,1,0:T(8,128)(2,1)} %bitcast.66), calls=%async_computation.2 | async-start | bytes 262144 | tf_op jit(solution)/shard_map/all_to_all | solution.py:108
  66.1 4.2 %collective-permute-done.1 = bf16[1,8,4,256]{3,1,2,0:T(8,128)(2,1)S(1)} collective-permute-done((bf16[1,8,4,256]{3,1,2,0:T(8,128)(2,1)S(1)}, bf16[1,8,4,256]{3,1,2,0:T(8,128)(2,1)S(1)}, u32[]{:S(2)}, u32[]{:S(2)}) %collective-permute-start.1) | collective-permute-done | bytes 16416 | tf_op jit(solution)/shard_map/ppermute | solution.py:19
  87.4 1.6 copy.174
  94.9 1.6 copy.176
  104.5 1.6 copy.172
  109.3 1.6 reshape.396
  112.5 1.6 reshape.395
  114.1 1.6 copy.168
  117.3 1.6 copy.167
  120.5 1.6 copy.165
  123.7 1.6 copy.164
  126.9 1.6 copy.162
  130.8 1.6 reshape.387
  158.5 1.8 copy-done.2
  164.4 137.2 %all-reduce.4.cloned.1.call-done = f32[6912,128]{1,0:T(8,128)} async-done(((f32[6912,128]{1,0:T(8,128)}), f32[6912,128]{1,0:T(8,128)}) %all-reduce.4.cloned.1.call-update) | async-done | bytes 3538960 | tf_op jit(solution)/shard_map/psum | solution.py:105
  301.6 3.4 %multiply_convert_fusion = bf16[6912,128]{1,0:T(8,128)(2,1)} fusion(f32[6912,128]{1,0:T(8,128)} %all-reduce.4.cloned.1.call-done), kind=kLoop, calls=%fused_computation.5 | loop fusion | flops 1769472 | bytes 5308416 | tf_op jit(solution)/shard_map/convert_element_type | solution.py:105
  (240 shorter events, 94.7 us)
Async XLA Ops:
  9.6 13.7 %all-to-all-start.1 = ((s32[16,1,1]{2,1,0:T(1,128)}), s32[16,1,1]{2,1,0:T(1,128)S(1)}, u32[]{:S(2)}, u32[]{:S(2)}) async-start(s32[16,1,1]{2,1,0:T(1,128)} %copy.183), calls=%async_computation.1 | async-start | bytes 16384 | tf_op jit(solution)/shard_map/all_to_all | solution.py:49
  23.3 20.9 %copy-start = (bf16[27,256,128]{2,1,0:T(8,128)(2,1)S(1)}, bf16[27,256,128]{2,1,0:T(8,128)(2,1)}, u32[]{:S(2)}) copy-start(bf16[27,256,128]{2,1,0:T(8,128)(2,1)} %param.8) | copy-start | bytes 5308420
  23.3 26.2 %all-to-all-start = ((bf16[16,16,256]{2,1,0:T(8,128)(2,1)}), bf16[16,16,256]{2,1,0:T(8,128)(2,1)S(1)}, u32[]{:S(2)}, u32[]{:S(2)}) async-start(bf16[16,16,256]{2,1,0:T(8,128)(2,1)} %bitcast.5), calls=%async_computation | async-start | bytes 262144 | tf_op jit(solution)/shard_map/all_to_all | solution.py:42
  30.0 6.8 %collective-permute-start.5 = (bf16[1,8,4,128]{3,2,1,0:T(4,128)(2,1)S(1)}, bf16[1,8,4,128]{3,2,1,0:T(4,128)(2,1)S(1)}, u32[]{:S(2)}, u32[]{:S(2)}) collective-permute-start(bf16[1,8,4,128]{3,2,1,0:T(4,128)(2,1)S(1)} %bitcast.501), channel_id=1, source_target_pairs={{16,0},{17,1},{18,2},{19,3},{20,4},{21,5},{22,6},{23,7},{24,8},{25... | collective-permute-start | bytes 24584 | tf_op jit(solution)/shard_map/ppermute | solution.py:19
  31.3 5.9 %collective-permute-start.4 = (bf16[1,8,4,128]{3,2,1,0:T(4,128)(2,1)S(1)}, bf16[1,8,4,128]{3,2,1,0:T(4,128)(2,1)S(1)}, u32[]{:S(2)}, u32[]{:S(2)}) collective-permute-start(bf16[1,8,4,128]{3,2,1,0:T(4,128)(2,1)S(1)} %bitcast.500), channel_id=1, source_target_pairs={{0,16},{1,17},{2,18},{3,19},{4,20},{5,21},{6,22},{7,23},{8,24},{9,... | collective-permute-start | bytes 24584 | tf_op jit(solution)/shard_map/ppermute | solution.py:17
  37.2 2.7 collective-permute-start.6
  38.5 5.1 %collective-permute-start.7 = (bf16[10,1,4,128]{3,2,1,0:T(4,128)(2,1)S(1)}, bf16[10,1,4,128]{3,2,1,0:T(4,128)(2,1)S(1)}, u32[]{:S(2)}, u32[]{:S(2)}) collective-permute-start(bf16[10,1,4,128]{3,2,1,0:T(4,128)(2,1)S(1)} %get-tuple-element.66), channel_id=1, source_target_pairs={{1,0},{2,1},{3,2},{4,3},{5,4},{6,5},{7,6},{8,7},{9,8},{10,9},{11,1... | collective-permute-start | bytes 30728 | tf_op jit(solution)/shard_map/ppermute | solution.py:19
  51.1 15.0 %collective-permute-start = (bf16[1,8,4,256]{3,1,2,0:T(8,128)(2,1)S(1)}, bf16[1,8,4,256]{3,1,2,0:T(8,128)(2,1)S(1)}, u32[]{:S(2)}, u32[]{:S(2)}) collective-permute-start(bf16[1,8,4,256]{3,1,2,0:T(8,128)(2,1)S(1)} %copy.152), channel_id=1, source_target_pairs={{0,16},{1,17},{2,18},{3,19},{4,20},{5,21},{6,22},{7,23},{8,24},{9,... | collective-permute-start | bytes 49160 | tf_op jit(solution)/shard_map/ppermute | solution.py:17
  57.2 17.1 %all-to-all-start.2 = ((bf16[16,16,256]{2,1,0:T(8,128)(2,1)}), bf16[16,16,256]{2,1,0:T(8,128)(2,1)S(1)}, u32[]{:S(2)}, u32[]{:S(2)}) async-start(bf16[16,16,256]{2,1,0:T(8,128)(2,1)} %bitcast.66), calls=%async_computation.2 | async-start | bytes 262144 | tf_op jit(solution)/shard_map/all_to_all | solution.py:108
  64.6 237.0 %all-reduce.4.cloned.1.call-start = ((), (), s32[]{:S(2)}) async-start(), calls=%async_computation.3 | async-start | bytes 7077888 | tf_op jit(solution)/shard_map/psum | solution.py:105
  64.7 8.7 %copy-start.19 = (bf16[8,8,4,256]{3,2,1,0:T(4,128)(2,1)}, bf16[8,8,4,256]{3,2,1,0:T(4,128)(2,1)S(1)}, u32[]{:S(2)}) copy-start(bf16[8,8,4,256]{3,2,1,0:T(4,128)(2,1)S(1)} %reshape.381) | copy-start | bytes 393220
  64.7 5.6 %collective-permute-start.1 = (bf16[1,8,4,256]{3,1,2,0:T(8,128)(2,1)S(1)}, bf16[1,8,4,256]{3,1,2,0:T(8,128)(2,1)S(1)}, u32[]{:S(2)}, u32[]{:S(2)}) collective-permute-start(bf16[1,8,4,256]{3,1,2,0:T(8,128)(2,1)S(1)} %copy.153), channel_id=1, source_target_pairs={{16,0},{17,1},{18,2},{19,3},{20,4},{21,5},{22,6},{23,7},{24,8},{25... | collective-permute-start | bytes 49160 | tf_op jit(solution)/shard_map/ppermute | solution.py:19
  66.1 9.7 %copy-start.30 = (bf16[9,8,4,256]{3,1,2,0:T(8,128)(2,1)}, bf16[9,8,4,256]{3,1,2,0:T(8,128)(2,1)S(1)}, u32[]{:S(2)}) copy-start(bf16[9,8,4,256]{3,1,2,0:T(8,128)(2,1)S(1)} %get-tuple-element.53) | copy-start | bytes 442372
  70.4 5.4 %copy-start.28 = (bf16[9,8,4,256]{3,1,2,0:T(8,128)(2,1)}, bf16[9,8,4,256]{3,1,2,0:T(8,128)(2,1)S(1)}, u32[]{:S(2)}) copy-start(bf16[9,8,4,256]{3,1,2,0:T(8,128)(2,1)S(1)} %get-tuple-element.71) | copy-start | bytes 442372
  70.4 5.4 %collective-permute-start.2 = (bf16[10,1,4,256]{3,1,2,0:T(2,128)(2,1)S(1)}, bf16[10,1,4,256]{3,1,2,0:T(2,128)(2,1)S(1)}, u32[]{:S(2)}, u32[]{:S(2)}) collective-permute-start(bf16[10,1,4,256]{3,1,2,0:T(2,128)(2,1)S(1)} %get-tuple-element.50), channel_id=1, source_target_pairs={{0,1},{1,2},{2,3},{3,4},{4,5},{5,6},{6,7},{7,8},{8,9},{9,10},{10,1... | collective-permute-start | bytes 61448 | tf_op jit(solution)/shard_map/ppermute | solution.py:17
  71.9 5.1 %collective-permute-start.3 = (bf16[10,1,4,256]{3,1,2,0:T(2,128)(2,1)S(1)}, bf16[10,1,4,256]{3,1,2,0:T(2,128)(2,1)S(1)}, u32[]{:S(2)}, u32[]{:S(2)}) collective-permute-start(bf16[10,1,4,256]{3,1,2,0:T(2,128)(2,1)S(1)} %get-tuple-element.51), channel_id=1, source_target_pairs={{1,0},{2,1},{3,2},{4,3},{5,4},{6,5},{7,6},{8,7},{9,8},{10,9},{11,1... | collective-permute-start | bytes 61448 | tf_op jit(solution)/shard_map/ppermute | solution.py:19
  80.6 9.3 %copy-start.15 = (bf16[8,8,4,256]{3,1,2,0:T(8,128)(2,1)S(1)}, bf16[8,8,4,256]{3,1,2,0:T(8,128)(2,1)}, u32[]{:S(2)}) copy-start(bf16[8,8,4,256]{3,1,2,0:T(8,128)(2,1)} %get-tuple-element.5) | copy-start | bytes 393220
  130.8 15.7 %copy-start.8 = (bf16[256,256]{1,0:T(8,128)(2,1)S(1)}, bf16[256,256]{1,0:T(8,128)(2,1)}, u32[]{:S(2)}) copy-start(bf16[256,256]{1,0:T(8,128)(2,1)} %reshape.386) | copy-start | bytes 393220
  142.0 4.7 %copy-start.18 = (bf16[256,256]{1,0:T(8,128)(2,1)S(1)}, bf16[256,256]{1,0:T(8,128)(2,1)}, u32[]{:S(2)}) copy-start(bf16[256,256]{1,0:T(8,128)(2,1)} %reshape.387) | copy-start | bytes 393220
  142.0 4.9 %copy-start.17 = (bf16[256,256]{1,0:T(8,128)(2,1)S(1)}, bf16[256,256]{1,0:T(8,128)(2,1)}, u32[]{:S(2)}) copy-start(bf16[256,256]{1,0:T(8,128)(2,1)} %reshape.388) | copy-start | bytes 393220
  142.0 5.1 %copy-start.11 = (bf16[256,256]{1,0:T(8,128)(2,1)S(1)}, bf16[256,256]{1,0:T(8,128)(2,1)}, u32[]{:S(2)}) copy-start(bf16[256,256]{1,0:T(8,128)(2,1)} %reshape.389) | copy-start | bytes 393220
  142.0 5.3 %copy-start.16 = (bf16[256,256]{1,0:T(8,128)(2,1)S(1)}, bf16[256,256]{1,0:T(8,128)(2,1)}, u32[]{:S(2)}) copy-start(bf16[256,256]{1,0:T(8,128)(2,1)} %reshape.390) | copy-start | bytes 393220
  143.1 4.3 %copy-start.14 = (bf16[256,256]{1,0:T(8,128)(2,1)S(1)}, bf16[256,256]{1,0:T(8,128)(2,1)}, u32[]{:S(2)}) copy-start(bf16[256,256]{1,0:T(8,128)(2,1)} %reshape.391) | copy-start | bytes 393220
  144.2 3.4 %copy-start.10 = (bf16[256,256]{1,0:T(8,128)(2,1)S(1)}, bf16[256,256]{1,0:T(8,128)(2,1)}, u32[]{:S(2)}) copy-start(bf16[256,256]{1,0:T(8,128)(2,1)} %reshape.392) | copy-start | bytes 393220
  (20 other events, 24.6 us)
Sparse Core Ops, SparseCore 0:
  160.5 141.0 all-reduce.3
where the time goes:
time: 314 us; the launch traced here: 312 us
  waiting for transfers between devices  150 us (48%)
  local copies, waits for them, and re-layouts  80.4 us (26%)
  starting transfers between devices  35.3 us (11%)
  matrix products  20.7 us (7%)
  between operations  15.1 us (5%)
  other arithmetic  10.5 us (3%)
    psum x1, waiting for transfers between devices, shards(): lax.psum(weight_terms, ('grp', 'blk')) * grad_scale  137 us
    slice x29, local copies, waits for them, and re-layouts, shards(): padded[shift_x:shift_x + size_x, shift_y:shift_y + size_y, shift_z:shift_...  32.3 us
    reshape x26, local copies, waits for them, and re-layouts, shards(): window = padded[shift_x:shift_x + size_x, shift_y:shift_y + size_y, shift...  30.6 us
    ppermute x4, starting transfers between devices, extended(): lax.ppermute(tail, axis, [(i, (i + 1) % count) for i in range(ends)])  11.5 us
    ppermute x4, waiting for transfers between devices, extended(): lax.ppermute(head, axis, [((i + 1) % count, i) for i in range(ends)])  9.19 us
    dot_general x27, matrix products, shards(): jnp.dot(window, weight[offset], preferred_element_type=jnp.float32)  8.97 us
    unnamed x66, local copies, waits for them, and re-layouts  7.83 us
    all_to_all x1, starting transfers between devices, shards(): lax.all_to_all(send_counts, 'blk', split_axis=0, concat_axis=0, tiled=True)  7.39 us
  transfers between devices with their start and end apart: 12, of which 6 were waited for; matrix products, arithmetic and copies ran while one was open for 7% of the time, Pallas kernels for 0%

commit v1 on v0

--- a/solution.py
+++ b/solution.py
@@ -1,9 +1,365 @@
+import functools
 import math
 
 import jax
 import jax.numpy as jnp
 from jax import lax
+from jax.experimental import pallas as pl
+from jax.experimental.pallas import tpu as pltpu
 from jax.sharding import PartitionSpec as P
+
+LANES = 128
+F32, BF16, I32 = jnp.float32, jnp.bfloat16, jnp.int32
+
+
+def iota(shape, axis):
+    return lax.broadcasted_iota(I32, shape, axis)
+
+
+def one_hot(hits):
+    return jnp.where(hits, 1.0, 0.0).astype(BF16)
+
+
+def mm(a, b):
+    return lax.dot_general(a, b, (((1,), (0,)), ((), ())), preferred_element_type=F32)
+
+
+def mm_t(a, b):
+    return lax.dot_general(a, b, (((1,), (1,)), ((), ())), preferred_element_type=F32)
+
+
+def pack_kernel(sizes, cap, features, dest, placement, grad, packed, slots):
+    size_x, size_y, size_z = sizes
+    rows, channels = features.shape
+    voxels = grad.shape[0]
+    lane = iota((rows, LANES), 1)
+    target = dest[...]
+    named = one_hot(lane == target)
+    earlier = one_hot(iota((rows, rows), 0) > iota((rows, rows), 1))
+    rank = jnp.sum(mm(earlier, named) * named.astype(F32), axis=1, keepdims=True)
+    slot = target.astype(F32) * cap + rank
+    diagonal = iota((rows, rows), 0) == iota((rows, rows), 1)
+    slot_row = jnp.sum(jnp.where(diagonal, slot, 0.0), axis=0, keepdims=True)
+    slots[...] = slot_row.astype(I32)
+    at = 0
+    for c in range(0, channels, LANES):
+        packed[at : at + rows, :] = features[:, c : c + LANES]
+        at += rows
+    row, col = iota((voxels, voxels), 0), iota((voxels, voxels), 1)
+    moved = (col % size_z) * (size_x * size_y) + col // size_z
+    packed[at : at + voxels, :] = mm(one_hot(row == moved), grad[...]).astype(BF16)
+    at += voxels
+    spots = placement[...].astype(F32)
+    index_rows = [slot_row] + [spots[:, c : c + LANES] for c in range(0, voxels, LANES)]
+    index_rows.append(jnp.zeros((16 - len(index_rows), LANES), F32))
+    packed[at : at + 16, :] = jnp.concatenate(index_rows, axis=0).astype(BF16)
+
+
+def scene_kernel(
+    dims,
+    me_ref,
+    where_ref,
+    slot_ref,
+    packed,
+    weight,
+    output,
+    grad_rows,
+    weight_grad,
+    slots,
+    grid,
+    masked,
+    masked_t,
+    padded_grad,
+    padded_grid,
+    gathered,
+    spots,
+    spots_s,
+    acc_w,
+    acc_o,
+    sem,
+):
+    grp_count, blk_count, cap, rows, channels, size_x, size_y, size_z, scale = dims
+    voxels = size_x * size_y * size_z
+    out_channels = LANES
+    devices = grp_count * blk_count
+    nx, ny = grp_count * size_x, blk_count * size_y
+    plane = size_x * size_y
+    tall = 8
+    halves = channels // LANES
+    grads_at = halves * rows
+    index_at = grads_at + voxels
+    my_grp, my_blk = me_ref[0], me_ref[1]
+
+    def fill(s, _):
+        at = where_ref[s]
+        slot_row = packed[at, index_at : index_at + 16, :].astype(F32)[0:1, :].astype(I32)
+        chosen = one_hot(iota((voxels, rows), 0) == slot_row)
+        pieces = [packed[at, h * rows : (h + 1) * rows, :] for h in range(halves)]
+        pieces.append(jnp.ones((rows, LANES), BF16))
+        held = mm(chosen, jnp.concatenate(pieces, axis=1)).astype(BF16)
+        g, b = s // blk_count, s % blk_count
+        place = pl.ds(pl.multiple_of(b * cap, cap), cap)
+        for d in range(blk_count):
+            slots[g * blk_count + d, place, :] = held[d * cap : (d + 1) * cap, :]
+        return 0
+
+    lax.fori_loop(0, devices, fill, 0)
+
+    padded_grad[...] = jnp.zeros(padded_grad.shape, F32)
+    padded_grid[...] = jnp.zeros(padded_grid.shape, F32)
+
+    stretch = one_hot(
+        iota((plane * tall, voxels), 0)
+        == (iota((plane * tall, voxels), 1) % plane) * tall + iota((plane * tall, voxels), 1) // plane + 1
+    )
+
+    def spot_row(r):
+        at = where_ref[r]
+        block = packed[at, index_at : index_at + 16, :].astype(F32)
+        return jnp.concatenate(
+            [block[1 + h : 2 + h, :] for h in range(voxels // LANES)], axis=1
+        ).astype(I32)
+
+    def place_region(r):
+        spot = spot_row(r)
+        spots[pl.ds(r, 1), :] = spot
+        key = (spot % size_z) * plane + spot // size_z
+        chosen = one_hot(iota((voxels, voxels), 0) == key)
+        found = mm(chosen, slots[r])
+        cells = found[:, :channels]
+        occupied = found[:, channels:]
+        cotangent = packed[where_ref[r], grads_at : grads_at + voxels, :].astype(F32) * occupied
+        g, d = r // blk_count, r % blk_count
+
+        tall_grad = mm(stretch, cotangent.astype(BF16)).reshape(size_x, size_y, tall, out_channels)
+        ys = pl.ds(d * size_y + 1, size_y)
+
+        @pl.when(g == my_grp)
+        def _():
+            padded_grad[1 : size_x + 1, ys] = tall_grad
+
+        @pl.when(g == my_grp - 1)
+        def _():
+            padded_grad[0:1, ys] = tall_grad[size_x - 1 : size_x]
+
+        @pl.when(g == my_grp + 1)
+        def _():
+            padded_grad[size_x + 1 : size_x + 2, ys] = tall_grad[0:1]
+
+        shape = (size_z, size_x, size_y, -1)
+        return cells.reshape(shape), cotangent.reshape(shape)
+
+    def place_pair(pair, _):
+        r = pair * 2
+        g, d = r // blk_count, r % blk_count
+        cells0, cot0 = place_region(r)
+        cells1, cot1 = place_region(r + 1)
+        xs = pl.ds(g * size_x, size_x)
+        ys = pl.ds(pl.multiple_of(d * size_y, 2 * size_y), 2 * size_y)
+        grid[:, xs, ys, :] = jnp.concatenate([cells0, cells1], axis=2).astype(BF16)
+        masked[:, xs, ys, :] = jnp.concatenate([cot0, cot1], axis=2).astype(BF16)
+        return 0
+
+    lax.fori_loop(0, devices // 2, place_pair, 0)
+
+    copy = pltpu.make_async_copy(spots.at[pl.ds(pl.multiple_of(my_grp * blk_count, blk_count), blk_count)], spots_s, sem)
+    copy.start()
+
+    lane = iota((out_channels, ny), 1)
+    zero = jnp.zeros((out_channels, ny), F32)
+
+    def turn(n, _):
+        z, x = n // nx, n % nx
+        block = masked[z, x].astype(F32).T
+        back = jnp.where(lane == ny - 1, zero, pltpu.roll(block, ny - 1, 1))
+        ahead = jnp.where(lane == 0, zero, pltpu.roll(block, 1, 1))
+        cols = pl.ds(pl.multiple_of(x * ny, ny), ny)
+        masked_t[z, 0:LANES, cols] = back.astype(BF16)
+        masked_t[z, LANES : 2 * LANES, cols] = block.astype(BF16)
+        masked_t[z, 2 * LANES : 3 * LANES, cols] = ahead.astype(BF16)
+        return 0
+
+    lax.fori_loop(0, size_z * nx, turn, 0)
+
+    for dx in (-1, 0, 1):
+        span = nx - abs(dx)
+        first = max(0, dx)
+
+        def for_dz(dz1, _, dx=dx, span=span, first=first):
+            dz = dz1 - 1
+            acc_w[...] = jnp.zeros(acc_w.shape, F32)
+
+            def add(z, _):
+                left = masked_t[z - dz, :, (first - dx) * ny : (first - dx + span) * ny]
+                right = grid[z, first : first + span].reshape(span * ny, channels)
+                acc_w[...] += mm(left, right)
+                return 0
+
+            lax.fori_loop(jnp.maximum(0, dz), jnp.minimum(size_z, size_z + dz), add, 0)
+            done = (acc_w[...].T * scale).astype(BF16)
+            for dy1 in range(3):
+                weight_grad[(dx + 1) * 9 + dy1 * 3 + dz1] = done[:, dy1 * LANES : (dy1 + 1) * LANES]
+            return 0
+
+        lax.fori_loop(0, 3, for_dz, 0)
+
+    def outer(dx, dy):
+        g, d = my_grp + dx, my_blk + dy
+        inside = (g >= 0) & (g < grp_count) & (d >= 0) & (d < blk_count)
+
+        @pl.when(inside)
+        def _():
+            r = g * blk_count + d
+            spot = spots[pl.ds(r, 1), :]
+            key = (spot // size_z) * tall + spot % size_z + 1
+            wide = (1 if dx else size_x) * (1 if dy else size_y) * tall
+            t = iota((wide, voxels), 0)
+            x0, y0 = (size_x - 1 if dx < 0 else 0), (size_y - 1 if dy < 0 else 0)
+            if dy and not dx:
+                want = (t // tall) * (size_y * tall) + y0 * tall + t % tall
+            else:
+                want = t + (x0 * size_y + y0) * tall
+            found = mm(one_hot(want == key), slots[r])
+            shape = ((1 if dx else size_x), (1 if dy else size_y), tall, channels)
+            at_x = {-1: 0, 0: 1, 1: size_x + 1}[dx]
+            at_y = {-1: 0, 0: 1, 1: size_y + 1}[dy]
+            padded_grid[at_x : at_x + shape[0], at_y : at_y + shape[1]] = found[:, :channels].reshape(shape)
+            if dx == 0 and dy == 0:
+                acc_o[:, 0:LANES] = found[:, channels:]
+
+    for dx in (-1, 0, 1):
+        for dy in (-1, 0, 1):
+            outer(dx, dy)
+    occupied = acc_o[:, 0:LANES]
+    acc_o[...] = jnp.zeros(acc_o.shape, F32)
+
+    def forward(n, _):
+        dx, dy = n // 3, n % 3
+        window = padded_grid[pl.ds(dx, size_x), pl.ds(dy, size_y)].reshape(plane * tall, channels)
+        taps = jnp.concatenate([weight[n * 3 + i] for i in range(3)], axis=1)
+        acc_o[...] += mm(window.astype(BF16), taps)
+        return 0
+
+    lax.fori_loop(0, 9, forward, 0)
+    total = (
+        pltpu.roll(acc_o[:, 0:LANES], 1, 0)
+        + acc_o[:, LANES : 2 * LANES]
+        + pltpu.roll(acc_o[:, 2 * LANES :], plane * tall - 1, 0)
+    )
+    rounded = (total * occupied).astype(BF16)
+    row, col = iota((voxels, plane * tall), 0), iota((voxels, plane * tall), 1)
+    squeeze = one_hot(col == (row // size_z) * tall + row % size_z + 1)
+    output[...] = mm(squeeze, rounded).astype(BF16)
+
+    copy.wait()
+
+    def gather(i, _):
+        slot = slot_ref[0, i]
+        d = slot // cap
+        v = spots_s[d, my_blk * cap + slot % cap]
+        x, y, z = v // (size_y * size_z), d * size_y + v // size_z % size_y, v % size_z
+        for n in range(9):
+            column = padded_grad[x + 2 - n // 3, y + 2 - n % 3]
+            gathered[n, pl.ds(pl.multiple_of(i * tall, tall), tall), :] = pltpu.roll(column, (tall - z) % tall, 0)
+        return 0
+
+    lax.fori_loop(0, rows, gather, 0)
+
+    def backward(n, total):
+        for dz1 in range(3):
+            window = gathered[n, pl.ds(2 - dz1, rows, stride=tall), :].astype(BF16)
+            total = total + mm_t(window, weight[n * 3 + dz1])
+        return total
+
+    grad_rows[...] = lax.fori_loop(0, 9, backward, jnp.zeros((rows, channels), F32)).astype(BF16)
+
+
+def exchange_masks(count):
+    even = [1 << i for i in range(count.bit_length() - 2, 0, -1)]
+    return even, even[1:] + even[:1]
+
+
+def gather_all(block, count):
+    axes = ("grp", "blk")
+    even, odd = exchange_masks(count)
+
+    def swap(value, masks):
+        pairs = [(i, i ^ masks[i % 2]) for i in range(count)]
+        return lax.ppermute(value, axes, pairs)
+
+    held = block[None]
+    for step in range(len(even) - 1):
+        held = jnp.concatenate([held, swap(held, (even[step], odd[step]))], axis=0)
+    last = swap(held, (even[-1], odd[-1]))
+    other = swap(held, (1, 1))
+    return jnp.concatenate([held, last, other, swap(last, (1, 1))], axis=0)
+
+
+def positions(count, me):
+    even, odd = exchange_masks(count)
+    apart = jnp.arange(count, dtype=I32) ^ me
+
+    def along(masks):
+        return sum(((apart // mask) % 2) << i for i, mask in enumerate(masks))
+
+    stream = (me + apart) % 2
+    return jnp.where(stream == 0, along(even), along(odd)) + (apart % 2) * (count // 2)
+
+
+def gathered_shards(features, dest, placement, weight, grad_out):
+    rows, channels = features.shape
+    grp_count, blk_count = lax.axis_size("grp"), lax.axis_size("blk")
+    devices = grp_count * blk_count
+    size_x, size_y, size_z, out_channels = grad_out.shape
+    voxels = size_x * size_y * size_z
+    cap = voxels // blk_count
+    nx, ny = grp_count * size_x, blk_count * size_y
+    packed_rows = channels // LANES * rows + voxels + 16
+    vmem = pl.BlockSpec(memory_space=pltpu.VMEM)
+    smem = pl.BlockSpec(memory_space=pltpu.SMEM)
+    packed, slot = pl.pallas_call(
+        functools.partial(pack_kernel, (size_x, size_y, size_z), cap),
+        out_shape=(
+            jax.ShapeDtypeStruct((packed_rows, LANES), BF16),
+            jax.ShapeDtypeStruct((1, rows), I32),
+        ),
+        in_specs=[vmem] * 4,
+        out_specs=(vmem, vmem),
+        name="pack",
+    )(features, dest, placement, grad_out.reshape(voxels, out_channels))
+    everything = gather_all(packed, devices)
+    my_grp, my_blk = lax.axis_index("grp"), lax.axis_index("blk")
+    me = jnp.stack([my_grp, my_blk]).astype(I32)
+    where = positions(devices, (my_grp * blk_count + my_blk).astype(I32))
+    scale = 1.0 / math.sqrt(rows * devices)
+    dims = (grp_count, blk_count, cap, rows, channels, size_x, size_y, size_z, scale)
+    output, grad_rows, weight_grad = pl.pallas_call(
+        functools.partial(scene_kernel, dims),
+        out_shape=(
+            jax.ShapeDtypeStruct((voxels, out_channels), BF16),
+            jax.ShapeDtypeStruct((rows, channels), BF16),
+            jax.ShapeDtypeStruct(weight.shape, BF16),
+        ),
+        in_specs=[smem, smem, smem, vmem, vmem],
+        out_specs=(vmem, vmem, vmem),
+        scratch_shapes=[
+            pltpu.VMEM((devices, voxels, channels + LANES), BF16),
+            pltpu.VMEM((size_z, nx, ny, channels), BF16),
+            pltpu.VMEM((size_z, nx, ny, out_channels), BF16),
+            pltpu.VMEM((size_z, 3 * out_channels, nx * ny), BF16),
+            pltpu.VMEM((size_x + 2, ny + 2, 8, out_channels), F32),
+            pltpu.VMEM((size_x + 2, size_y + 2, 8, channels), F32),
+            pltpu.VMEM((9, rows * 8, out_channels), F32),
+            pltpu.VMEM((devices, voxels), I32),
+            pltpu.SMEM((blk_count, voxels), I32),
+            pltpu.VMEM((3 * out_channels, channels), F32),
+            pltpu.VMEM((size_x * size_y * 8, 3 * out_channels), F32),
+            pltpu.SemaphoreType.DMA,
+        ],
+        compiler_params=pltpu.CompilerParams(vmem_limit_bytes=56 * 1024 * 1024),
+        name="scene",
+    )(me, where, slot, everything, weight)
+    return output.reshape(grad_out.shape), grad_rows, weight_grad
 
 
 def extended(cells, sides, width):
@@ -23,7 +379,7 @@
     return cells
 
 
-def shards(features, dest, placement, weight, grad_out):
+def summed_shards(features, dest, placement, weight, grad_out):
     row_count, channels = features.shape
     blk_count = lax.axis_size("blk")
     grp_count = lax.axis_size("grp")
@@ -110,6 +466,11 @@
     return (output, grad_rows, weight_grad)
 
 
+def fits(mesh):
+    grp_count, blk_count = mesh.shape["grp"], mesh.shape["blk"]
+    return grp_count * blk_count <= 64 and blk_count == 16 and grp_count & (grp_count - 1) == 0
+
+
 def solution(mesh):
     in_specs = (
         P(("grp", "blk"), None),
@@ -119,4 +480,5 @@
         P("grp", "blk", None, None),
     )
     out_specs = (P("grp", "blk", None, None), P(("grp", "blk"), None), P())
+    shards = gathered_shards if fits(mesh) else summed_shards
     return jax.shard_map(shards, mesh=mesh, in_specs=in_specs, out_specs=out_specs, check_vma=False)

time: 314 us -> 122 us (0.39)
  waiting for transfers between devices: 150 us -> 30.2 us
  local copies, waits for them, and re-layouts: 80.4 us -> 6.09 us
  Pallas kernels: 0 us -> 69.8 us
  starting transfers between devices: 35.3 us -> 10.8 us
  matrix products: 20.7 us -> 0 us
  between operations: 15.1 us -> 0.72 us
  other arithmetic: 10.5 us -> 4.07 us
    psum x1 -> x0, waiting for transfers between devices: 137 us -> none  [shards(): lax.psum(weight_terms, ('grp', 'blk')) * grad_scale]
    pallas_call x0 -> x2, Pallas kernels: none -> 69.8 us  [the longest x1 67.8 us: gathered_shards(): pl.pallas_call(functools.partial(scene_kernel, dims), out_shape=(jax.Shap...]
    slice x38 -> x0, local copies, waits for them, and re-layouts: 33 us -> none  [the longest x29 32.3 us: shards(): padded[shift_x:shift_x + size_x, shift_y:shift_y + size_y, shift_z:shift_...]
    reshape x27 -> x0, local copies, waits for them, and re-layouts: 30.6 us -> none  [the longest x26 30.6 us: shards(): window = padded[shift_x:shift_x + size_x, shift_y:shift_y + size_y, shift...]
    dot_general x81 -> x0, matrix products: 20.7 us -> none  [the longest x27 8.97 us: shards(): jnp.dot(window, weight[offset], preferred_element_type=jnp.float32)]
    ppermute x8 -> x6, waiting for transfers between devices: 9.56 us -> 30.2 us  [swap(): return lax.ppermute(value, axes, pairs)]
    all_to_all x3 -> x0, starting transfers between devices: 18.4 us -> none  [the longest x1 7.39 us: shards(): lax.all_to_all(send_counts, 'blk', split_axis=0, concat_axis=0, tiled=True)]
    convert_element_type x5 -> x0, other arithmetic: 6.12 us -> none  [the longest x1 3.4 us: shards(): (lax.psum(weight_terms, ('grp', 'blk')) * grad_scale).astype(jnp.bfloat16)]
  transfers between devices with their start and end apart: 12 -> 6, of which waited for: 6 -> 4; matrix products, arithmetic and copies ran while one was open for 7% -> 3% of each run, Pallas kernels for 0% -> 0%
where the time goes in v1:
time: 122 us
  Pallas kernels  69.8 us (57%)
  waiting for transfers between devices  30.2 us (25%)
  starting transfers between devices  10.8 us (9%)
  local copies, waits for them, and re-layouts  6.09 us (5%)
  other arithmetic  4.07 us (3%)
    pallas_call x1, Pallas kernels, gathered_shards(): pl.pallas_call(functools.partial(scene_kernel, dims), out_shape=(jax.Shap...  67.8 us
    ppermute x6, waiting for transfers between devices, swap(): return lax.ppermute(value, axes, pairs)  30.2 us
    ppermute x6, starting transfers between devices, swap(): return lax.ppermute(value, axes, pairs)  10.8 us
    unnamed x9, local copies, waits for them, and re-layouts  5.95 us
    concatenate x3, other arithmetic, gather_all(): held = jnp.concatenate([held, swap(held, (even[step], odd[step]))], axis=0)  2.9 us
  transfers between devices with their start and end apart: 6, of which 4 were waited for; matrix products, arithmetic and copies ran while one was open for 3% of the time, Pallas kernels for 0%

profile of v1, /device:TPU:0, one launch (start us, length us, event | category | flops | bytes accessed | tf_op | source)
XLA Modules:
  0.0 121.8 jit_solution(2758213516094646083)
XLA Ops:
  0.6 1.4 %copy.8.dest = s32[128,1]{1,0:T(8,128)} copy(s32[128,1]{0,1:T(1,128)} %param.6) | data formatting | bytes 1024 | tf_op args[1]
  2.0 2.0 %pack.1 = (bf16[528,128]{1,0:T(8,128)(2,1)}, s32[1,128]{1,0:T(1,128)}) custom-call(bf16[128,256]{1,0:T(8,128)(2,1)} %features.1, s32[128,1]{1,0:T(8,128)} %copy.8.dest, s32[1,256]{1,0:T(1,128)} %placement.1, bf16[256,128]{1,0:T(8,128)(2,1)} %bitcast.10), custom_call_target="tpu_custom_call" | custom-call | tf_op jit(solution)/shard_map/pack/pallas_call | solution.py:320
  4.0 2.9 %collective-permute-start = (bf16[1,528,128]{2,1,0:T(8,128)(2,1)}, bf16[1,528,128]{2,1,0:T(8,128)(2,1)S(1)}, u32[]{:S(2)}, u32[]{:S(2)}) collective-permute-start(bf16[1,528,128]{2,1,0:T(8,128)(2,1)} %bitcast.6), channel_id=1, source_target_pairs={{0,16},{1,9},{2,18},{3,11},{4,20},{5,13},{6,22},{7,15},{8,24},{9,1... | collective-permute-start | bytes 405512 | tf_op jit(solution)/shard_map/ppermute | solution.py:288
  6.9 3.2 %collective-permute-done = bf16[1,528,128]{2,1,0:T(8,128)(2,1)S(1)} collective-permute-done((bf16[1,528,128]{2,1,0:T(8,128)(2,1)}, bf16[1,528,128]{2,1,0:T(8,128)(2,1)S(1)}, u32[]{:S(2)}, u32[]{:S(2)}) %collective-permute-start) | collective-permute-done | bytes 135200 | tf_op jit(solution)/shard_map/ppermute | solution.py:288
  10.1 0.9 pad_maximum_fusion.2
  11.0 3.2 %collective-permute-start.1 = (bf16[2,528,128]{2,1,0:T(8,128)(2,1)S(1)}, bf16[2,528,128]{2,1,0:T(8,128)(2,1)S(1)}, u32[]{:S(2)}, u32[]{:S(2)}) collective-permute-start(bf16[2,528,128]{2,1,0:T(8,128)(2,1)S(1)} %pad_maximum_fusion.2), channel_id=1, source_target_pairs={{0,8},{1,5},{2,10},{3,7},{4,12},{5,1},{6,14},{7,3},{8,0},{9,13},{1... | collective-permute-start | bytes 811016 | tf_op jit(solution)/shard_map/ppermute | solution.py:288
  14.2 6.1 %collective-permute-done.1 = bf16[2,528,128]{2,1,0:T(8,128)(2,1)S(1)} collective-permute-done((bf16[2,528,128]{2,1,0:T(8,128)(2,1)S(1)}, bf16[2,528,128]{2,1,0:T(8,128)(2,1)S(1)}, u32[]{:S(2)}, u32[]{:S(2)}) %collective-permute-start.1) | collective-permute-done | bytes 270368 | tf_op jit(solution)/shard_map/ppermute | solution.py:288
  20.3 1.0 pad_maximum_fusion.1
  21.3 3.1 %collective-permute-start.2 = (bf16[4,528,128]{2,1,0:T(8,128)(2,1)S(1)}, bf16[4,528,128]{2,1,0:T(8,128)(2,1)S(1)}, u32[]{:S(2)}, u32[]{:S(2)}) collective-permute-start(bf16[4,528,128]{2,1,0:T(8,128)(2,1)S(1)} %pad_maximum_fusion.1), channel_id=1, source_target_pairs={{0,4},{1,3},{2,6},{3,1},{4,0},{5,7},{6,2},{7,5},{8,12},{9,11},{10,... | collective-permute-start | bytes 1622024 | tf_op jit(solution)/shard_map/ppermute | solution.py:288
  24.4 7.3 %collective-permute-done.2 = bf16[4,528,128]{2,1,0:T(8,128)(2,1)S(1)} collective-permute-done((bf16[4,528,128]{2,1,0:T(8,128)(2,1)S(1)}, bf16[4,528,128]{2,1,0:T(8,128)(2,1)S(1)}, u32[]{:S(2)}, u32[]{:S(2)}) %collective-permute-start.2) | collective-permute-done | bytes 540704 | tf_op jit(solution)/shard_map/ppermute | solution.py:288
  31.7 1.0 pad_maximum_fusion
  32.8 1.6 %collective-permute-start.3 = (bf16[8,528,128]{2,1,0:T(8,128)(2,1)S(1)}, bf16[8,528,128]{2,1,0:T(8,128)(2,1)S(1)}, u32[]{:S(2)}, u32[]{:S(2)}) collective-permute-start(bf16[8,528,128]{2,1,0:T(8,128)(2,1)S(1)} %pad_maximum_fusion), channel_id=1, source_target_pairs={{0,2},{1,17},{2,0},{3,19},{4,6},{5,21},{6,4},{7,23},{8,10},{9,25},... | collective-permute-start | bytes 3244040 | tf_op jit(solution)/shard_map/ppermute | solution.py:288
  34.3 13.6 %collective-permute-done.3 = bf16[8,528,128]{2,1,0:T(8,128)(2,1)S(1)} collective-permute-done((bf16[8,528,128]{2,1,0:T(8,128)(2,1)S(1)}, bf16[8,528,128]{2,1,0:T(8,128)(2,1)S(1)}, u32[]{:S(2)}, u32[]{:S(2)}) %collective-permute-start.3) | collective-permute-done | bytes 1081376 | tf_op jit(solution)/shard_map/ppermute | solution.py:288
  48.0 0.0 collective-permute-start.5
  48.0 0.6 fusion.1.where_ref
  48.5 0.6 pad_add_fusion.me_ref
  49.1 0.9 constant_dynamic-update-slice_fusion.6
  50.1 0.1 constant_dynamic-update-slice_fusion.3
  50.2 0.1 constant_dynamic-update-slice_fusion.2
  50.4 0.0 collective-permute-done.4
  50.4 1.4 %constant_dynamic-update-slice_fusion.1 = bf16[32,528,128]{2,1,0:T(8,128)(2,1)S(1)} fusion(bf16[32,528,128]{2,1,0:T(8,128)(2,1)S(1)} %constant_dynamic-update-slice_fusion.2, bf16[8,528,128]{2,1,0:T(8,128)(2,1)} %collective-permute-done.4), kind=kLoop, calls=%fused_computation.4 | loop fusion | bytes 2162688
  51.8 0.1 constant_dynamic-update-slice_fusion.packed
  51.9 2.0 %copy-done = bf16[32,528,128]{2,1,0:T(8,128)(2,1)} copy-done((bf16[32,528,128]{2,1,0:T(8,128)(2,1)}, bf16[32,528,128]{2,1,0:T(8,128)(2,1)S(1)}, u32[]{:S(2)}) %copy-start) | copy-done | bytes 4325400
  53.9 67.8 %scene.1 = (bf16[256,128]{1,0:T(8,128)(2,1)}, bf16[128,256]{1,0:T(8,128)(2,1)}, bf16[27,256,128]{2,1,0:T(8,128)(2,1)}) custom-call(s32[2]{0:T(128)} %pad_add_fusion.me_ref, s32[32]{0:T(128)} %fusion.1.where_ref, s32[1,128]{1,0:T(1,128)} %get-tuple-element.8.slot_ref, bf16[32,528,128]{2,1,0:T(8,128)(2,1)} %copy-done, bf16[27,256,128]{2,1,0:T(8,128)(2,1)} %weight.1), custom_call_target="tpu_custom_call" | custom-call | tf_op jit(solution)/shard_map/scene/pallas_call | solution.py:336
  (5 shorter events, 0.1 us)
Async XLA Ops:
  4.0 6.1 %collective-permute-start = (bf16[1,528,128]{2,1,0:T(8,128)(2,1)}, bf16[1,528,128]{2,1,0:T(8,128)(2,1)S(1)}, u32[]{:S(2)}, u32[]{:S(2)}) collective-permute-start(bf16[1,528,128]{2,1,0:T(8,128)(2,1)} %bitcast.6), channel_id=1, source_target_pairs={{0,16},{1,9},{2,18},{3,11},{4,20},{5,13},{6,22},{7,15},{8,24},{9,1... | collective-permute-start | bytes 405512 | tf_op jit(solution)/shard_map/ppermute | solution.py:288
  11.0 9.3 %collective-permute-start.1 = (bf16[2,528,128]{2,1,0:T(8,128)(2,1)S(1)}, bf16[2,528,128]{2,1,0:T(8,128)(2,1)S(1)}, u32[]{:S(2)}, u32[]{:S(2)}) collective-permute-start(bf16[2,528,128]{2,1,0:T(8,128)(2,1)S(1)} %pad_maximum_fusion.2), channel_id=1, source_target_pairs={{0,8},{1,5},{2,10},{3,7},{4,12},{5,1},{6,14},{7,3},{8,0},{9,13},{1... | collective-permute-start | bytes 811016 | tf_op jit(solution)/shard_map/ppermute | solution.py:288
  21.3 10.5 %collective-permute-start.2 = (bf16[4,528,128]{2,1,0:T(8,128)(2,1)S(1)}, bf16[4,528,128]{2,1,0:T(8,128)(2,1)S(1)}, u32[]{:S(2)}, u32[]{:S(2)}) collective-permute-start(bf16[4,528,128]{2,1,0:T(8,128)(2,1)S(1)} %pad_maximum_fusion.1), channel_id=1, source_target_pairs={{0,4},{1,3},{2,6},{3,1},{4,0},{5,7},{6,2},{7,5},{8,12},{9,11},{10,... | collective-permute-start | bytes 1622024 | tf_op jit(solution)/shard_map/ppermute | solution.py:288
  32.8 15.2 %collective-permute-start.3 = (bf16[8,528,128]{2,1,0:T(8,128)(2,1)S(1)}, bf16[8,528,128]{2,1,0:T(8,128)(2,1)S(1)}, u32[]{:S(2)}, u32[]{:S(2)}) collective-permute-start(bf16[8,528,128]{2,1,0:T(8,128)(2,1)S(1)} %pad_maximum_fusion), channel_id=1, source_target_pairs={{0,2},{1,17},{2,0},{3,19},{4,6},{5,21},{6,4},{7,23},{8,10},{9,25},... | collective-permute-start | bytes 3244040 | tf_op jit(solution)/shard_map/ppermute | solution.py:288
  34.3 16.0 %collective-permute-start.4 = (bf16[8,528,128]{2,1,0:T(8,128)(2,1)S(1)}, bf16[8,528,128]{2,1,0:T(8,128)(2,1)}, u32[]{:S(2)}, u32[]{:S(2)}) collective-permute-start(bf16[8,528,128]{2,1,0:T(8,128)(2,1)S(1)} %pad_maximum_fusion), channel_id=1, source_target_pairs={{0,1},{1,0},{2,3},{3,2},{4,5},{5,4},{6,7},{7,6},{8,9},{9,8},{10,11... | collective-permute-start | bytes 3244040 | tf_op jit(solution)/shard_map/ppermute | solution.py:288
  48.0 3.8 %collective-permute-start.5 = (bf16[8,528,128]{2,1,0:T(8,128)(2,1)S(1)}, bf16[8,528,128]{2,1,0:T(8,128)(2,1)S(1)}, u32[]{:S(2)}, u32[]{:S(2)}) collective-permute-start(bf16[8,528,128]{2,1,0:T(8,128)(2,1)S(1)} %collective-permute-done.3), channel_id=1, source_target_pairs={{0,1},{1,0},{2,3},{3,2},{4,5},{5,4},{6,7},{7,6},{8,9},{9,8},{10,11... | collective-permute-start | bytes 3244040 | tf_op jit(solution)/shard_map/ppermute | solution.py:288
  51.9 2.0 %copy-start = (bf16[32,528,128]{2,1,0:T(8,128)(2,1)}, bf16[32,528,128]{2,1,0:T(8,128)(2,1)S(1)}, u32[]{:S(2)}) copy-start(bf16[32,528,128]{2,1,0:T(8,128)(2,1)S(1)} %constant_dynamic-update-slice_fusion.packed) | copy-start | bytes 12976132

commit v2 on v0

--- a/solution.py
+++ b/solution.py
@@ -1,9 +1,495 @@
+import functools
 import math
 
 import jax
 import jax.numpy as jnp
 from jax import lax
+from jax.experimental import pallas as pl
+from jax.experimental.pallas import tpu as pltpu
 from jax.sharding import PartitionSpec as P
+
+LANES = 128
+TALL = 8
+F32, BF16, I32 = jnp.float32, jnp.bfloat16, jnp.int32
+
+
+def iota(shape, axis):
+    return lax.broadcasted_iota(I32, shape, axis)
+
+
+def one_hot(hits):
+    return jnp.where(hits, 1.0, 0.0).astype(BF16)
+
+
+def rows_at(count, key):
+    shape = (count, key.shape[1])
+    places = iota(shape, 0).astype(BF16)
+    return jnp.where(places == jnp.broadcast_to(key.astype(BF16), shape), 1.0, 0.0).astype(BF16)
+
+
+def mm(a, b):
+    return lax.dot_general(a, b, (((1,), (0,)), ((), ())), preferred_element_type=F32)
+
+
+def mm_t(a, b):
+    return lax.dot_general(a, b, (((1,), (1,)), ((), ())), preferred_element_type=F32)
+
+
+def half_order(z, flat, group, plane):
+    return z // 2 * (2 * plane) + (z + group) % 2 * plane + flat
+
+
+def pack_kernel(sizes, cap, dest, placement, grad, packed, slots):
+    size_x, size_y, size_z = sizes
+    rows = dest.shape[1]
+    voxels = grad.shape[0]
+    plane = size_x * size_y
+    lane = iota((rows, LANES), 1)
+    upright = iota((rows, rows), 0) == iota((rows, rows), 1)
+    target = jnp.sum(jnp.where(upright, dest[...], 0), axis=1, keepdims=True)
+    named = one_hot(lane == target)
+    earlier = one_hot(iota((rows, rows), 0) > iota((rows, rows), 1))
+    rank = jnp.sum(mm(earlier, named) * named.astype(F32), axis=1, keepdims=True)
+    slot = target.astype(F32) * cap + rank
+    slot_row = jnp.sum(jnp.where(upright, slot, 0.0), axis=0, keepdims=True)
+    counts = jnp.sum(named.astype(F32), axis=0, keepdims=True)
+    slots[...] = slot_row.astype(I32)
+    row, col = iota((voxels, voxels), 0), iota((voxels, voxels), 1)
+    moved = half_order(row % size_z, row // size_z, lax.axis_index("grp"), plane)
+    turned = mm(grad[...].astype(F32).T.astype(BF16), one_hot(col == moved)).astype(BF16)
+    halves = voxels // LANES
+    for h in range(halves):
+        packed[h * LANES : (h + 1) * LANES, :] = turned[:, h * LANES : (h + 1) * LANES]
+    spots = placement[...].astype(F32)
+    index_rows = [slot_row, counts] + [spots[:, h * LANES : (h + 1) * LANES] for h in range(halves)]
+    index_rows.append(jnp.zeros((16 - len(index_rows), LANES), F32))
+    packed[halves * LANES : halves * LANES + 16, :] = jnp.concatenate(index_rows, axis=0).astype(BF16)
+
+
+def source(me, buffer, t, count):
+    even, odd = exchange_masks(count)
+
+    def apart(masks):
+        total = masks[-1] * (buffer % 2)
+        for i in range(len(masks) - 1):
+            total = total + (t >> i) % 2 * masks[i]
+        return total
+
+    holder = me ^ (buffer // 2)
+    return holder ^ jnp.where(holder % 2 == 0, apart(even), apart(odd))
+
+
+def cotangent_kernel(
+    dims,
+    slot_ref,
+    block0,
+    block1,
+    block2,
+    block3,
+    weight,
+    grad_rows,
+    tiles,
+    slot_rows,
+    spots,
+    filled,
+    padded,
+    gathered,
+    stretch,
+    counts,
+    occupied,
+    masked,
+    spots_s,
+    sem,
+):
+    grp_count, blk_count, cap, rows, channels, size_x, size_y, size_z = dims
+    voxels = size_x * size_y * size_z
+    devices = grp_count * blk_count
+    plane = size_x * size_y
+    halves = voxels // LANES
+    blocks = (block0, block1, block2, block3)
+    each = devices // 4
+    my_grp, my_blk = lax.axis_index("grp"), lax.axis_index("blk")
+    me = my_grp * blk_count + my_blk
+
+    for k, block in enumerate(blocks):
+
+        def read(t, _, k=k, block=block):
+            s = source(me, k, t, devices)
+            index = block[t, halves * LANES : halves * LANES + 16, :].astype(F32)
+            slot_rows[pl.ds(s, 1), :] = index[0:1].astype(I32)
+            counts[pl.ds(s, 1), :] = index[1:2]
+            row = jnp.concatenate([index[2 + h : 3 + h] for h in range(halves)], axis=1)
+            spots[pl.ds(s, 1), :] = row.astype(I32)
+            return 0
+
+        lax.fori_loop(0, each, read, 0)
+    copy = pltpu.make_async_copy(
+        spots.at[pl.ds(pl.multiple_of(my_grp * blk_count, blk_count), blk_count)], spots_s, sem
+    )
+    copy.start()
+
+    spread = one_hot(iota((blk_count, voxels), 0) == iota((blk_count, voxels), 1) // cap)
+    rank = (iota((blk_count, voxels), 1) % cap).astype(F32)
+    for g in range(grp_count):
+        sent = counts[g * blk_count : (g + 1) * blk_count, :].T[:blk_count].astype(BF16)
+        held = jnp.where(rank < mm(sent, spread), 1.0, 0.0)
+        filled[g * blk_count : (g + 1) * blk_count, :] = held
+        row, col = iota((plane * TALL, voxels), 0), iota((plane * TALL, voxels), 1)
+        z = row % TALL - 1
+        inside = (z >= 0) & (z < size_z)
+        stretch[g] = one_hot(inside & (col == half_order(z, row // TALL, g, plane)))
+
+    zero_plane = jnp.zeros((1,) + padded.shape[1:], F32)
+    zero_line = jnp.zeros((padded.shape[0], 1) + padded.shape[2:], F32)
+
+    @pl.when(my_grp == 0)
+    def _():
+        padded[0:1] = zero_plane
+
+    @pl.when(my_grp == grp_count - 1)
+    def _():
+        padded[size_x + 1 : size_x + 2] = zero_plane
+
+    padded[:, 0:1] = zero_line
+    padded[:, padded.shape[1] - 1 :] = zero_line
+    for z in range(size_z):
+        tiles[z, :, 0:LANES] = jnp.zeros((LANES, LANES), BF16)
+        tiles[z, :, (blk_count + 1) * LANES :] = jnp.zeros((LANES, LANES), BF16)
+
+    def occupy(r, _):
+        spot = spots[pl.ds(r, 1), :]
+        key = half_order(spot % size_z, spot // size_z, r // blk_count, plane)
+        held = jnp.broadcast_to(filled[pl.ds(r, 1), :], (16, voxels)).astype(BF16)
+        occupied[pl.ds(r, 1), :] = mm_t(held, rows_at(voxels, key))[0:1]
+        return 0
+
+    lax.fori_loop(0, devices, occupy, 0, unroll=8)
+
+    for k, block in enumerate(blocks):
+
+        def mask(t, _, k=k, block=block):
+            r = source(me, k, t, devices)
+            there = occupied[pl.ds(r, 1), :].astype(BF16)
+            for h in range(halves):
+                at = slice(h * LANES, (h + 1) * LANES)
+                masked[r, :, at] = block[t, at, :] * there[:, at]
+            return 0
+
+        lax.fori_loop(0, each, mask, 0, unroll=4)
+
+    first = iota((LANES, LANES), 1) < plane
+
+    def tile(d, _):
+        cols = pl.ds(pl.multiple_of((d + 1) * LANES, LANES), LANES)
+        for h in range(halves):
+            at = slice(h * LANES, (h + 1) * LANES)
+            left, right = masked[d, :, at], masked[blk_count + d, :, at]
+            tiles[2 * h, :, cols] = jnp.where(first, left, right)
+            tiles[2 * h + 1, :, cols] = pltpu.roll(jnp.where(first, right, left), plane, 1)
+        return 0
+
+    lax.fori_loop(0, blk_count, tile, 0, unroll=4)
+
+    def stand(d, _):
+        found = mm_t(stretch[my_grp], masked[my_grp * blk_count + d])
+        padded[1 : size_x + 1, pl.ds(d * size_y + 1, size_y)] = found.reshape(size_x, size_y, TALL, LANES)
+        return 0
+
+    lax.fori_loop(0, blk_count, stand, 0, unroll=2)
+
+    near = 1 - my_grp
+    lines = pl.ds(pl.multiple_of(jnp.where(my_grp == 0, 0, size_x - 1) * size_y * TALL, size_y * TALL), size_y * TALL)
+
+    def stand_near(d, _):
+        found = mm_t(stretch[near, lines, :], masked[near * blk_count + d])
+        at_x = pl.ds(jnp.where(my_grp == 0, size_x + 1, 0), 1)
+        padded[at_x, pl.ds(d * size_y + 1, size_y)] = found.reshape(1, size_y, TALL, LANES)
+        return 0
+
+    lax.fori_loop(0, blk_count, stand_near, 0, unroll=4)
+
+    copy.wait()
+    sub = iota((TALL, LANES), 0)
+
+    def gather(group, _):
+        found = [jnp.zeros((TALL, LANES), F32)] * 27
+        for j in range(TALL):
+            slot = slot_ref[0, group * TALL + j]
+            d = slot // cap
+            v = spots_s[d, my_blk * cap + slot % cap]
+            x, y, z = v // (size_y * size_z), d * size_y + v // size_z % size_y, v % size_z
+            for n in range(27):
+                line = padded[x + 2 - n // 9, y + 2 - n // 3 % 3, pl.ds(z + 2 - n % 3, 1), :]
+                found[n] = jnp.where(sub == j, jnp.broadcast_to(line, (TALL, LANES)), found[n])
+        for n in range(27):
+            gathered[n, pl.ds(pl.multiple_of(group * TALL, TALL), TALL), :] = found[n]
+        return 0
+
+    lax.fori_loop(0, rows // TALL, gather, 0)
+
+    def backward(n, total):
+        windows = jnp.concatenate([gathered[n * 3 + i] for i in range(3)], axis=1).astype(BF16)
+        taps = jnp.concatenate([weight[n * 3 + i] for i in range(3)], axis=1)
+        return total + mm_t(windows, taps)
+
+    grad_rows[...] = lax.fori_loop(0, 9, backward, jnp.zeros((rows, channels), F32), unroll=3).astype(BF16)
+
+
+def scene_kernel(
+    dims,
+    block0,
+    block1,
+    block2,
+    block3,
+    weight,
+    tiles,
+    slot_rows,
+    spots,
+    filled,
+    output,
+    weight_grad,
+    slots,
+    grid,
+    shifted,
+    padded,
+    acc_w,
+    acc_o,
+):
+    grp_count, blk_count, cap, rows, channels, size_x, size_y, size_z, scale = dims
+    voxels = size_x * size_y * size_z
+    devices = grp_count * blk_count
+    plane = size_x * size_y
+    blocks = (block0, block1, block2, block3)
+    each = devices // 4
+    my_grp, my_blk = lax.axis_index("grp"), lax.axis_index("blk")
+    me = my_grp * blk_count + my_blk
+    half = me % 2
+
+    for k, block in enumerate(blocks):
+
+        def fill(t, _, k=k, block=block):
+            s = source(me, k, t, devices)
+            chosen = rows_at(voxels, slot_rows[pl.ds(s, 1), :])
+            held = mm(chosen, block[t]).astype(BF16)
+            g, b = s // blk_count, s % blk_count
+            place = pl.ds(pl.multiple_of(b * cap, cap), cap)
+            for d in range(blk_count):
+                slots[g * blk_count + d, place, :] = held[d * cap : (d + 1) * cap, :]
+            return 0
+
+        lax.fori_loop(0, each, fill, 0, unroll=4)
+
+    def place_region(r, _):
+        spot = spots[pl.ds(r, 1), :]
+        key = spot % size_z * plane + spot // size_z
+        found = mm(rows_at(voxels, key), slots[r]).astype(BF16)
+        at = r % blk_count * LANES + r // blk_count * plane
+        for z in range(size_z):
+            grid[z, pl.ds(pl.multiple_of(at, plane), plane), :] = found[z * plane : (z + 1) * plane]
+        return 0
+
+    lax.fori_loop(0, devices, place_region, 0, unroll=4)
+
+    def outer(dx, dy):
+        g, d = my_grp + dx, my_blk + dy
+        inside = (g >= 0) & (g < grp_count) & (d >= 0) & (d < blk_count)
+        shape = ((1 if dx else size_x), (1 if dy else size_y), TALL, channels)
+        at_x = {-1: 0, 0: 1, 1: size_x + 1}[dx]
+        at_y = {-1: 0, 0: 1, 1: size_y + 1}[dy]
+        there = (slice(at_x, at_x + shape[0]), slice(at_y, at_y + shape[1]))
+
+        @pl.when(inside)
+        def _():
+            r = g * blk_count + d
+            spot = spots[pl.ds(r, 1), :]
+            key = spot // size_z * TALL + spot % size_z + 1
+            t = iota((shape[0] * shape[1] * TALL, voxels), 0)
+            x0, y0 = (size_x - 1 if dx < 0 else 0), (size_y - 1 if dy < 0 else 0)
+            if dy and not dx:
+                want = t // TALL * (size_y * TALL) + y0 * TALL + t % TALL
+            else:
+                want = t + (x0 * size_y + y0) * TALL
+            padded[there] = mm(one_hot(want == key), slots[r]).reshape(shape)
+
+        @pl.when(jnp.logical_not(inside))
+        def _():
+            padded[there] = jnp.zeros(shape, F32)
+
+    for dx in (-1, 0, 1):
+        for dy in (-1, 0, 1):
+            outer(dx, dy)
+
+    acc_o[...] = jnp.zeros(acc_o.shape, F32)
+
+    def forward(n, _):
+        dx, dy = n // 3, n % 3
+        window = padded[pl.ds(dx, size_x), pl.ds(dy, size_y)].reshape(plane * TALL, channels)
+        taps = jnp.concatenate([weight[n * 3 + i] for i in range(3)], axis=1)
+        acc_o[...] += mm(window.astype(BF16), taps)
+        return 0
+
+    lax.fori_loop(0, 9, forward, 0)
+    spot = spots[pl.ds(me, 1), :]
+    key = jnp.where(filled[pl.ds(me, 1), :] > 0, spot // size_z * TALL + spot % size_z + 1, -1)
+    occupied = mm(one_hot(iota((plane * TALL, voxels), 0) == key), jnp.ones((voxels, LANES), BF16))
+    total = (
+        pltpu.roll(acc_o[:, 0:LANES], 1, 0)
+        + acc_o[:, LANES : 2 * LANES]
+        + pltpu.roll(acc_o[:, 2 * LANES :], plane * TALL - 1, 0)
+    )
+    rounded = (total * occupied).astype(BF16)
+    row, col = iota((voxels, plane * TALL), 0), iota((voxels, plane * TALL), 1)
+    squeeze = one_hot(col == row // size_z * TALL + row % size_z + 1)
+    output[...] = mm(squeeze, rounded).astype(BF16)
+
+    acc_w[...] = jnp.zeros(acc_w.shape, F32)
+    lane = iota((LANES, LANES), 1)
+    x, y = lane // size_y, lane % size_y
+    nx = grp_count * size_x
+    zero = jnp.zeros((LANES, LANES), BF16)
+
+    def for_z(z, _):
+        for own_half in range(2):
+
+            def shift(d, _, own_half=own_half):
+                def tile(offset):
+                    return tiles[z, :, pl.ds(pl.multiple_of((d + 1 + offset) * LANES, LANES), LANES)]
+
+                cols = pl.ds(pl.multiple_of(d * LANES, LANES), LANES)
+                beside = {dy: tile(-dy) for dy in (-1, 0, 1)}
+                for n in range(5):
+                    place = n + 4 * own_half
+                    dx, dy = place // 3 - 1, place % 3 - 1
+                    ahead = dx * size_y + dy
+                    value = beside[0]
+                    if ahead:
+                        value = pltpu.roll(value, ahead % LANES, 1)
+                    if dy:
+                        crossing = y == (0 if dy > 0 else size_y - 1)
+                        value = jnp.where(crossing, pltpu.roll(beside[dy], (ahead - dy * size_y) % LANES, 1), value)
+                    if dx:
+                        value = jnp.where((x - dx >= 0) & (x - dx < nx), value, zero)
+                    shifted[n * LANES : (n + 1) * LANES, cols] = value
+                return 0
+
+            @pl.when(half == own_half)
+            def _(shift=shift):
+                lax.fori_loop(0, blk_count, shift, 0, unroll=2)
+
+        def add(dz1, _):
+            acc_w[dz1] += mm(shifted[...], grid[z + dz1 - 1])
+            return 0
+
+        lax.fori_loop(jnp.where(z == 0, 1, 0), jnp.where(z == size_z - 1, 2, 3), add, 0)
+        return 0
+
+    lax.fori_loop(0, size_z, for_z, 0)
+
+    def finish(dz1, _):
+        done = (acc_w[dz1].T * scale).astype(BF16)
+        for n in range(5):
+            weight_grad[n * 3 + dz1] = done[:, n * LANES : (n + 1) * LANES]
+        return 0
+
+    lax.fori_loop(0, 3, finish, 0)
+
+
+def exchange_masks(count):
+    even = [1 << i for i in range(count.bit_length() - 2, 0, -1)]
+    return even, even[1:] + even[:1]
+
+
+def swap(value, count, masks):
+    pairs = [(i, i ^ masks[i % 2]) for i in range(count)]
+    return lax.ppermute(value, ("grp", "blk"), pairs)
+
+
+def gather_all(block, count):
+    even, odd = exchange_masks(count)
+    held = block[None]
+    for step in range(len(even) - 1):
+        held = jnp.concatenate([held, swap(held, count, (even[step], odd[step]))], axis=0)
+    last = swap(held, count, (even[-1], odd[-1]))
+    return held, last, swap(held, count, (1, 1)), swap(last, count, (1, 1))
+
+
+def gathered_shards(features, dest, placement, weight, grad_out):
+    rows, channels = features.shape
+    grp_count, blk_count = lax.axis_size("grp"), lax.axis_size("blk")
+    devices = grp_count * blk_count
+    size_x, size_y, size_z, out_channels = grad_out.shape
+    sizes = (size_x, size_y, size_z)
+    voxels = size_x * size_y * size_z
+    plane = size_x * size_y
+    cap = voxels // blk_count
+    vmem = pl.BlockSpec(memory_space=pltpu.VMEM)
+    smem = pl.BlockSpec(memory_space=pltpu.SMEM)
+    packed, slot = pl.pallas_call(
+        functools.partial(pack_kernel, sizes, cap),
+        out_shape=(
+            jax.ShapeDtypeStruct((voxels + 16, LANES), BF16),
+            jax.ShapeDtypeStruct((1, rows), I32),
+        ),
+        in_specs=[vmem] * 3,
+        out_specs=(vmem, vmem),
+        name="pack",
+    )(dest.reshape(1, rows), placement, grad_out.reshape(voxels, out_channels))
+    cotangents = gather_all(packed, devices)
+    cells = gather_all(features, devices)
+    dims = (grp_count, blk_count, cap, rows, channels) + sizes
+    grad_rows, tiles, slot_rows, spots, filled = pl.pallas_call(
+        functools.partial(cotangent_kernel, dims),
+        out_shape=(
+            jax.ShapeDtypeStruct((rows, channels), BF16),
+            jax.ShapeDtypeStruct((size_z, out_channels, (blk_count + 2) * LANES), BF16),
+            jax.ShapeDtypeStruct((devices, rows), I32),
+            jax.ShapeDtypeStruct((devices, voxels), I32),
+            jax.ShapeDtypeStruct((devices, voxels), F32),
+        ),
+        in_specs=[smem] + [vmem] * 5,
+        out_specs=(vmem,) * 5,
+        scratch_shapes=[
+            pltpu.VMEM((size_x + 2, blk_count * size_y + 2, TALL, out_channels), F32),
+            pltpu.VMEM((27, rows, out_channels), F32),
+            pltpu.VMEM((grp_count, plane * TALL, voxels), BF16),
+            pltpu.VMEM((devices, LANES), F32),
+            pltpu.VMEM((devices, voxels), F32),
+            pltpu.VMEM((devices, out_channels, voxels), BF16),
+            pltpu.SMEM((blk_count, voxels), I32),
+            pltpu.SemaphoreType.DMA,
+        ],
+        compiler_params=pltpu.CompilerParams(vmem_limit_bytes=28 * 1024 * 1024),
+        name="cotangent",
+    )(slot, *cotangents, weight)
+    scale = 1.0 / math.sqrt(rows * devices)
+    output, some = pl.pallas_call(
+        functools.partial(scene_kernel, dims + (scale,)),
+        out_shape=(
+            jax.ShapeDtypeStruct((voxels, out_channels), BF16),
+            jax.ShapeDtypeStruct((15, channels, out_channels), BF16),
+        ),
+        in_specs=[vmem] * 9,
+        out_specs=(vmem, vmem),
+        scratch_shapes=[
+            pltpu.VMEM((devices, voxels, channels), BF16),
+            pltpu.VMEM((size_z, blk_count * LANES, channels), BF16),
+            pltpu.VMEM((5 * out_channels, blk_count * LANES), BF16),
+            pltpu.VMEM((size_x + 2, size_y + 2, TALL, channels), F32),
+            pltpu.VMEM((3, 5 * out_channels, channels), F32),
+            pltpu.VMEM((plane * TALL, 3 * out_channels), F32),
+        ],
+        compiler_params=pltpu.CompilerParams(vmem_limit_bytes=36 * 1024 * 1024),
+        name="scene",
+    )(*cells, weight, tiles, slot_rows, spots, filled)
+    odd = lax.axis_index("blk") % 2
+    sent = lax.dynamic_slice_in_dim(some, 3 * odd, 12, axis=0)
+    received = swap(sent, devices, (1, 1))
+    weight_grad = jnp.where(
+        odd == 0,
+        jnp.concatenate([some, received], axis=0),
+        jnp.concatenate([received, some], axis=0),
+    )
+    return output.reshape(grad_out.shape), grad_rows, weight_grad
 
 
 def extended(cells, sides, width):
@@ -23,7 +509,7 @@
     return cells
 
 
-def shards(features, dest, placement, weight, grad_out):
+def summed_shards(features, dest, placement, weight, grad_out):
     row_count, channels = features.shape
     blk_count = lax.axis_size("blk")
     grp_count = lax.axis_size("grp")
@@ -110,6 +596,11 @@
     return (output, grad_rows, weight_grad)
 
 
+def fits(mesh):
+    grp_count, blk_count = mesh.shape["grp"], mesh.shape["blk"]
+    return blk_count == 16 and grp_count == 2
+
+
 def solution(mesh):
     in_specs = (
         P(("grp", "blk"), None),
@@ -119,4 +610,5 @@
         P("grp", "blk", None, None),
     )
     out_specs = (P("grp", "blk", None, None), P(("grp", "blk"), None), P())
+    shards = gathered_shards if fits(mesh) else summed_shards
     return jax.shard_map(shards, mesh=mesh, in_specs=in_specs, out_specs=out_specs, check_vma=False)

time: 314 us -> 86.6 us (0.28)
  waiting for transfers between devices: 150 us -> 20.6 us
  local copies, waits for them, and re-layouts: 80.4 us -> 0.07 us
  Pallas kernels: 0 us -> 42.4 us
  matrix products: 20.7 us -> 0 us
  starting transfers between devices: 35.3 us -> 15.5 us
  between operations: 15.1 us -> 0.74 us
  other arithmetic: 10.5 us -> 6 us
    psum x1 -> x0, waiting for transfers between devices: 137 us -> none  [shards(): lax.psum(weight_terms, ('grp', 'blk')) * grad_scale]
    pallas_call x0 -> x3, Pallas kernels: none -> 42.4 us  [the longest x1 26.5 us: gathered_shards(): pl.pallas_call(functools.partial(scene_kernel, dims + (scale,)), out_shap...]
    slice x38 -> x0, local copies, waits for them, and re-layouts: 33 us -> none  [the longest x29 32.3 us: shards(): padded[shift_x:shift_x + size_x, shift_y:shift_y + size_y, shift_z:shift_...]
    reshape x27 -> x0, local copies, waits for them, and re-layouts: 30.6 us -> none  [the longest x26 30.6 us: shards(): window = padded[shift_x:shift_x + size_x, shift_y:shift_y + size_y, shift...]
    dot_general x81 -> x0, matrix products: 20.7 us -> none  [the longest x27 8.97 us: shards(): jnp.dot(window, weight[offset], preferred_element_type=jnp.float32)]
    all_to_all x3 -> x0, starting transfers between devices: 18.4 us -> none  [the longest x1 7.39 us: shards(): lax.all_to_all(send_counts, 'blk', split_axis=0, concat_axis=0, tiled=True)]
    ppermute x8 -> x13, waiting for transfers between devices: 9.56 us -> 20.6 us  [swap(): return lax.ppermute(value, ('grp', 'blk'), pairs)]
    unnamed x66 -> x6, local copies, waits for them, and re-layouts: 7.83 us -> 0.02 us
  transfers between devices with their start and end apart: 12 -> 13, of which waited for: 6 -> 8; matrix products, arithmetic and copies ran while one was open for 7% -> 5% of each run, Pallas kernels for 0% -> 16%
where the time goes in v2:
time: 86.6 us; the launch traced here: 85.3 us
  Pallas kernels  42.4 us (49%)
  waiting for transfers between devices  20.6 us (24%)
  starting transfers between devices  15.5 us (18%)
  other arithmetic  6 us (7%)
    pallas_call x1, Pallas kernels, gathered_shards(): pl.pallas_call(functools.partial(scene_kernel, dims + (scale,)), out_shap...  26.5 us
    ppermute x13, waiting for transfers between devices, swap(): return lax.ppermute(value, ('grp', 'blk'), pairs)  20.6 us
    ppermute x13, starting transfers between devices, swap(): return lax.ppermute(value, ('grp', 'blk'), pairs)  15.5 us
    pallas_call x1, Pallas kernels, gathered_shards(): pl.pallas_call(functools.partial(cotangent_kernel, dims), out_shape=(jax....  14 us
    concatenate x6, other arithmetic, gather_all(): jnp.concatenate([held, swap(held, count, (even[step], odd[step]))], axis=0)  4.52 us
    pallas_call x1, Pallas kernels, gathered_shards(): pl.pallas_call(functools.partial(pack_kernel, sizes, cap), out_shape=(jax...  1.91 us
  transfers between devices with their start and end apart: 13, of which 8 were waited for; matrix products, arithmetic and copies ran while one was open for 5% of the time, Pallas kernels for 16%

profile of v2, /device:TPU:0, one launch (start us, length us, event | category | flops | bytes accessed | tf_op | source)
XLA Modules:
  0.0 85.3 jit_solution(6846228540056499872)
XLA Ops:
  0.6 1.9 %pack.1 = (bf16[272,128]{1,0:T(8,128)(2,1)}, s32[1,128]{1,0:T(1,128)}) custom-call(s32[1,128]{1,0:T(1,128)} %bitcast.14, s32[1,256]{1,0:T(1,128)} %placement.1, bf16[256,128]{1,0:T(8,128)(2,1)} %bitcast.13), custom_call_target="tpu_custom_call" | custom-call | tf_op jit(solution)/shard_map/pack/pallas_call | solution.py:427
  2.6 2.9 %collective-permute-start.6 = (bf16[1,272,128]{2,1,0:T(8,128)(2,1)}, bf16[1,272,128]{2,1,0:T(8,128)(2,1)S(1)}, u32[]{:S(2)}, u32[]{:S(2)}) collective-permute-start(bf16[1,272,128]{2,1,0:T(8,128)(2,1)} %bitcast.5), channel_id=1, source_target_pairs={{0,16},{1,9},{2,18},{3,11},{4,20},{5,13},{6,22},{7,15},{8,24},{9,1... | collective-permute-start | bytes 208904 | tf_op jit(solution)/shard_map/ppermute | solution.py:404
  5.5 2.5 %collective-permute-done.6 = bf16[1,272,128]{2,1,0:T(8,128)(2,1)S(1)} collective-permute-done((bf16[1,272,128]{2,1,0:T(8,128)(2,1)}, bf16[1,272,128]{2,1,0:T(8,128)(2,1)S(1)}, u32[]{:S(2)}, u32[]{:S(2)}) %collective-permute-start.6) | collective-permute-done | bytes 69664 | tf_op jit(solution)/shard_map/ppermute | solution.py:404
  8.0 0.9 %pad_maximum_fusion.4 = bf16[2,272,128]{2,1,0:T(8,128)(2,1)S(1)} fusion(bf16[1,272,128]{2,1,0:T(8,128)(2,1)S(1)} %collective-permute-done.6, bf16[1,272,128]{2,1,0:T(8,128)(2,1)} %bitcast.6), kind=kLoop, calls=%fused_computation.5 | loop fusion | flops 69632 | bytes 278528 | tf_op jit(solution)/shard_map/concatenate | solution.py:411
  8.9 3.2 %collective-permute-start.7 = (bf16[2,272,128]{2,1,0:T(8,128)(2,1)S(1)}, bf16[2,272,128]{2,1,0:T(8,128)(2,1)S(1)}, u32[]{:S(2)}, u32[]{:S(2)}) collective-permute-start(bf16[2,272,128]{2,1,0:T(8,128)(2,1)S(1)} %pad_maximum_fusion.4), channel_id=1, source_target_pairs={{0,8},{1,5},{2,10},{3,7},{4,12},{5,1},{6,14},{7,3},{8,0},{9,13},{1... | collective-permute-start | bytes 417800 | tf_op jit(solution)/shard_map/ppermute | solution.py:404
  12.1 0.9 %pad_maximum_fusion.5 = bf16[2,128,256]{2,1,0:T(8,128)(2,1)S(1)} fusion(bf16[1,128,256]{2,1,0:T(8,128)(2,1)S(1)} %collective-permute-done, bf16[1,128,256]{2,1,0:T(8,128)(2,1)} %bitcast.10), kind=kLoop, calls=%fused_computation.6 | loop fusion | flops 65536 | bytes 262144 | tf_op jit(solution)/shard_map/concatenate | solution.py:411
  13.0 0.5 collective-permute-start.1
  13.5 2.6 %collective-permute-done.7 = bf16[2,272,128]{2,1,0:T(8,128)(2,1)S(1)} collective-permute-done((bf16[2,272,128]{2,1,0:T(8,128)(2,1)S(1)}, bf16[2,272,128]{2,1,0:T(8,128)(2,1)S(1)}, u32[]{:S(2)}, u32[]{:S(2)}) %collective-permute-start.7) | collective-permute-done | bytes 139296 | tf_op jit(solution)/shard_map/ppermute | solution.py:404
  16.1 0.9 %pad_maximum_fusion.2 = bf16[4,272,128]{2,1,0:T(8,128)(2,1)S(1)} fusion(bf16[2,272,128]{2,1,0:T(8,128)(2,1)S(1)} %collective-permute-done.7, bf16[1,272,128]{2,1,0:T(8,128)(2,1)S(1)} %collective-permute-done.6, bf16[1,272,128]{2,1,0:T(8,128)(2,1)} %bitcast.7), kind=kLoop, calls=%fused_computation.3 | loop fusion | flops 278528 | bytes 557056 | tf_op jit(solution)/shard_map/concatenate | solution.py:411
  17.0 2.5 %collective-permute-start.8 = (bf16[4,272,128]{2,1,0:T(8,128)(2,1)S(1)}, bf16[4,272,128]{2,1,0:T(8,128)(2,1)S(1)}, u32[]{:S(2)}, u32[]{:S(2)}) collective-permute-start(bf16[4,272,128]{2,1,0:T(8,128)(2,1)S(1)} %pad_maximum_fusion.2), channel_id=1, source_target_pairs={{0,4},{1,3},{2,6},{3,1},{4,0},{5,7},{6,2},{7,5},{8,12},{9,11},{10,... | collective-permute-start | bytes 835592 | tf_op jit(solution)/shard_map/ppermute | solution.py:404
  19.7 0.9 %pad_maximum_fusion.3 = bf16[4,128,256]{2,1,0:T(8,128)(2,1)S(1)} fusion(bf16[2,128,256]{2,1,0:T(8,128)(2,1)S(1)} %collective-permute-done.1, bf16[1,128,256]{2,1,0:T(8,128)(2,1)S(1)} %collective-permute-done, bf16[1,128,256]{2,1,0:T(8,128)(2,1)} %bitcast.11), kind=kLoop, calls=%fused_computation.4 | loop fusion | flops 262144 | bytes 524288 | tf_op jit(solution)/shard_map/concatenate | solution.py:411
  20.6 1.6 %collective-permute-start.2 = (bf16[4,128,256]{2,1,0:T(8,128)(2,1)S(1)}, bf16[4,128,256]{2,1,0:T(8,128)(2,1)S(1)}, u32[]{:S(2)}, u32[]{:S(2)}) collective-permute-start(bf16[4,128,256]{2,1,0:T(8,128)(2,1)S(1)} %pad_maximum_fusion.3), channel_id=1, source_target_pairs={{0,4},{1,3},{2,6},{3,1},{4,0},{5,7},{6,2},{7,5},{8,12},{9,11},{10,... | collective-permute-start | bytes 786440 | tf_op jit(solution)/shard_map/ppermute | solution.py:404
  22.2 1.9 %collective-permute-done.8 = bf16[4,272,128]{2,1,0:T(8,128)(2,1)S(1)} collective-permute-done((bf16[4,272,128]{2,1,0:T(8,128)(2,1)S(1)}, bf16[4,272,128]{2,1,0:T(8,128)(2,1)S(1)}, u32[]{:S(2)}, u32[]{:S(2)}) %collective-permute-start.8) | collective-permute-done | bytes 278560 | tf_op jit(solution)/shard_map/ppermute | solution.py:404
  24.0 0.9 %pad_maximum_fusion.block0 = bf16[8,272,128]{2,1,0:T(8,128)(2,1)S(1)} fusion(bf16[4,272,128]{2,1,0:T(8,128)(2,1)S(1)} %collective-permute-done.8, bf16[2,272,128]{2,1,0:T(8,128)(2,1)S(1)} %collective-permute-done.7, bf16[1,272,128]{2,1,0:T(8,128)(2,1)S(1)} %collective-permute-done.6, bf16[1,272,128]{2,1,0:T(8,128)(2,1)} %bitcast.8), kind=kLoop, calls=%fused_computation.1 | loop fusion | flops 835584 | bytes 1114112 | tf_op jit(solution)/shard_map/concatenate | solution.py:411
  25.0 1.6 %collective-permute-start.9 = (bf16[8,272,128]{2,1,0:T(8,128)(2,1)S(1)}, bf16[8,272,128]{2,1,0:T(8,128)(2,1)}, u32[]{:S(2)}, u32[]{:S(2)}) collective-permute-start(bf16[8,272,128]{2,1,0:T(8,128)(2,1)S(1)} %pad_maximum_fusion.block0), channel_id=1, source_target_pairs={{0,2},{1,17},{2,0},{3,19},{4,6},{5,21},{6,4},{7,23},{8,10},{9,25},... | collective-permute-start | bytes 1671176 | tf_op jit(solution)/shard_map/ppermute | solution.py:404
  27.1 1.6 %collective-permute-start.3 = (bf16[8,128,256]{2,1,0:T(8,128)(2,1)S(1)}, bf16[8,128,256]{2,1,0:T(8,128)(2,1)}, u32[]{:S(2)}, u32[]{:S(2)}) collective-permute-start(bf16[8,128,256]{2,1,0:T(8,128)(2,1)S(1)} %pad_maximum_fusion.1.block0), channel_id=1, source_target_pairs={{0,2},{1,17},{2,0},{3,19},{4,6},{5,21},{6,4},{7,23},{8,10},{9,25},... | collective-permute-start | bytes 1572872 | tf_op jit(solution)/shard_map/ppermute | solution.py:404
  28.7 6.0 %collective-permute-done.9.block1 = bf16[8,272,128]{2,1,0:T(8,128)(2,1)} collective-permute-done((bf16[8,272,128]{2,1,0:T(8,128)(2,1)S(1)}, bf16[8,272,128]{2,1,0:T(8,128)(2,1)}, u32[]{:S(2)}, u32[]{:S(2)}) %collective-permute-start.9) | collective-permute-done | bytes 557088 | tf_op jit(solution)/shard_map/ppermute | solution.py:404
  34.7 0.5 collective-permute-start.4
  35.2 5.1 %collective-permute-done.3.block1 = bf16[8,128,256]{2,1,0:T(8,128)(2,1)} collective-permute-done((bf16[8,128,256]{2,1,0:T(8,128)(2,1)S(1)}, bf16[8,128,256]{2,1,0:T(8,128)(2,1)}, u32[]{:S(2)}, u32[]{:S(2)}) %collective-permute-start.3) | collective-permute-done | bytes 524320 | tf_op jit(solution)/shard_map/ppermute | solution.py:404
  40.3 14.0 %cotangent.1 = (bf16[128,256]{1,0:T(8,128)(2,1)}, bf16[4,128,2304]{2,1,0:T(8,128)(2,1)S(1)}, s32[32,128]{1,0:T(8,128)S(1)}, s32[32,256]{1,0:T(8,128)S(1)}, f32[32,256]{1,0:T(8,128)S(1)}) custom-call(s32[1,128]{1,0:T(1,128)S(1)} %copy-done.1, bf16[8,272,128]{2,1,0:T(8,128)(2,1)S(1)} %pad_maximum_fusion.block0, ...), custom_call_target="tpu_custom_call" | custom-call | tf_op jit(solution)/shard_map/cotangent/pallas_call | solution.py:440
  54.4 26.5 %scene.1 = (bf16[256,128]{1,0:T(8,128)(2,1)}, bf16[15,256,128]{2,1,0:T(8,128)(2,1)S(1)}) custom-call(bf16[8,128,256]{2,1,0:T(8,128)(2,1)S(1)} %pad_maximum_fusion.1.block0, bf16[8,128,256]{2,1,0:T(8,128)(2,1)} %collective-permute-done.3.block1, bf16[8,128,256]{2,1,0:T(8,128)(2,1)} %collective-permute-done.4.block2, ...), custom_call_target="tpu_custom_call" | custom-call | tf_op jit(solution)/shard_map/scene/pallas_call | solution.py:465
  80.9 1.0 %collective-permute-start.12 = (bf16[12,256,128]{2,1,0:T(8,128)(2,1)S(1)}, bf16[12,256,128]{2,1,0:T(8,128)(2,1)S(1)}, u32[]{:S(2)}, u32[]{:S(2)}) collective-permute-start(bf16[12,256,128]{2,1,0:T(8,128)(2,1)S(1)} %constant_dynamic-slice_fusion), channel_id=1, source_target_pairs={{0,1},{1,0},{2,3},{3,2},{4,5},{5,4},{6,7},{7,6},{8,9},{9,8},{10,11... | collective-permute-start | bytes 2359304 | tf_op jit(solution)/shard_map/ppermute | solution.py:404
  81.9 1.9 %collective-permute-done.12 = bf16[12,256,128]{2,1,0:T(8,128)(2,1)S(1)} collective-permute-done((bf16[12,256,128]{2,1,0:T(8,128)(2,1)S(1)}, bf16[12,256,128]{2,1,0:T(8,128)(2,1)S(1)}, u32[]{:S(2)}, u32[]{:S(2)}) %collective-permute-start.12) | collective-permute-done | bytes 786464 | tf_op jit(solution)/shard_map/ppermute | solution.py:404
  83.8 1.5 %maximum_select_fusion = bf16[27,256,128]{2,1,0:T(8,128)(2,1)} fusion(bf16[12,256,128]{2,1,0:T(8,128)(2,1)S(1)} %collective-permute-done.12, bf16[15,256,128]{2,1,0:T(8,128)(2,1)S(1)} %get-tuple-element.20, pred[]{:T(512)S(6)} %eq.5), kind=kLoop, calls=%fused_computation | loop fusion | flops 2654208 | bytes 3538945 | tf_op jit(solution)/shard_map/jit(_where)/select_n | solution.py:487
  (19 shorter events, 0.8 us)
Async XLA Ops:
  0.6 26.4 %copy-start.2 = (bf16[128,256]{1,0:T(8,128)(2,1)S(1)}, bf16[128,256]{1,0:T(8,128)(2,1)}, u32[]{:S(2)}) copy-start(bf16[128,256]{1,0:T(8,128)(2,1)} %param.5) | copy-start | bytes 196612
  2.6 5.4 %collective-permute-start.6 = (bf16[1,272,128]{2,1,0:T(8,128)(2,1)}, bf16[1,272,128]{2,1,0:T(8,128)(2,1)S(1)}, u32[]{:S(2)}, u32[]{:S(2)}) collective-permute-start(bf16[1,272,128]{2,1,0:T(8,128)(2,1)} %bitcast.5), channel_id=1, source_target_pairs={{0,16},{1,9},{2,18},{3,11},{4,20},{5,13},{6,22},{7,15},{8,24},{9,1... | collective-permute-start | bytes 208904 | tf_op jit(solution)/shard_map/ppermute | solution.py:404
  5.5 6.6 %collective-permute-start = (bf16[1,128,256]{2,1,0:T(8,128)(2,1)}, bf16[1,128,256]{2,1,0:T(8,128)(2,1)S(1)}, u32[]{:S(2)}, u32[]{:S(2)}) collective-permute-start(bf16[1,128,256]{2,1,0:T(8,128)(2,1)} %bitcast.9), channel_id=1, source_target_pairs={{0,16},{1,9},{2,18},{3,11},{4,20},{5,13},{6,22},{7,15},{8,24},{9,1... | collective-permute-start | bytes 196616 | tf_op jit(solution)/shard_map/ppermute | solution.py:404
  8.9 31.4 %copy-start = (bf16[27,256,128]{2,1,0:T(8,128)(2,1)S(1)}, bf16[27,256,128]{2,1,0:T(8,128)(2,1)}, u32[]{:S(2)}) copy-start(bf16[27,256,128]{2,1,0:T(8,128)(2,1)} %weight.3) | copy-start | bytes 5308420
  8.9 31.4 %copy-start.1 = (s32[1,128]{1,0:T(1,128)S(1)}, s32[1,128]{1,0:T(1,128)}, u32[]{:S(2)}) copy-start(s32[1,128]{1,0:T(1,128)} %get-tuple-element.12.slot_ref) | copy-start | bytes 1540
  8.9 7.2 %collective-permute-start.7 = (bf16[2,272,128]{2,1,0:T(8,128)(2,1)S(1)}, bf16[2,272,128]{2,1,0:T(8,128)(2,1)S(1)}, u32[]{:S(2)}, u32[]{:S(2)}) collective-permute-start(bf16[2,272,128]{2,1,0:T(8,128)(2,1)S(1)} %pad_maximum_fusion.4), channel_id=1, source_target_pairs={{0,8},{1,5},{2,10},{3,7},{4,12},{5,1},{6,14},{7,3},{8,0},{9,13},{1... | collective-permute-start | bytes 417800 | tf_op jit(solution)/shard_map/ppermute | solution.py:404
  13.0 6.7 %collective-permute-start.1 = (bf16[2,128,256]{2,1,0:T(8,128)(2,1)S(1)}, bf16[2,128,256]{2,1,0:T(8,128)(2,1)S(1)}, u32[]{:S(2)}, u32[]{:S(2)}) collective-permute-start(bf16[2,128,256]{2,1,0:T(8,128)(2,1)S(1)} %pad_maximum_fusion.5), channel_id=1, source_target_pairs={{0,8},{1,5},{2,10},{3,7},{4,12},{5,1},{6,14},{7,3},{8,0},{9,13},{1... | collective-permute-start | bytes 393224 | tf_op jit(solution)/shard_map/ppermute | solution.py:404
  17.0 7.0 %collective-permute-start.8 = (bf16[4,272,128]{2,1,0:T(8,128)(2,1)S(1)}, bf16[4,272,128]{2,1,0:T(8,128)(2,1)S(1)}, u32[]{:S(2)}, u32[]{:S(2)}) collective-permute-start(bf16[4,272,128]{2,1,0:T(8,128)(2,1)S(1)} %pad_maximum_fusion.2), channel_id=1, source_target_pairs={{0,4},{1,3},{2,6},{3,1},{4,0},{5,7},{6,2},{7,5},{8,12},{9,11},{10,... | collective-permute-start | bytes 835592 | tf_op jit(solution)/shard_map/ppermute | solution.py:404
  20.6 6.4 %collective-permute-start.2 = (bf16[4,128,256]{2,1,0:T(8,128)(2,1)S(1)}, bf16[4,128,256]{2,1,0:T(8,128)(2,1)S(1)}, u32[]{:S(2)}, u32[]{:S(2)}) collective-permute-start(bf16[4,128,256]{2,1,0:T(8,128)(2,1)S(1)} %pad_maximum_fusion.3), channel_id=1, source_target_pairs={{0,4},{1,3},{2,6},{3,1},{4,0},{5,7},{6,2},{7,5},{8,12},{9,11},{10,... | collective-permute-start | bytes 786440 | tf_op jit(solution)/shard_map/ppermute | solution.py:404
  25.0 9.7 %collective-permute-start.9 = (bf16[8,272,128]{2,1,0:T(8,128)(2,1)S(1)}, bf16[8,272,128]{2,1,0:T(8,128)(2,1)}, u32[]{:S(2)}, u32[]{:S(2)}) collective-permute-start(bf16[8,272,128]{2,1,0:T(8,128)(2,1)S(1)} %pad_maximum_fusion.block0), channel_id=1, source_target_pairs={{0,2},{1,17},{2,0},{3,19},{4,6},{5,21},{6,4},{7,23},{8,10},{9,25},... | collective-permute-start | bytes 1671176 | tf_op jit(solution)/shard_map/ppermute | solution.py:404
  27.1 13.2 %collective-permute-start.3 = (bf16[8,128,256]{2,1,0:T(8,128)(2,1)S(1)}, bf16[8,128,256]{2,1,0:T(8,128)(2,1)}, u32[]{:S(2)}, u32[]{:S(2)}) collective-permute-start(bf16[8,128,256]{2,1,0:T(8,128)(2,1)S(1)} %pad_maximum_fusion.1.block0), channel_id=1, source_target_pairs={{0,2},{1,17},{2,0},{3,19},{4,6},{5,21},{6,4},{7,23},{8,10},{9,25},... | collective-permute-start | bytes 1572872 | tf_op jit(solution)/shard_map/ppermute | solution.py:404
  28.7 11.7 %collective-permute-start.10 = (bf16[8,272,128]{2,1,0:T(8,128)(2,1)S(1)}, bf16[8,272,128]{2,1,0:T(8,128)(2,1)}, u32[]{:S(2)}, u32[]{:S(2)}) collective-permute-start(bf16[8,272,128]{2,1,0:T(8,128)(2,1)S(1)} %pad_maximum_fusion.block0), channel_id=1, source_target_pairs={{0,1},{1,0},{2,3},{3,2},{4,5},{5,4},{6,7},{7,6},{8,9},{9,8},{10,11... | collective-permute-start | bytes 1671176 | tf_op jit(solution)/shard_map/ppermute | solution.py:404
  34.7 5.6 %collective-permute-start.11 = (bf16[8,272,128]{2,1,0:T(8,128)(2,1)}, bf16[8,272,128]{2,1,0:T(8,128)(2,1)}, u32[]{:S(2)}, u32[]{:S(2)}) collective-permute-start(bf16[8,272,128]{2,1,0:T(8,128)(2,1)} %collective-permute-done.9.block1), channel_id=1, source_target_pairs={{0,1},{1,0},{2,3},{3,2},{4,5},{5,4},{6,7},{7,6},{8,9},{9,8},{10,11... | collective-permute-start | bytes 1671176 | tf_op jit(solution)/shard_map/ppermute | solution.py:404
  34.7 19.7 %collective-permute-start.4 = (bf16[8,128,256]{2,1,0:T(8,128)(2,1)S(1)}, bf16[8,128,256]{2,1,0:T(8,128)(2,1)}, u32[]{:S(2)}, u32[]{:S(2)}) collective-permute-start(bf16[8,128,256]{2,1,0:T(8,128)(2,1)S(1)} %pad_maximum_fusion.1.block0), channel_id=1, source_target_pairs={{0,1},{1,0},{2,3},{3,2},{4,5},{5,4},{6,7},{7,6},{8,9},{9,8},{10,11... | collective-permute-start | bytes 1572872 | tf_op jit(solution)/shard_map/ppermute | solution.py:404
  40.3 14.1 %collective-permute-start.5 = (bf16[8,128,256]{2,1,0:T(8,128)(2,1)}, bf16[8,128,256]{2,1,0:T(8,128)(2,1)}, u32[]{:S(2)}, u32[]{:S(2)}) collective-permute-start(bf16[8,128,256]{2,1,0:T(8,128)(2,1)} %collective-permute-done.3.block1), channel_id=1, source_target_pairs={{0,1},{1,0},{2,3},{3,2},{4,5},{5,4},{6,7},{7,6},{8,9},{9,8},{10,11... | collective-permute-start | bytes 1572872 | tf_op jit(solution)/shard_map/ppermute | solution.py:404
  80.9 2.9 %collective-permute-start.12 = (bf16[12,256,128]{2,1,0:T(8,128)(2,1)S(1)}, bf16[12,256,128]{2,1,0:T(8,128)(2,1)S(1)}, u32[]{:S(2)}, u32[]{:S(2)}) collective-permute-start(bf16[12,256,128]{2,1,0:T(8,128)(2,1)S(1)} %constant_dynamic-slice_fusion), channel_id=1, source_target_pairs={{0,1},{1,0},{2,3},{3,2},{4,5},{5,4},{6,7},{7,6},{8,9},{9,8},{10,11... | collective-permute-start | bytes 2359304 | tf_op jit(solution)/shard_map/ppermute | solution.py:404

commit v3 on v2

--- a/solution.py
+++ b/solution.py
@@ -195,7 +195,7 @@
         padded[1 : size_x + 1, pl.ds(d * size_y + 1, size_y)] = found.reshape(size_x, size_y, TALL, LANES)
         return 0
 
-    lax.fori_loop(0, blk_count, stand, 0, unroll=2)
+    lax.fori_loop(0, blk_count, stand, 0, unroll=4)
 
     near = 1 - my_grp
     lines = pl.ds(pl.multiple_of(jnp.where(my_grp == 0, 0, size_x - 1) * size_y * TALL, size_y * TALL), size_y * TALL)
@@ -232,7 +232,7 @@
         taps = jnp.concatenate([weight[n * 3 + i] for i in range(3)], axis=1)
         return total + mm_t(windows, taps)
 
-    grad_rows[...] = lax.fori_loop(0, 9, backward, jnp.zeros((rows, channels), F32), unroll=3).astype(BF16)
+    grad_rows[...] = lax.fori_loop(0, 9, backward, jnp.zeros((rows, channels), F32), unroll=9).astype(BF16)
 
 
 def scene_kernel(
@@ -241,19 +241,19 @@
     block1,
     block2,
     block3,
-    weight,
     tiles,
     slot_rows,
     spots,
-    filled,
-    output,
+    padded,
     weight_grad,
+    sent,
     slots,
     grid,
-    shifted,
-    padded,
+    shifted0,
+    shifted1,
     acc_w,
-    acc_o,
+    kept,
+    sems,
 ):
     grp_count, blk_count, cap, rows, channels, size_x, size_y, size_z, scale = dims
     voxels = size_x * size_y * size_z
@@ -319,6 +319,95 @@
         for dy in (-1, 0, 1):
             outer(dx, dy)
 
+    acc_w[...] = jnp.zeros(acc_w.shape, F32)
+    offsets = ((-1, -1), (-1, 0), (-1, 1), (0, -1), (0, 0))
+    sign = 1 - 2 * half
+    lane = iota((LANES, LANES), 1)
+    x, y = lane // size_y, lane % size_y
+    nx = grp_count * size_x
+
+    def mask(hits):
+        return jnp.where(hits, 1.0, 0.0).astype(BF16)
+
+    within, across = [], []
+    for dx0, dy0 in offsets:
+        dx, dy = sign * dx0, sign * dy0
+        valid = (x - dx >= 0) & (x - dx < nx)
+        stays = (y - dy >= 0) & (y - dy < size_y)
+        within.append(mask(valid & stays))
+        across.append(mask(valid & jnp.logical_not(stays)))
+
+    def shift(z, d, there):
+        def tile(dy):
+            return tiles[z, :, pl.ds(pl.multiple_of((d + 1 - dy) * LANES, LANES), LANES)]
+
+        own = tile(0)
+        beside = {dy0: tile(sign * dy0) for dy0 in (-1, 1)}
+        cols = pl.ds(pl.multiple_of(d * LANES, LANES), LANES)
+        for m, (dx0, dy0) in enumerate(offsets):
+            value = own
+            if dx0 or dy0:
+                ahead = sign * (dx0 * size_y + dy0)
+                value = pltpu.roll(own, (ahead + LANES) % LANES, 1) * within[m]
+            if dy0:
+                ahead = sign * (dx0 * size_y + dy0 - dy0 * size_y)
+                value = value + pltpu.roll(beside[dy0], (ahead + LANES) % LANES, 1) * across[m]
+            there[m * LANES : (m + 1) * LANES, cols] = value
+
+    def shift_first(d, _):
+        shift(0, d, shifted0)
+        return 0
+
+    lax.fori_loop(0, blk_count, shift_first, 0, unroll=8)
+    for z in range(size_z):
+        here, there = (shifted0, shifted1) if z % 2 == 0 else (shifted1, shifted0)
+        first, count = max(0, 1 - z), min(3, size_z + 1 - z) - max(0, 1 - z)
+        share = -(-blk_count // count)
+
+        def add(j, _, z=z, here=here, there=there, first=first, share=share):
+            dz1 = first + j
+            done = 0
+            for m in range(5):
+                rows_m = slice(m * LANES, (m + 1) * LANES)
+                acc_w[dz1, rows_m] += mm(here[rows_m, :], grid[z + dz1 - 1])
+                if z + 1 < size_z:
+                    for i in range(done, share * (m + 1) // 5):
+                        shift(z + 1, jnp.minimum(j * share + i, blk_count - 1), there)
+                    done = share * (m + 1) // 5
+            return 0
+
+        lax.fori_loop(0, count, add, 0)
+
+    def finish(dz1, _):
+        done = (acc_w[dz1].T * scale).astype(BF16)
+        for m in range(5):
+            n = m + half * (4 - 2 * m)
+            piece = done[:, m * LANES : (m + 1) * LANES]
+            kept[n * 3 + dz1] = piece
+        return 0
+
+    lax.fori_loop(0, 3, finish, 0)
+    mine = pltpu.make_async_copy(kept, weight_grad.at[pl.ds(12 * half, 15)], sems.at[0])
+    theirs = pltpu.make_async_copy(kept.at[pl.ds(3 * half, 12)], sent, sems.at[1])
+    theirs.start()
+    mine.start()
+    theirs.wait()
+    mine.wait()
+
+
+def place_kernel(received, mine, weight_grad, sem):
+    other = 1 - lax.axis_index("blk") % 2
+    copy = pltpu.make_async_copy(received, weight_grad.at[pl.ds(15 * other, 12)], sem)
+    copy.start()
+    copy.wait()
+
+
+def output_kernel(sizes, padded, weight, spots, filled, output, acc_o):
+    size_x, size_y, size_z = sizes
+    voxels = size_x * size_y * size_z
+    plane = size_x * size_y
+    channels = weight.shape[1]
+    me = lax.axis_index("grp") * lax.axis_size("blk") + lax.axis_index("blk")
     acc_o[...] = jnp.zeros(acc_o.shape, F32)
 
     def forward(n, _):
@@ -328,7 +417,7 @@
         acc_o[...] += mm(window.astype(BF16), taps)
         return 0
 
-    lax.fori_loop(0, 9, forward, 0)
+    lax.fori_loop(0, 9, forward, 0, unroll=3)
     spot = spots[pl.ds(me, 1), :]
     key = jnp.where(filled[pl.ds(me, 1), :] > 0, spot // size_z * TALL + spot % size_z + 1, -1)
     occupied = mm(one_hot(iota((plane * TALL, voxels), 0) == key), jnp.ones((voxels, LANES), BF16))
@@ -342,57 +431,6 @@
     squeeze = one_hot(col == row // size_z * TALL + row % size_z + 1)
     output[...] = mm(squeeze, rounded).astype(BF16)
 
-    acc_w[...] = jnp.zeros(acc_w.shape, F32)
-    lane = iota((LANES, LANES), 1)
-    x, y = lane // size_y, lane % size_y
-    nx = grp_count * size_x
-    zero = jnp.zeros((LANES, LANES), BF16)
-
-    def for_z(z, _):
-        for own_half in range(2):
-
-            def shift(d, _, own_half=own_half):
-                def tile(offset):
-                    return tiles[z, :, pl.ds(pl.multiple_of((d + 1 + offset) * LANES, LANES), LANES)]
-
-                cols = pl.ds(pl.multiple_of(d * LANES, LANES), LANES)
-                beside = {dy: tile(-dy) for dy in (-1, 0, 1)}
-                for n in range(5):
-                    place = n + 4 * own_half
-                    dx, dy = place // 3 - 1, place % 3 - 1
-                    ahead = dx * size_y + dy
-                    value = beside[0]
-                    if ahead:
-                        value = pltpu.roll(value, ahead % LANES, 1)
-                    if dy:
-                        crossing = y == (0 if dy > 0 else size_y - 1)
-                        value = jnp.where(crossing, pltpu.roll(beside[dy], (ahead - dy * size_y) % LANES, 1), value)
-                    if dx:
-                        value = jnp.where((x - dx >= 0) & (x - dx < nx), value, zero)
-                    shifted[n * LANES : (n + 1) * LANES, cols] = value
-                return 0
-
-            @pl.when(half == own_half)
-            def _(shift=shift):
-                lax.fori_loop(0, blk_count, shift, 0, unroll=2)
-
-        def add(dz1, _):
-            acc_w[dz1] += mm(shifted[...], grid[z + dz1 - 1])
-            return 0
-
-        lax.fori_loop(jnp.where(z == 0, 1, 0), jnp.where(z == size_z - 1, 2, 3), add, 0)
-        return 0
-
-    lax.fori_loop(0, size_z, for_z, 0)
-
-    def finish(dz1, _):
-        done = (acc_w[dz1].T * scale).astype(BF16)
-        for n in range(5):
-            weight_grad[n * 3 + dz1] = done[:, n * LANES : (n + 1) * LANES]
-        return 0
-
-    lax.fori_loop(0, 3, finish, 0)
-
 
 def exchange_masks(count):
     even = [1 << i for i in range(count.bit_length() - 2, 0, -1)]
@@ -424,6 +462,7 @@
     cap = voxels // blk_count
     vmem = pl.BlockSpec(memory_space=pltpu.VMEM)
     smem = pl.BlockSpec(memory_space=pltpu.SMEM)
+    hbm = pl.BlockSpec(memory_space=pl.ANY)
     packed, slot = pl.pallas_call(
         functools.partial(pack_kernel, sizes, cap),
         out_shape=(
@@ -458,37 +497,50 @@
             pltpu.SMEM((blk_count, voxels), I32),
             pltpu.SemaphoreType.DMA,
         ],
-        compiler_params=pltpu.CompilerParams(vmem_limit_bytes=28 * 1024 * 1024),
+        compiler_params=pltpu.CompilerParams(vmem_limit_bytes=24 * 1024 * 1024),
         name="cotangent",
     )(slot, *cotangents, weight)
     scale = 1.0 / math.sqrt(rows * devices)
-    output, some = pl.pallas_call(
+    padded, some, sent = pl.pallas_call(
         functools.partial(scene_kernel, dims + (scale,)),
         out_shape=(
-            jax.ShapeDtypeStruct((voxels, out_channels), BF16),
-            jax.ShapeDtypeStruct((15, channels, out_channels), BF16),
+            jax.ShapeDtypeStruct((size_x + 2, size_y + 2, TALL, channels), F32),
+            jax.ShapeDtypeStruct(weight.shape, BF16),
+            jax.ShapeDtypeStruct((12, channels, out_channels), BF16),
         ),
-        in_specs=[vmem] * 9,
-        out_specs=(vmem, vmem),
+        in_specs=[vmem] * 7,
+        out_specs=(vmem, hbm, hbm),
         scratch_shapes=[
             pltpu.VMEM((devices, voxels, channels), BF16),
             pltpu.VMEM((size_z, blk_count * LANES, channels), BF16),
             pltpu.VMEM((5 * out_channels, blk_count * LANES), BF16),
-            pltpu.VMEM((size_x + 2, size_y + 2, TALL, channels), F32),
+            pltpu.VMEM((5 * out_channels, blk_count * LANES), BF16),
             pltpu.VMEM((3, 5 * out_channels, channels), F32),
-            pltpu.VMEM((plane * TALL, 3 * out_channels), F32),
+            pltpu.VMEM((15, channels, out_channels), BF16),
+            pltpu.SemaphoreType.DMA((2,)),
         ],
-        compiler_params=pltpu.CompilerParams(vmem_limit_bytes=36 * 1024 * 1024),
+        compiler_params=pltpu.CompilerParams(vmem_limit_bytes=24 * 1024 * 1024),
         name="scene",
-    )(*cells, weight, tiles, slot_rows, spots, filled)
-    odd = lax.axis_index("blk") % 2
-    sent = lax.dynamic_slice_in_dim(some, 3 * odd, 12, axis=0)
+    )(*cells, tiles, slot_rows, spots)
     received = swap(sent, devices, (1, 1))
-    weight_grad = jnp.where(
-        odd == 0,
-        jnp.concatenate([some, received], axis=0),
-        jnp.concatenate([received, some], axis=0),
-    )
+    output = pl.pallas_call(
+        functools.partial(output_kernel, sizes),
+        out_shape=jax.ShapeDtypeStruct((voxels, out_channels), BF16),
+        in_specs=[vmem] * 4,
+        out_specs=vmem,
+        scratch_shapes=[pltpu.VMEM((plane * TALL, 3 * out_channels), F32)],
+        compiler_params=pltpu.CompilerParams(vmem_limit_bytes=8 * 1024 * 1024),
+        name="output",
+    )(padded, weight, spots, filled)
+    weight_grad = pl.pallas_call(
+        place_kernel,
+        out_shape=jax.ShapeDtypeStruct(weight.shape, BF16),
+        in_specs=[vmem, hbm],
+        out_specs=hbm,
+        scratch_shapes=[pltpu.SemaphoreType.DMA],
+        input_output_aliases={1: 0},
+        name="place",
+    )(received, some)
     return output.reshape(grad_out.shape), grad_rows, weight_grad
 
 

time: 86.6 us -> 78.5 us (0.906)
  Pallas kernels: 42.4 us -> 37.4 us
  waiting for transfers between devices: 20.6 us -> 18.6 us
  other arithmetic: 6 us -> 4.52 us
    pallas_call x1, Pallas kernels: 26.5 us -> 18.4 us  [gathered_shards(): pl.pallas_call(functools.partial(scene_kernel, dims + (scale,)), out_shap...]
    pallas_call x0 -> x2, Pallas kernels: none -> 4.91 us  [the longest x1 2.89 us: gathered_shards(): pl.pallas_call(functools.partial(output_kernel, sizes), out_shape=jax.Sha...]
    ppermute x13, waiting for transfers between devices: 20.6 us -> 18.6 us  [swap(): return lax.ppermute(value, ('grp', 'blk'), pairs)]
    pallas_call x1, Pallas kernels: 14 us -> 12.2 us  [gathered_shards(): pl.pallas_call(functools.partial(cotangent_kernel, dims), out_shape=(jax....]
    select_n x1 -> x0, other arithmetic: 1.48 us -> none  [gathered_shards(): jnp.where(odd == 0, jnp.concatenate([some, received], axis=0), jnp.concat...]
    unnamed x6 -> x8, local copies, waits for them, and re-layouts: 0.02 us -> 0.91 us
  transfers between devices with their start and end apart: 13 -> 13, of which waited for: 8 -> 7; matrix products, arithmetic and copies ran while one was open for 5% -> 6% of each run, Pallas kernels for 16% -> 19%
where the time goes in v3:
time: 78.5 us; the launch traced here: 77.5 us
  Pallas kernels  37.4 us (48%)
  waiting for transfers between devices  18.6 us (24%)
  starting transfers between devices  15.3 us (19%)
  other arithmetic  4.52 us (6%)
  local copies, waits for them, and re-layouts  0.91 us (1%)
    ppermute x13, waiting for transfers between devices, swap(): return lax.ppermute(value, ('grp', 'blk'), pairs)  18.6 us
    pallas_call x1, Pallas kernels, gathered_shards(): pl.pallas_call(functools.partial(scene_kernel, dims + (scale,)), out_shap...  18.4 us
    ppermute x13, starting transfers between devices, swap(): return lax.ppermute(value, ('grp', 'blk'), pairs)  15.3 us
    pallas_call x1, Pallas kernels, gathered_shards(): pl.pallas_call(functools.partial(cotangent_kernel, dims), out_shape=(jax....  12.2 us
    concatenate x6, other arithmetic, gather_all(): jnp.concatenate([held, swap(held, count, (even[step], odd[step]))], axis=0)  4.52 us
    pallas_call x1, Pallas kernels, gathered_shards(): pl.pallas_call(functools.partial(output_kernel, sizes), out_shape=jax.Sha...  2.89 us
    pallas_call x1, Pallas kernels, gathered_shards(): pl.pallas_call(place_kernel, out_shape=jax.ShapeDtypeStruct(weight.shape,...  2.02 us
    pallas_call x1, Pallas kernels, gathered_shards(): pl.pallas_call(functools.partial(pack_kernel, sizes, cap), out_shape=(jax...  1.91 us
  transfers between devices with their start and end apart: 13, of which 7 were waited for; matrix products, arithmetic and copies ran while one was open for 6% of the time, Pallas kernels for 19%

profile of v3, /device:TPU:0, one launch (start us, length us, event | category | flops | bytes accessed | tf_op | source)
XLA Modules:
  0.0 77.5 jit_solution(2286429449398442010)
XLA Ops:
  0.6 1.9 %pack.1 = (bf16[272,128]{1,0:T(8,128)(2,1)}, s32[1,128]{1,0:T(1,128)}) custom-call(s32[1,128]{1,0:T(1,128)} %bitcast.15, s32[1,256]{1,0:T(1,128)} %placement.1, bf16[256,128]{1,0:T(8,128)(2,1)} %bitcast.14), custom_call_target="tpu_custom_call" | custom-call | tf_op jit(solution)/shard_map/pack/pallas_call | solution.py:466
  2.6 2.9 %collective-permute-start.6 = (bf16[1,272,128]{2,1,0:T(8,128)(2,1)}, bf16[1,272,128]{2,1,0:T(8,128)(2,1)S(1)}, u32[]{:S(2)}, u32[]{:S(2)}) collective-permute-start(bf16[1,272,128]{2,1,0:T(8,128)(2,1)} %bitcast.5), channel_id=1, source_target_pairs={{0,16},{1,9},{2,18},{3,11},{4,20},{5,13},{6,22},{7,15},{8,24},{9,1... | collective-permute-start | bytes 208904 | tf_op jit(solution)/shard_map/ppermute | solution.py:442
  5.5 2.5 %collective-permute-done.6 = bf16[1,272,128]{2,1,0:T(8,128)(2,1)S(1)} collective-permute-done((bf16[1,272,128]{2,1,0:T(8,128)(2,1)}, bf16[1,272,128]{2,1,0:T(8,128)(2,1)S(1)}, u32[]{:S(2)}, u32[]{:S(2)}) %collective-permute-start.6) | collective-permute-done | bytes 69664 | tf_op jit(solution)/shard_map/ppermute | solution.py:442
  8.0 0.9 %pad_maximum_fusion.4 = bf16[2,272,128]{2,1,0:T(8,128)(2,1)S(1)} fusion(bf16[1,272,128]{2,1,0:T(8,128)(2,1)S(1)} %collective-permute-done.6, bf16[1,272,128]{2,1,0:T(8,128)(2,1)} %bitcast.6), kind=kLoop, calls=%fused_computation.4 | loop fusion | flops 69632 | bytes 278528 | tf_op jit(solution)/shard_map/concatenate | solution.py:449
  8.9 3.2 %collective-permute-start.7 = (bf16[2,272,128]{2,1,0:T(8,128)(2,1)S(1)}, bf16[2,272,128]{2,1,0:T(8,128)(2,1)S(1)}, u32[]{:S(2)}, u32[]{:S(2)}) collective-permute-start(bf16[2,272,128]{2,1,0:T(8,128)(2,1)S(1)} %pad_maximum_fusion.4), channel_id=1, source_target_pairs={{0,8},{1,5},{2,10},{3,7},{4,12},{5,1},{6,14},{7,3},{8,0},{9,13},{1... | collective-permute-start | bytes 417800 | tf_op jit(solution)/shard_map/ppermute | solution.py:442
  12.1 0.9 %pad_maximum_fusion.5 = bf16[2,128,256]{2,1,0:T(8,128)(2,1)S(1)} fusion(bf16[1,128,256]{2,1,0:T(8,128)(2,1)S(1)} %collective-permute-done, bf16[1,128,256]{2,1,0:T(8,128)(2,1)} %bitcast.10), kind=kLoop, calls=%fused_computation.5 | loop fusion | flops 65536 | bytes 262144 | tf_op jit(solution)/shard_map/concatenate | solution.py:449
  13.0 0.5 collective-permute-start.1
  13.5 2.6 %collective-permute-done.7 = bf16[2,272,128]{2,1,0:T(8,128)(2,1)S(1)} collective-permute-done((bf16[2,272,128]{2,1,0:T(8,128)(2,1)S(1)}, bf16[2,272,128]{2,1,0:T(8,128)(2,1)S(1)}, u32[]{:S(2)}, u32[]{:S(2)}) %collective-permute-start.7) | collective-permute-done | bytes 139296 | tf_op jit(solution)/shard_map/ppermute | solution.py:442
  16.1 0.9 %pad_maximum_fusion.2 = bf16[4,272,128]{2,1,0:T(8,128)(2,1)S(1)} fusion(bf16[2,272,128]{2,1,0:T(8,128)(2,1)S(1)} %collective-permute-done.7, bf16[1,272,128]{2,1,0:T(8,128)(2,1)S(1)} %collective-permute-done.6, bf16[1,272,128]{2,1,0:T(8,128)(2,1)} %bitcast.7), kind=kLoop, calls=%fused_computation.2 | loop fusion | flops 278528 | bytes 557056 | tf_op jit(solution)/shard_map/concatenate | solution.py:449
  17.0 2.5 %collective-permute-start.8 = (bf16[4,272,128]{2,1,0:T(8,128)(2,1)S(1)}, bf16[4,272,128]{2,1,0:T(8,128)(2,1)S(1)}, u32[]{:S(2)}, u32[]{:S(2)}) collective-permute-start(bf16[4,272,128]{2,1,0:T(8,128)(2,1)S(1)} %pad_maximum_fusion.2), channel_id=1, source_target_pairs={{0,4},{1,3},{2,6},{3,1},{4,0},{5,7},{6,2},{7,5},{8,12},{9,11},{10,... | collective-permute-start | bytes 835592 | tf_op jit(solution)/shard_map/ppermute | solution.py:442
  19.7 0.9 %pad_maximum_fusion.3 = bf16[4,128,256]{2,1,0:T(8,128)(2,1)S(1)} fusion(bf16[2,128,256]{2,1,0:T(8,128)(2,1)S(1)} %collective-permute-done.1, bf16[1,128,256]{2,1,0:T(8,128)(2,1)S(1)} %collective-permute-done, bf16[1,128,256]{2,1,0:T(8,128)(2,1)} %bitcast.11), kind=kLoop, calls=%fused_computation.3 | loop fusion | flops 262144 | bytes 524288 | tf_op jit(solution)/shard_map/concatenate | solution.py:449
  20.6 1.6 %collective-permute-start.2 = (bf16[4,128,256]{2,1,0:T(8,128)(2,1)S(1)}, bf16[4,128,256]{2,1,0:T(8,128)(2,1)S(1)}, u32[]{:S(2)}, u32[]{:S(2)}) collective-permute-start(bf16[4,128,256]{2,1,0:T(8,128)(2,1)S(1)} %pad_maximum_fusion.3), channel_id=1, source_target_pairs={{0,4},{1,3},{2,6},{3,1},{4,0},{5,7},{6,2},{7,5},{8,12},{9,11},{10,... | collective-permute-start | bytes 786440 | tf_op jit(solution)/shard_map/ppermute | solution.py:442
  22.2 1.9 %collective-permute-done.8 = bf16[4,272,128]{2,1,0:T(8,128)(2,1)S(1)} collective-permute-done((bf16[4,272,128]{2,1,0:T(8,128)(2,1)S(1)}, bf16[4,272,128]{2,1,0:T(8,128)(2,1)S(1)}, u32[]{:S(2)}, u32[]{:S(2)}) %collective-permute-start.8) | collective-permute-done | bytes 278560 | tf_op jit(solution)/shard_map/ppermute | solution.py:442
  24.0 0.9 %pad_maximum_fusion.block0 = bf16[8,272,128]{2,1,0:T(8,128)(2,1)S(1)} fusion(bf16[4,272,128]{2,1,0:T(8,128)(2,1)S(1)} %collective-permute-done.8, bf16[2,272,128]{2,1,0:T(8,128)(2,1)S(1)} %collective-permute-done.7, bf16[1,272,128]{2,1,0:T(8,128)(2,1)S(1)} %collective-permute-done.6, bf16[1,272,128]{2,1,0:T(8,128)(2,1)} %bitcast.8), kind=kLoop, calls=%fused_computation | loop fusion | flops 835584 | bytes 1114112 | tf_op jit(solution)/shard_map/concatenate | solution.py:449
  25.0 1.6 %collective-permute-start.9 = (bf16[8,272,128]{2,1,0:T(8,128)(2,1)S(1)}, bf16[8,272,128]{2,1,0:T(8,128)(2,1)S(1)}, u32[]{:S(2)}, u32[]{:S(2)}) collective-permute-start(bf16[8,272,128]{2,1,0:T(8,128)(2,1)S(1)} %pad_maximum_fusion.block0), channel_id=1, source_target_pairs={{0,2},{1,17},{2,0},{3,19},{4,6},{5,21},{6,4},{7,23},{8,10},{9,25},... | collective-permute-start | bytes 1671176 | tf_op jit(solution)/shard_map/ppermute | solution.py:442
  27.1 1.6 %collective-permute-start.3 = (bf16[8,128,256]{2,1,0:T(8,128)(2,1)S(1)}, bf16[8,128,256]{2,1,0:T(8,128)(2,1)S(1)}, u32[]{:S(2)}, u32[]{:S(2)}) collective-permute-start(bf16[8,128,256]{2,1,0:T(8,128)(2,1)S(1)} %pad_maximum_fusion.1.block0), channel_id=1, source_target_pairs={{0,2},{1,17},{2,0},{3,19},{4,6},{5,21},{6,4},{7,23},{8,10},{9,25},... | collective-permute-start | bytes 1572872 | tf_op jit(solution)/shard_map/ppermute | solution.py:442
  28.7 5.9 %collective-permute-done.9.block1 = bf16[8,272,128]{2,1,0:T(8,128)(2,1)S(1)} collective-permute-done((bf16[8,272,128]{2,1,0:T(8,128)(2,1)S(1)}, bf16[8,272,128]{2,1,0:T(8,128)(2,1)S(1)}, u32[]{:S(2)}, u32[]{:S(2)}) %collective-permute-start.9) | collective-permute-done | bytes 557088 | tf_op jit(solution)/shard_map/ppermute | solution.py:442
  35.1 5.1 %collective-permute-done.3.block1 = bf16[8,128,256]{2,1,0:T(8,128)(2,1)S(1)} collective-permute-done((bf16[8,128,256]{2,1,0:T(8,128)(2,1)S(1)}, bf16[8,128,256]{2,1,0:T(8,128)(2,1)S(1)}, u32[]{:S(2)}, u32[]{:S(2)}) %collective-permute-start.3) | collective-permute-done | bytes 524320 | tf_op jit(solution)/shard_map/ppermute | solution.py:442
  40.2 12.2 %cotangent.1 = (bf16[128,256]{1,0:T(8,128)(2,1)}, bf16[4,128,2304]{2,1,0:T(8,128)(2,1)S(1)}, s32[32,128]{1,0:T(8,128)S(1)}, s32[32,256]{1,0:T(8,128)S(1)}, f32[32,256]{1,0:T(8,128)S(1)}) custom-call(s32[1,128]{1,0:T(1,128)S(1)} %copy-done.1, bf16[8,272,128]{2,1,0:T(8,128)(2,1)S(1)} %pad_maximum_fusion.block0, ...), custom_call_target="tpu_custom_call" | custom-call | tf_op jit(solution)/shard_map/cotangent/pallas_call | solution.py:479
  52.5 18.4 %scene.1 = (f32[10,10,8,256]{3,2,1,0:T(8,128)S(1)}, bf16[27,256,128]{2,1,0:T(8,128)(2,1)}, bf16[12,256,128]{2,1,0:T(8,128)(2,1)S(1)}) custom-call(bf16[8,128,256]{2,1,0:T(8,128)(2,1)S(1)} %pad_maximum_fusion.1.block0, bf16[8,128,256]{2,1,0:T(8,128)(2,1)S(1)} %collective-permute-done.3.block1, bf16[8,128,256]{2,1,0:T(8,128)(2,1)S(1)} %collective-permute-done.4.block2, ...), custom_call_target="tpu_custom_call" | custom-call | tf_op jit(solution)/shard_map/scene/pallas_call | solution.py:504
  70.9 0.9 %collective-permute-start.12 = (bf16[12,256,128]{2,1,0:T(8,128)(2,1)S(1)}, bf16[12,256,128]{2,1,0:T(8,128)(2,1)S(1)}, u32[]{:S(2)}, u32[]{:S(2)}) collective-permute-start(bf16[12,256,128]{2,1,0:T(8,128)(2,1)S(1)} %get-tuple-element.21), channel_id=1, source_target_pairs={{0,1},{1,0},{2,3},{3,2},{4,5},{5,4},{6,7},{7,6},{8,9},{9,8},{10,11... | collective-permute-start | bytes 2359304 | tf_op jit(solution)/shard_map/ppermute | solution.py:442
  71.7 2.9 %output.1 = bf16[256,128]{1,0:T(8,128)(2,1)} custom-call(f32[10,10,8,256]{3,2,1,0:T(8,128)S(1)} %get-tuple-element.18.padded, bf16[27,256,128]{2,1,0:T(8,128)(2,1)S(1)} %copy-done, s32[32,256]{1,0:T(8,128)S(1)} %get-tuple-element.17.spots, f32[32,256]{1,0:T(8,128)S(1)} %get-tuple-element.19.filled), custom_call_target="tpu_custom_call" | custom-call | tf_op jit(solution)/shard_map/output/pallas_call | solution.py:526
  74.6 0.9 %copy-done.2 = bf16[12,256,128]{2,1,0:T(8,128)(2,1)} copy-done((bf16[12,256,128]{2,1,0:T(8,128)(2,1)}, bf16[12,256,128]{2,1,0:T(8,128)(2,1)S(1)}, u32[]{:S(2)}) %copy-start.2) | copy-done | bytes 786456
  75.5 2.0 %place.1 = bf16[27,256,128]{2,1,0:T(8,128)(2,1)} custom-call(bf16[12,256,128]{2,1,0:T(8,128)(2,1)} %copy-done.2, bf16[27,256,128]{2,1,0:T(8,128)(2,1)} %get-tuple-element.22.mine), custom_call_target="tpu_custom_call", output_to_operand_aliasing={{}: (1, {})} | custom-call | tf_op jit(solution)/shard_map/place/pallas_call | solution.py:535
  (21 shorter events, 1.3 us)
Async XLA Ops:
  0.6 26.4 %copy-start.3 = (bf16[128,256]{1,0:T(8,128)(2,1)S(1)}, bf16[128,256]{1,0:T(8,128)(2,1)}, u32[]{:S(2)}) copy-start(bf16[128,256]{1,0:T(8,128)(2,1)} %param.5) | copy-start | bytes 196612
  2.6 5.4 %collective-permute-start.6 = (bf16[1,272,128]{2,1,0:T(8,128)(2,1)}, bf16[1,272,128]{2,1,0:T(8,128)(2,1)S(1)}, u32[]{:S(2)}, u32[]{:S(2)}) collective-permute-start(bf16[1,272,128]{2,1,0:T(8,128)(2,1)} %bitcast.5), channel_id=1, source_target_pairs={{0,16},{1,9},{2,18},{3,11},{4,20},{5,13},{6,22},{7,15},{8,24},{9,1... | collective-permute-start | bytes 208904 | tf_op jit(solution)/shard_map/ppermute | solution.py:442
  5.5 6.6 %collective-permute-start = (bf16[1,128,256]{2,1,0:T(8,128)(2,1)}, bf16[1,128,256]{2,1,0:T(8,128)(2,1)S(1)}, u32[]{:S(2)}, u32[]{:S(2)}) collective-permute-start(bf16[1,128,256]{2,1,0:T(8,128)(2,1)} %bitcast.9), channel_id=1, source_target_pairs={{0,16},{1,9},{2,18},{3,11},{4,20},{5,13},{6,22},{7,15},{8,24},{9,1... | collective-permute-start | bytes 196616 | tf_op jit(solution)/shard_map/ppermute | solution.py:442
  8.9 31.3 %copy-start = (bf16[27,256,128]{2,1,0:T(8,128)(2,1)S(1)}, bf16[27,256,128]{2,1,0:T(8,128)(2,1)}, u32[]{:S(2)}) copy-start(bf16[27,256,128]{2,1,0:T(8,128)(2,1)} %weight.3) | copy-start | bytes 5308420
  8.9 31.3 %copy-start.1 = (s32[1,128]{1,0:T(1,128)S(1)}, s32[1,128]{1,0:T(1,128)}, u32[]{:S(2)}) copy-start(s32[1,128]{1,0:T(1,128)} %get-tuple-element.13.slot_ref) | copy-start | bytes 1540
  8.9 7.2 %collective-permute-start.7 = (bf16[2,272,128]{2,1,0:T(8,128)(2,1)S(1)}, bf16[2,272,128]{2,1,0:T(8,128)(2,1)S(1)}, u32[]{:S(2)}, u32[]{:S(2)}) collective-permute-start(bf16[2,272,128]{2,1,0:T(8,128)(2,1)S(1)} %pad_maximum_fusion.4), channel_id=1, source_target_pairs={{0,8},{1,5},{2,10},{3,7},{4,12},{5,1},{6,14},{7,3},{8,0},{9,13},{1... | collective-permute-start | bytes 417800 | tf_op jit(solution)/shard_map/ppermute | solution.py:442
  13.0 6.7 %collective-permute-start.1 = (bf16[2,128,256]{2,1,0:T(8,128)(2,1)S(1)}, bf16[2,128,256]{2,1,0:T(8,128)(2,1)S(1)}, u32[]{:S(2)}, u32[]{:S(2)}) collective-permute-start(bf16[2,128,256]{2,1,0:T(8,128)(2,1)S(1)} %pad_maximum_fusion.5), channel_id=1, source_target_pairs={{0,8},{1,5},{2,10},{3,7},{4,12},{5,1},{6,14},{7,3},{8,0},{9,13},{1... | collective-permute-start | bytes 393224 | tf_op jit(solution)/shard_map/ppermute | solution.py:442
  17.0 7.0 %collective-permute-start.8 = (bf16[4,272,128]{2,1,0:T(8,128)(2,1)S(1)}, bf16[4,272,128]{2,1,0:T(8,128)(2,1)S(1)}, u32[]{:S(2)}, u32[]{:S(2)}) collective-permute-start(bf16[4,272,128]{2,1,0:T(8,128)(2,1)S(1)} %pad_maximum_fusion.2), channel_id=1, source_target_pairs={{0,4},{1,3},{2,6},{3,1},{4,0},{5,7},{6,2},{7,5},{8,12},{9,11},{10,... | collective-permute-start | bytes 835592 | tf_op jit(solution)/shard_map/ppermute | solution.py:442
  20.6 6.4 %collective-permute-start.2 = (bf16[4,128,256]{2,1,0:T(8,128)(2,1)S(1)}, bf16[4,128,256]{2,1,0:T(8,128)(2,1)S(1)}, u32[]{:S(2)}, u32[]{:S(2)}) collective-permute-start(bf16[4,128,256]{2,1,0:T(8,128)(2,1)S(1)} %pad_maximum_fusion.3), channel_id=1, source_target_pairs={{0,4},{1,3},{2,6},{3,1},{4,0},{5,7},{6,2},{7,5},{8,12},{9,11},{10,... | collective-permute-start | bytes 786440 | tf_op jit(solution)/shard_map/ppermute | solution.py:442
  25.0 9.6 %collective-permute-start.9 = (bf16[8,272,128]{2,1,0:T(8,128)(2,1)S(1)}, bf16[8,272,128]{2,1,0:T(8,128)(2,1)S(1)}, u32[]{:S(2)}, u32[]{:S(2)}) collective-permute-start(bf16[8,272,128]{2,1,0:T(8,128)(2,1)S(1)} %pad_maximum_fusion.block0), channel_id=1, source_target_pairs={{0,2},{1,17},{2,0},{3,19},{4,6},{5,21},{6,4},{7,23},{8,10},{9,25},... | collective-permute-start | bytes 1671176 | tf_op jit(solution)/shard_map/ppermute | solution.py:442
  27.1 13.1 %collective-permute-start.3 = (bf16[8,128,256]{2,1,0:T(8,128)(2,1)S(1)}, bf16[8,128,256]{2,1,0:T(8,128)(2,1)S(1)}, u32[]{:S(2)}, u32[]{:S(2)}) collective-permute-start(bf16[8,128,256]{2,1,0:T(8,128)(2,1)S(1)} %pad_maximum_fusion.1.block0), channel_id=1, source_target_pairs={{0,2},{1,17},{2,0},{3,19},{4,6},{5,21},{6,4},{7,23},{8,10},{9,25},... | collective-permute-start | bytes 1572872 | tf_op jit(solution)/shard_map/ppermute | solution.py:442
  28.7 11.6 %collective-permute-start.10 = (bf16[8,272,128]{2,1,0:T(8,128)(2,1)S(1)}, bf16[8,272,128]{2,1,0:T(8,128)(2,1)S(1)}, u32[]{:S(2)}, u32[]{:S(2)}) collective-permute-start(bf16[8,272,128]{2,1,0:T(8,128)(2,1)S(1)} %pad_maximum_fusion.block0), channel_id=1, source_target_pairs={{0,1},{1,0},{2,3},{3,2},{4,5},{5,4},{6,7},{7,6},{8,9},{9,8},{10,11... | collective-permute-start | bytes 1671176 | tf_op jit(solution)/shard_map/ppermute | solution.py:442
  34.6 5.6 %collective-permute-start.11 = (bf16[8,272,128]{2,1,0:T(8,128)(2,1)S(1)}, bf16[8,272,128]{2,1,0:T(8,128)(2,1)S(1)}, u32[]{:S(2)}, u32[]{:S(2)}) collective-permute-start(bf16[8,272,128]{2,1,0:T(8,128)(2,1)S(1)} %collective-permute-done.9.block1), channel_id=1, source_target_pairs={{0,1},{1,0},{2,3},{3,2},{4,5},{5,4},{6,7},{7,6},{8,9},{9,8},{10,11... | collective-permute-start | bytes 1671176 | tf_op jit(solution)/shard_map/ppermute | solution.py:442
  34.6 17.9 %collective-permute-start.4 = (bf16[8,128,256]{2,1,0:T(8,128)(2,1)S(1)}, bf16[8,128,256]{2,1,0:T(8,128)(2,1)S(1)}, u32[]{:S(2)}, u32[]{:S(2)}) collective-permute-start(bf16[8,128,256]{2,1,0:T(8,128)(2,1)S(1)} %pad_maximum_fusion.1.block0), channel_id=1, source_target_pairs={{0,1},{1,0},{2,3},{3,2},{4,5},{5,4},{6,7},{7,6},{8,9},{9,8},{10,11... | collective-permute-start | bytes 1572872 | tf_op jit(solution)/shard_map/ppermute | solution.py:442
  40.2 12.2 %collective-permute-start.5 = (bf16[8,128,256]{2,1,0:T(8,128)(2,1)S(1)}, bf16[8,128,256]{2,1,0:T(8,128)(2,1)S(1)}, u32[]{:S(2)}, u32[]{:S(2)}) collective-permute-start(bf16[8,128,256]{2,1,0:T(8,128)(2,1)S(1)} %collective-permute-done.3.block1), channel_id=1, source_target_pairs={{0,1},{1,0},{2,3},{3,2},{4,5},{5,4},{6,7},{7,6},{8,9},{9,8},{10,11... | collective-permute-start | bytes 1572872 | tf_op jit(solution)/shard_map/ppermute | solution.py:442
  70.9 3.8 %collective-permute-start.12 = (bf16[12,256,128]{2,1,0:T(8,128)(2,1)S(1)}, bf16[12,256,128]{2,1,0:T(8,128)(2,1)S(1)}, u32[]{:S(2)}, u32[]{:S(2)}) collective-permute-start(bf16[12,256,128]{2,1,0:T(8,128)(2,1)S(1)} %get-tuple-element.21), channel_id=1, source_target_pairs={{0,1},{1,0},{2,3},{3,2},{4,5},{5,4},{6,7},{7,6},{8,9},{9,8},{10,11... | collective-permute-start | bytes 2359304 | tf_op jit(solution)/shard_map/ppermute | solution.py:442
  74.6 0.9 %copy-start.2 = (bf16[12,256,128]{2,1,0:T(8,128)(2,1)}, bf16[12,256,128]{2,1,0:T(8,128)(2,1)S(1)}, u32[]{:S(2)}) copy-start(bf16[12,256,128]{2,1,0:T(8,128)(2,1)S(1)} %collective-permute-done.12.received) | copy-start | bytes 2359300

commit v4 on v3

--- a/solution.py
+++ b/solution.py
@@ -122,7 +122,7 @@
             spots[pl.ds(s, 1), :] = row.astype(I32)
             return 0
 
-        lax.fori_loop(0, each, read, 0)
+        lax.fori_loop(0, each, read, 0, unroll=8)
     copy = pltpu.make_async_copy(
         spots.at[pl.ds(pl.multiple_of(my_grp * blk_count, blk_count), blk_count)], spots_s, sem
     )
@@ -163,7 +163,7 @@
         occupied[pl.ds(r, 1), :] = mm_t(held, rows_at(voxels, key))[0:1]
         return 0
 
-    lax.fori_loop(0, devices, occupy, 0, unroll=8)
+    lax.fori_loop(0, devices, occupy, 0, unroll=16)
 
     for k, block in enumerate(blocks):
 
@@ -175,7 +175,7 @@
                 masked[r, :, at] = block[t, at, :] * there[:, at]
             return 0
 
-        lax.fori_loop(0, each, mask, 0, unroll=4)
+        lax.fori_loop(0, each, mask, 0, unroll=8)
 
     first = iota((LANES, LANES), 1) < plane
 
@@ -188,14 +188,14 @@
             tiles[2 * h + 1, :, cols] = pltpu.roll(jnp.where(first, right, left), plane, 1)
         return 0
 
-    lax.fori_loop(0, blk_count, tile, 0, unroll=4)
+    lax.fori_loop(0, blk_count, tile, 0, unroll=8)
 
     def stand(d, _):
         found = mm_t(stretch[my_grp], masked[my_grp * blk_count + d])
         padded[1 : size_x + 1, pl.ds(d * size_y + 1, size_y)] = found.reshape(size_x, size_y, TALL, LANES)
         return 0
 
-    lax.fori_loop(0, blk_count, stand, 0, unroll=4)
+    lax.fori_loop(0, blk_count, stand, 0, unroll=8)
 
     near = 1 - my_grp
     lines = pl.ds(pl.multiple_of(jnp.where(my_grp == 0, 0, size_x - 1) * size_y * TALL, size_y * TALL), size_y * TALL)
@@ -206,7 +206,7 @@
         padded[at_x, pl.ds(d * size_y + 1, size_y)] = found.reshape(1, size_y, TALL, LANES)
         return 0
 
-    lax.fori_loop(0, blk_count, stand_near, 0, unroll=4)
+    lax.fori_loop(0, blk_count, stand_near, 0, unroll=16)
 
     copy.wait()
     sub = iota((TALL, LANES), 0)
@@ -252,8 +252,7 @@
     shifted0,
     shifted1,
     acc_w,
-    kept,
-    sems,
+    sem,
 ):
     grp_count, blk_count, cap, rows, channels, size_x, size_y, size_z, scale = dims
     voxels = size_x * size_y * size_z
@@ -277,7 +276,7 @@
                 slots[g * blk_count + d, place, :] = held[d * cap : (d + 1) * cap, :]
             return 0
 
-        lax.fori_loop(0, each, fill, 0, unroll=4)
+        lax.fori_loop(0, each, fill, 0, unroll=8)
 
     def place_region(r, _):
         spot = spots[pl.ds(r, 1), :]
@@ -288,7 +287,7 @@
             grid[z, pl.ds(pl.multiple_of(at, plane), plane), :] = found[z * plane : (z + 1) * plane]
         return 0
 
-    lax.fori_loop(0, devices, place_region, 0, unroll=4)
+    lax.fori_loop(0, devices, place_region, 0, unroll=8)
 
     def outer(dx, dy):
         g, d = my_grp + dx, my_blk + dy
@@ -358,7 +357,7 @@
         shift(0, d, shifted0)
         return 0
 
-    lax.fori_loop(0, blk_count, shift_first, 0, unroll=8)
+    lax.fori_loop(0, blk_count, shift_first, 0, unroll=16)
     for z in range(size_z):
         here, there = (shifted0, shifted1) if z % 2 == 0 else (shifted1, shifted0)
         first, count = max(0, 1 - z), min(3, size_z + 1 - z) - max(0, 1 - z)
@@ -383,26 +382,23 @@
         for m in range(5):
             n = m + half * (4 - 2 * m)
             piece = done[:, m * LANES : (m + 1) * LANES]
-            kept[n * 3 + dz1] = piece
-        return 0
-
-    lax.fori_loop(0, 3, finish, 0)
-    mine = pltpu.make_async_copy(kept, weight_grad.at[pl.ds(12 * half, 15)], sems.at[0])
-    theirs = pltpu.make_async_copy(kept.at[pl.ds(3 * half, 12)], sent, sems.at[1])
+            weight_grad[n * 3 + dz1] = piece
+        return 0
+
+    lax.fori_loop(0, 3, finish, 0, unroll=3)
+    theirs = pltpu.make_async_copy(weight_grad.at[pl.ds(3 * half, 12)], sent, sem)
     theirs.start()
-    mine.start()
     theirs.wait()
-    mine.wait()
-
-
-def place_kernel(received, mine, weight_grad, sem):
-    other = 1 - lax.axis_index("blk") % 2
-    copy = pltpu.make_async_copy(received, weight_grad.at[pl.ds(15 * other, 12)], sem)
-    copy.start()
-    copy.wait()
-
-
-def output_kernel(sizes, padded, weight, spots, filled, output, acc_o):
+
+
+def output_kernel(sizes, padded, weight, spots, filled, mine, received, output, weight_grad, acc_o, sems):
+    half = lax.axis_index("blk") % 2
+    copies = (
+        pltpu.make_async_copy(mine, weight_grad.at[pl.ds(12 * half, 15)], sems.at[0]),
+        pltpu.make_async_copy(received, weight_grad.at[pl.ds(15 * (1 - half), 12)], sems.at[1]),
+    )
+    for copy in copies:
+        copy.start()
     size_x, size_y, size_z = sizes
     voxels = size_x * size_y * size_z
     plane = size_x * size_y
@@ -417,7 +413,7 @@
         acc_o[...] += mm(window.astype(BF16), taps)
         return 0
 
-    lax.fori_loop(0, 9, forward, 0, unroll=3)
+    lax.fori_loop(0, 9, forward, 0, unroll=9)
     spot = spots[pl.ds(me, 1), :]
     key = jnp.where(filled[pl.ds(me, 1), :] > 0, spot // size_z * TALL + spot % size_z + 1, -1)
     occupied = mm(one_hot(iota((plane * TALL, voxels), 0) == key), jnp.ones((voxels, LANES), BF16))
@@ -430,6 +426,8 @@
     row, col = iota((voxels, plane * TALL), 0), iota((voxels, plane * TALL), 1)
     squeeze = one_hot(col == row // size_z * TALL + row % size_z + 1)
     output[...] = mm(squeeze, rounded).astype(BF16)
+    for copy in copies:
+        copy.wait()
 
 
 def exchange_masks(count):
@@ -440,6 +438,10 @@
 def swap(value, count, masks):
     pairs = [(i, i ^ masks[i % 2]) for i in range(count)]
     return lax.ppermute(value, ("grp", "blk"), pairs)
+
+
+def after(value, *others):
+    return lax.optimization_barrier((value,) + others)[0]
 
 
 def gather_all(block, count):
@@ -447,6 +449,8 @@
     held = block[None]
     for step in range(len(even) - 1):
         held = jnp.concatenate([held, swap(held, count, (even[step], odd[step]))], axis=0)
+        if step == 0 and block.shape[1] == LANES:
+            held = after(held)
     last = swap(held, count, (even[-1], odd[-1]))
     return held, last, swap(held, count, (1, 1)), swap(last, count, (1, 1))
 
@@ -505,42 +509,38 @@
         functools.partial(scene_kernel, dims + (scale,)),
         out_shape=(
             jax.ShapeDtypeStruct((size_x + 2, size_y + 2, TALL, channels), F32),
-            jax.ShapeDtypeStruct(weight.shape, BF16),
+            jax.ShapeDtypeStruct((15, channels, out_channels), BF16),
             jax.ShapeDtypeStruct((12, channels, out_channels), BF16),
         ),
         in_specs=[vmem] * 7,
-        out_specs=(vmem, hbm, hbm),
+        out_specs=(vmem, vmem, hbm),
         scratch_shapes=[
             pltpu.VMEM((devices, voxels, channels), BF16),
             pltpu.VMEM((size_z, blk_count * LANES, channels), BF16),
             pltpu.VMEM((5 * out_channels, blk_count * LANES), BF16),
             pltpu.VMEM((5 * out_channels, blk_count * LANES), BF16),
             pltpu.VMEM((3, 5 * out_channels, channels), F32),
-            pltpu.VMEM((15, channels, out_channels), BF16),
-            pltpu.SemaphoreType.DMA((2,)),
+            pltpu.SemaphoreType.DMA,
         ],
         compiler_params=pltpu.CompilerParams(vmem_limit_bytes=24 * 1024 * 1024),
         name="scene",
     )(*cells, tiles, slot_rows, spots)
     received = swap(sent, devices, (1, 1))
-    output = pl.pallas_call(
+    output, weight_grad = pl.pallas_call(
         functools.partial(output_kernel, sizes),
-        out_shape=jax.ShapeDtypeStruct((voxels, out_channels), BF16),
-        in_specs=[vmem] * 4,
-        out_specs=vmem,
-        scratch_shapes=[pltpu.VMEM((plane * TALL, 3 * out_channels), F32)],
-        compiler_params=pltpu.CompilerParams(vmem_limit_bytes=8 * 1024 * 1024),
+        out_shape=(
+            jax.ShapeDtypeStruct((voxels, out_channels), BF16),
+            jax.ShapeDtypeStruct(weight.shape, BF16),
+        ),
+        in_specs=[vmem] * 6,
+        out_specs=(vmem, hbm),
+        scratch_shapes=[
+            pltpu.VMEM((plane * TALL, 3 * out_channels), F32),
+            pltpu.SemaphoreType.DMA((2,)),
+        ],
+        compiler_params=pltpu.CompilerParams(vmem_limit_bytes=12 * 1024 * 1024),
         name="output",
-    )(padded, weight, spots, filled)
-    weight_grad = pl.pallas_call(
-        place_kernel,
-        out_shape=jax.ShapeDtypeStruct(weight.shape, BF16),
-        in_specs=[vmem, hbm],
-        out_specs=hbm,
-        scratch_shapes=[pltpu.SemaphoreType.DMA],
-        input_output_aliases={1: 0},
-        name="place",
-    )(received, some)
+    )(padded, weight, spots, filled, some, received)
     return output.reshape(grad_out.shape), grad_rows, weight_grad
 
 

time: 78.5 us -> 72 us (0.917)
  Pallas kernels: 37.4 us -> 31.2 us
  waiting for transfers between devices: 18.6 us -> 20.5 us
  other arithmetic: 4.52 us -> 2.75 us
  local copies, waits for them, and re-layouts: 0.91 us -> 0.02 us
    pallas_call x1, Pallas kernels: 18.4 us -> 15.7 us  [gathered_shards(): pl.pallas_call(functools.partial(scene_kernel, dims + (scale,)), out_shap...]
    ppermute x13, waiting for transfers between devices: 18.6 us -> 20.5 us  [swap(): return lax.ppermute(value, ('grp', 'blk'), pairs)]
    pallas_call x2 -> x1, Pallas kernels: 4.91 us -> 3.11 us  [gathered_shards(): pl.pallas_call(functools.partial(output_kernel, sizes), out_shape=(jax.Sh...]
    concatenate x6, other arithmetic: 4.52 us -> 2.75 us  [gather_all(): jnp.concatenate([held, swap(held, count, (even[step], odd[step]))], axis=0)]
    pallas_call x1, Pallas kernels: 12.2 us -> 10.5 us  [gathered_shards(): pl.pallas_call(functools.partial(cotangent_kernel, dims), out_shape=(jax....]
    unnamed x8 -> x6, local copies, waits for them, and re-layouts: 0.91 us -> 0.02 us
  transfers between devices with their start and end apart: 13 -> 13, of which waited for: 7 -> 8; matrix products, arithmetic and copies ran while one was open for 6% -> 4% of each run, Pallas kernels for 19% -> 15%
where the time goes in v4:
time: 72 us; the launch traced here: 70.7 us
  Pallas kernels  31.2 us (43%)
  waiting for transfers between devices  20.5 us (28%)
  starting transfers between devices  15.3 us (21%)
  other arithmetic  2.75 us (4%)
  between operations  0.9 us (1%)
    ppermute x13, waiting for transfers between devices, swap(): return lax.ppermute(value, ('grp', 'blk'), pairs)  20.5 us
    pallas_call x1, Pallas kernels, gathered_shards(): pl.pallas_call(functools.partial(scene_kernel, dims + (scale,)), out_shap...  15.7 us
    ppermute x13, starting transfers between devices, swap(): return lax.ppermute(value, ('grp', 'blk'), pairs)  15.3 us
    pallas_call x1, Pallas kernels, gathered_shards(): pl.pallas_call(functools.partial(cotangent_kernel, dims), out_shape=(jax....  10.5 us
    pallas_call x1, Pallas kernels, gathered_shards(): pl.pallas_call(functools.partial(output_kernel, sizes), out_shape=(jax.Sh...  3.11 us
    concatenate x6, other arithmetic, gather_all(): jnp.concatenate([held, swap(held, count, (even[step], odd[step]))], axis=0)  2.75 us
    pallas_call x1, Pallas kernels, gathered_shards(): pl.pallas_call(functools.partial(pack_kernel, sizes, cap), out_shape=(jax...  1.91 us
  transfers between devices with their start and end apart: 13, of which 8 were waited for; matrix products, arithmetic and copies ran while one was open for 4% of the time, Pallas kernels for 15%

profile of v4, /device:TPU:0, one launch (start us, length us, event | category | flops | bytes accessed | tf_op | source)
XLA Modules:
  0.0 70.7 jit_solution(17333859928761712069)
XLA Ops:
  0.6 1.9 %pack.1 = (bf16[272,128]{1,0:T(8,128)(2,1)}, s32[1,128]{1,0:T(1,128)}) custom-call(s32[1,128]{1,0:T(1,128)} %bitcast.12, s32[1,256]{1,0:T(1,128)} %placement.1, bf16[256,128]{1,0:T(8,128)(2,1)} %bitcast.11), custom_call_target="tpu_custom_call" | custom-call | tf_op jit(solution)/shard_map/pack/pallas_call | solution.py:470
  2.6 2.9 %collective-permute-start.6 = (bf16[1,272,128]{2,1,0:T(8,128)(2,1)}, bf16[1,272,128]{2,1,0:T(8,128)(2,1)S(1)}, u32[]{:S(2)}, u32[]{:S(2)}) collective-permute-start(bf16[1,272,128]{2,1,0:T(8,128)(2,1)} %bitcast.9), channel_id=1, source_target_pairs={{0,16},{1,9},{2,18},{3,11},{4,20},{5,13},{6,22},{7,15},{8,24},{9,1... | collective-permute-start | bytes 208904 | tf_op jit(solution)/shard_map/ppermute | solution.py:440
  5.5 2.5 %collective-permute-done.6 = bf16[1,272,128]{2,1,0:T(8,128)(2,1)S(1)} collective-permute-done((bf16[1,272,128]{2,1,0:T(8,128)(2,1)}, bf16[1,272,128]{2,1,0:T(8,128)(2,1)S(1)}, u32[]{:S(2)}, u32[]{:S(2)}) %collective-permute-start.6) | collective-permute-done | bytes 69664 | tf_op jit(solution)/shard_map/ppermute | solution.py:440
  8.0 0.9 %pad_maximum_fusion.4 = bf16[2,272,128]{2,1,0:T(8,128)(2,1)S(1)} fusion(bf16[1,272,128]{2,1,0:T(8,128)(2,1)S(1)} %collective-permute-done.6, bf16[1,272,128]{2,1,0:T(8,128)(2,1)} %bitcast.10), kind=kLoop, calls=%fused_computation.4 | loop fusion | flops 69632 | bytes 278528 | tf_op jit(solution)/shard_map/concatenate | solution.py:451
  8.9 3.2 %collective-permute-start.7 = (bf16[2,272,128]{2,1,0:T(8,128)(2,1)S(1)}, bf16[2,272,128]{2,1,0:T(8,128)(2,1)S(1)}, u32[]{:S(2)}, u32[]{:S(2)}) collective-permute-start(bf16[2,272,128]{2,1,0:T(8,128)(2,1)S(1)} %pad_maximum_fusion.4), channel_id=1, source_target_pairs={{0,8},{1,5},{2,10},{3,7},{4,12},{5,1},{6,14},{7,3},{8,0},{9,13},{1... | collective-permute-start | bytes 417800 | tf_op jit(solution)/shard_map/ppermute | solution.py:440
  12.1 0.9 %pad_maximum_fusion.5 = bf16[2,128,256]{2,1,0:T(8,128)(2,1)S(1)} fusion(bf16[1,128,256]{2,1,0:T(8,128)(2,1)S(1)} %collective-permute-done, bf16[1,128,256]{2,1,0:T(8,128)(2,1)} %bitcast.6), kind=kLoop, calls=%fused_computation.5 | loop fusion | flops 65536 | bytes 262144 | tf_op jit(solution)/shard_map/concatenate | solution.py:451
  13.0 0.5 collective-permute-start.1
  13.5 2.6 %collective-permute-done.7 = bf16[2,272,128]{2,1,0:T(8,128)(2,1)S(1)} collective-permute-done((bf16[2,272,128]{2,1,0:T(8,128)(2,1)S(1)}, bf16[2,272,128]{2,1,0:T(8,128)(2,1)S(1)}, u32[]{:S(2)}, u32[]{:S(2)}) %collective-permute-start.7) | collective-permute-done | bytes 139296 | tf_op jit(solution)/shard_map/ppermute | solution.py:440
  16.1 2.5 %collective-permute-start.8 = (bf16[4,272,128]{2,1,0:T(8,128)(2,1)S(1)}, bf16[4,272,128]{2,1,0:T(8,128)(2,1)S(1)}, u32[]{:S(2)}, u32[]{:S(2)}) collective-permute-start(bf16[4,272,128]{2,1,0:T(8,128)(2,1)S(1)} %pad_maximum_fusion.2), channel_id=1, source_target_pairs={{0,4},{1,3},{2,6},{3,1},{4,0},{5,7},{6,2},{7,5},{8,12},{9,11},{10,... | collective-permute-start | bytes 835592 | tf_op jit(solution)/shard_map/ppermute | solution.py:440
  18.6 1.1 %collective-permute-done.1 = bf16[2,128,256]{2,1,0:T(8,128)(2,1)S(1)} collective-permute-done((bf16[2,128,256]{2,1,0:T(8,128)(2,1)S(1)}, bf16[2,128,256]{2,1,0:T(8,128)(2,1)S(1)}, u32[]{:S(2)}, u32[]{:S(2)}) %collective-permute-start.1) | collective-permute-done | bytes 131104 | tf_op jit(solution)/shard_map/ppermute | solution.py:440
  19.7 0.9 %pad_maximum_fusion.3 = bf16[4,128,256]{2,1,0:T(8,128)(2,1)S(1)} fusion(bf16[2,128,256]{2,1,0:T(8,128)(2,1)S(1)} %collective-permute-done.1, bf16[1,128,256]{2,1,0:T(8,128)(2,1)S(1)} %collective-permute-done, bf16[1,128,256]{2,1,0:T(8,128)(2,1)} %bitcast.7), kind=kLoop, calls=%fused_computation.3 | loop fusion | flops 262144 | bytes 524288 | tf_op jit(solution)/shard_map/concatenate | solution.py:451
  20.6 1.6 %collective-permute-start.2 = (bf16[4,128,256]{2,1,0:T(8,128)(2,1)S(1)}, bf16[4,128,256]{2,1,0:T(8,128)(2,1)S(1)}, u32[]{:S(2)}, u32[]{:S(2)}) collective-permute-start(bf16[4,128,256]{2,1,0:T(8,128)(2,1)S(1)} %pad_maximum_fusion.3), channel_id=1, source_target_pairs={{0,4},{1,3},{2,6},{3,1},{4,0},{5,7},{6,2},{7,5},{8,12},{9,11},{10,... | collective-permute-start | bytes 786440 | tf_op jit(solution)/shard_map/ppermute | solution.py:440
  22.2 1.0 %collective-permute-done.8 = bf16[4,272,128]{2,1,0:T(8,128)(2,1)S(1)} collective-permute-done((bf16[4,272,128]{2,1,0:T(8,128)(2,1)S(1)}, bf16[4,272,128]{2,1,0:T(8,128)(2,1)S(1)}, u32[]{:S(2)}, u32[]{:S(2)}) %collective-permute-start.8) | collective-permute-done | bytes 278560 | tf_op jit(solution)/shard_map/ppermute | solution.py:440
  23.2 1.6 %collective-permute-start.9 = (bf16[8,272,128]{2,1,0:T(8,128)(2,1)S(1)}, bf16[8,272,128]{2,1,0:T(8,128)(2,1)S(1)}, u32[]{:S(2)}, u32[]{:S(2)}) collective-permute-start(bf16[8,272,128]{2,1,0:T(8,128)(2,1)S(1)} %pad_maximum_fusion.block0), channel_id=1, source_target_pairs={{0,2},{1,17},{2,0},{3,19},{4,6},{5,21},{6,4},{7,23},{8,10},{9,25},... | collective-permute-start | bytes 1671176 | tf_op jit(solution)/shard_map/ppermute | solution.py:440
  24.8 2.2 %collective-permute-done.2 = bf16[4,128,256]{2,1,0:T(8,128)(2,1)S(1)} collective-permute-done((bf16[4,128,256]{2,1,0:T(8,128)(2,1)S(1)}, bf16[4,128,256]{2,1,0:T(8,128)(2,1)S(1)}, u32[]{:S(2)}, u32[]{:S(2)}) %collective-permute-start.2) | collective-permute-done | bytes 262176 | tf_op jit(solution)/shard_map/ppermute | solution.py:440
  27.1 1.6 %collective-permute-start.3 = (bf16[8,128,256]{2,1,0:T(8,128)(2,1)S(1)}, bf16[8,128,256]{2,1,0:T(8,128)(2,1)S(1)}, u32[]{:S(2)}, u32[]{:S(2)}) collective-permute-start(bf16[8,128,256]{2,1,0:T(8,128)(2,1)S(1)} %pad_maximum_fusion.1.block0), channel_id=1, source_target_pairs={{0,2},{1,17},{2,0},{3,19},{4,6},{5,21},{6,4},{7,23},{8,10},{9,25},... | collective-permute-start | bytes 1572872 | tf_op jit(solution)/shard_map/ppermute | solution.py:440
  28.7 4.2 %collective-permute-done.9.block1 = bf16[8,272,128]{2,1,0:T(8,128)(2,1)S(1)} collective-permute-done((bf16[8,272,128]{2,1,0:T(8,128)(2,1)S(1)}, bf16[8,272,128]{2,1,0:T(8,128)(2,1)S(1)}, u32[]{:S(2)}, u32[]{:S(2)}) %collective-permute-start.9) | collective-permute-done | bytes 557088 | tf_op jit(solution)/shard_map/ppermute | solution.py:440
  32.8 0.5 collective-permute-start.4
  33.3 5.1 %collective-permute-done.3.block1 = bf16[8,128,256]{2,1,0:T(8,128)(2,1)S(1)} collective-permute-done((bf16[8,128,256]{2,1,0:T(8,128)(2,1)S(1)}, bf16[8,128,256]{2,1,0:T(8,128)(2,1)S(1)}, u32[]{:S(2)}, u32[]{:S(2)}) %collective-permute-start.3) | collective-permute-done | bytes 524320 | tf_op jit(solution)/shard_map/ppermute | solution.py:440
  38.5 10.5 %cotangent.1 = (bf16[128,256]{1,0:T(8,128)(2,1)}, bf16[4,128,2304]{2,1,0:T(8,128)(2,1)S(1)}, s32[32,128]{1,0:T(8,128)S(1)}, s32[32,256]{1,0:T(8,128)S(1)}, f32[32,256]{1,0:T(8,128)S(1)}) custom-call(s32[1,128]{1,0:T(1,128)S(1)} %copy-done.1, bf16[8,272,128]{2,1,0:T(8,128)(2,1)S(1)} %pad_maximum_fusion.block0, ...), custom_call_target="tpu_custom_call" | custom-call | tf_op jit(solution)/shard_map/cotangent/pallas_call | solution.py:483
  49.0 15.7 %scene.1 = (f32[10,10,8,256]{3,2,1,0:T(8,128)S(1)}, bf16[15,256,128]{2,1,0:T(8,128)(2,1)S(1)}, bf16[12,256,128]{2,1,0:T(8,128)(2,1)S(1)}) custom-call(bf16[8,128,256]{2,1,0:T(8,128)(2,1)S(1)} %pad_maximum_fusion.1.block0, bf16[8,128,256]{2,1,0:T(8,128)(2,1)S(1)} %collective-permute-done.3.block1, bf16[8,128,256]{2,1,0:T(8,128)(2,1)S(1)} %collective-permute-done.4.block2, ...), custom_call_target="tpu_custom_call" | custom-call | tf_op jit(solution)/shard_map/scene/pallas_call | solution.py:508
  64.7 0.9 %collective-permute-start.12 = (bf16[12,256,128]{2,1,0:T(8,128)(2,1)S(1)}, bf16[12,256,128]{2,1,0:T(8,128)(2,1)S(1)}, u32[]{:S(2)}, u32[]{:S(2)}) collective-permute-start(bf16[12,256,128]{2,1,0:T(8,128)(2,1)S(1)} %get-tuple-element.23), channel_id=1, source_target_pairs={{0,1},{1,0},{2,3},{3,2},{4,5},{5,4},{6,7},{7,6},{8,9},{9,8},{10,11... | collective-permute-start | bytes 2359304 | tf_op jit(solution)/shard_map/ppermute | solution.py:440
  65.5 1.9 %collective-permute-done.12.received = bf16[12,256,128]{2,1,0:T(8,128)(2,1)S(1)} collective-permute-done((bf16[12,256,128]{2,1,0:T(8,128)(2,1)S(1)}, bf16[12,256,128]{2,1,0:T(8,128)(2,1)S(1)}, u32[]{:S(2)}, u32[]{:S(2)}) %collective-permute-start.12) | collective-permute-done | bytes 786464 | tf_op jit(solution)/shard_map/ppermute | solution.py:440
  67.5 3.1 %output.1 = (bf16[256,128]{1,0:T(8,128)(2,1)}, bf16[27,256,128]{2,1,0:T(8,128)(2,1)}) custom-call(f32[10,10,8,256]{3,2,1,0:T(8,128)S(1)} %get-tuple-element.20.padded, bf16[27,256,128]{2,1,0:T(8,128)(2,1)S(1)} %copy-done, s32[32,256]{1,0:T(8,128)S(1)} %get-tuple-element.19.spots, f32[32,256]{1,0:T(8,128)S(1)} %get-tuple-element.21.filled, ...), custom_call_target="tpu_custom_call" | custom-call | tf_op jit(solution)/shard_map/output/pallas_call | solution.py:529
  (18 shorter events, 0.2 us)
Async XLA Ops:
  0.6 26.4 %copy-start.2 = (bf16[128,256]{1,0:T(8,128)(2,1)S(1)}, bf16[128,256]{1,0:T(8,128)(2,1)}, u32[]{:S(2)}) copy-start(bf16[128,256]{1,0:T(8,128)(2,1)} %param.5) | copy-start | bytes 196612
  2.6 5.4 %collective-permute-start.6 = (bf16[1,272,128]{2,1,0:T(8,128)(2,1)}, bf16[1,272,128]{2,1,0:T(8,128)(2,1)S(1)}, u32[]{:S(2)}, u32[]{:S(2)}) collective-permute-start(bf16[1,272,128]{2,1,0:T(8,128)(2,1)} %bitcast.9), channel_id=1, source_target_pairs={{0,16},{1,9},{2,18},{3,11},{4,20},{5,13},{6,22},{7,15},{8,24},{9,1... | collective-permute-start | bytes 208904 | tf_op jit(solution)/shard_map/ppermute | solution.py:440
  5.5 6.6 %collective-permute-start = (bf16[1,128,256]{2,1,0:T(8,128)(2,1)}, bf16[1,128,256]{2,1,0:T(8,128)(2,1)S(1)}, u32[]{:S(2)}, u32[]{:S(2)}) collective-permute-start(bf16[1,128,256]{2,1,0:T(8,128)(2,1)} %bitcast.5), channel_id=1, source_target_pairs={{0,16},{1,9},{2,18},{3,11},{4,20},{5,13},{6,22},{7,15},{8,24},{9,1... | collective-permute-start | bytes 196616 | tf_op jit(solution)/shard_map/ppermute | solution.py:440
  8.9 29.6 %copy-start = (bf16[27,256,128]{2,1,0:T(8,128)(2,1)S(1)}, bf16[27,256,128]{2,1,0:T(8,128)(2,1)}, u32[]{:S(2)}) copy-start(bf16[27,256,128]{2,1,0:T(8,128)(2,1)} %weight.3) | copy-start | bytes 5308420
  8.9 29.6 %copy-start.1 = (s32[1,128]{1,0:T(1,128)S(1)}, s32[1,128]{1,0:T(1,128)}, u32[]{:S(2)}) copy-start(s32[1,128]{1,0:T(1,128)} %get-tuple-element.15.slot_ref) | copy-start | bytes 1540
  8.9 7.2 %collective-permute-start.7 = (bf16[2,272,128]{2,1,0:T(8,128)(2,1)S(1)}, bf16[2,272,128]{2,1,0:T(8,128)(2,1)S(1)}, u32[]{:S(2)}, u32[]{:S(2)}) collective-permute-start(bf16[2,272,128]{2,1,0:T(8,128)(2,1)S(1)} %pad_maximum_fusion.4), channel_id=1, source_target_pairs={{0,8},{1,5},{2,10},{3,7},{4,12},{5,1},{6,14},{7,3},{8,0},{9,13},{1... | collective-permute-start | bytes 417800 | tf_op jit(solution)/shard_map/ppermute | solution.py:440
  13.0 6.7 %collective-permute-start.1 = (bf16[2,128,256]{2,1,0:T(8,128)(2,1)S(1)}, bf16[2,128,256]{2,1,0:T(8,128)(2,1)S(1)}, u32[]{:S(2)}, u32[]{:S(2)}) collective-permute-start(bf16[2,128,256]{2,1,0:T(8,128)(2,1)S(1)} %pad_maximum_fusion.5), channel_id=1, source_target_pairs={{0,8},{1,5},{2,10},{3,7},{4,12},{5,1},{6,14},{7,3},{8,0},{9,13},{1... | collective-permute-start | bytes 393224 | tf_op jit(solution)/shard_map/ppermute | solution.py:440
  16.1 7.0 %collective-permute-start.8 = (bf16[4,272,128]{2,1,0:T(8,128)(2,1)S(1)}, bf16[4,272,128]{2,1,0:T(8,128)(2,1)S(1)}, u32[]{:S(2)}, u32[]{:S(2)}) collective-permute-start(bf16[4,272,128]{2,1,0:T(8,128)(2,1)S(1)} %pad_maximum_fusion.2), channel_id=1, source_target_pairs={{0,4},{1,3},{2,6},{3,1},{4,0},{5,7},{6,2},{7,5},{8,12},{9,11},{10,... | collective-permute-start | bytes 835592 | tf_op jit(solution)/shard_map/ppermute | solution.py:440
  20.6 6.4 %collective-permute-start.2 = (bf16[4,128,256]{2,1,0:T(8,128)(2,1)S(1)}, bf16[4,128,256]{2,1,0:T(8,128)(2,1)S(1)}, u32[]{:S(2)}, u32[]{:S(2)}) collective-permute-start(bf16[4,128,256]{2,1,0:T(8,128)(2,1)S(1)} %pad_maximum_fusion.3), channel_id=1, source_target_pairs={{0,4},{1,3},{2,6},{3,1},{4,0},{5,7},{6,2},{7,5},{8,12},{9,11},{10,... | collective-permute-start | bytes 786440 | tf_op jit(solution)/shard_map/ppermute | solution.py:440
  23.2 9.6 %collective-permute-start.9 = (bf16[8,272,128]{2,1,0:T(8,128)(2,1)S(1)}, bf16[8,272,128]{2,1,0:T(8,128)(2,1)S(1)}, u32[]{:S(2)}, u32[]{:S(2)}) collective-permute-start(bf16[8,272,128]{2,1,0:T(8,128)(2,1)S(1)} %pad_maximum_fusion.block0), channel_id=1, source_target_pairs={{0,2},{1,17},{2,0},{3,19},{4,6},{5,21},{6,4},{7,23},{8,10},{9,25},... | collective-permute-start | bytes 1671176 | tf_op jit(solution)/shard_map/ppermute | solution.py:440
  27.1 11.4 %collective-permute-start.3 = (bf16[8,128,256]{2,1,0:T(8,128)(2,1)S(1)}, bf16[8,128,256]{2,1,0:T(8,128)(2,1)S(1)}, u32[]{:S(2)}, u32[]{:S(2)}) collective-permute-start(bf16[8,128,256]{2,1,0:T(8,128)(2,1)S(1)} %pad_maximum_fusion.1.block0), channel_id=1, source_target_pairs={{0,2},{1,17},{2,0},{3,19},{4,6},{5,21},{6,4},{7,23},{8,10},{9,25},... | collective-permute-start | bytes 1572872 | tf_op jit(solution)/shard_map/ppermute | solution.py:440
  28.7 9.8 %collective-permute-start.10 = (bf16[8,272,128]{2,1,0:T(8,128)(2,1)S(1)}, bf16[8,272,128]{2,1,0:T(8,128)(2,1)S(1)}, u32[]{:S(2)}, u32[]{:S(2)}) collective-permute-start(bf16[8,272,128]{2,1,0:T(8,128)(2,1)S(1)} %pad_maximum_fusion.block0), channel_id=1, source_target_pairs={{0,1},{1,0},{2,3},{3,2},{4,5},{5,4},{6,7},{7,6},{8,9},{9,8},{10,11... | collective-permute-start | bytes 1671176 | tf_op jit(solution)/shard_map/ppermute | solution.py:440
  32.8 5.6 %collective-permute-start.11 = (bf16[8,272,128]{2,1,0:T(8,128)(2,1)S(1)}, bf16[8,272,128]{2,1,0:T(8,128)(2,1)S(1)}, u32[]{:S(2)}, u32[]{:S(2)}) collective-permute-start(bf16[8,272,128]{2,1,0:T(8,128)(2,1)S(1)} %collective-permute-done.9.block1), channel_id=1, source_target_pairs={{0,1},{1,0},{2,3},{3,2},{4,5},{5,4},{6,7},{7,6},{8,9},{9,8},{10,11... | collective-permute-start | bytes 1671176 | tf_op jit(solution)/shard_map/ppermute | solution.py:440
  32.8 16.1 %collective-permute-start.4 = (bf16[8,128,256]{2,1,0:T(8,128)(2,1)S(1)}, bf16[8,128,256]{2,1,0:T(8,128)(2,1)S(1)}, u32[]{:S(2)}, u32[]{:S(2)}) collective-permute-start(bf16[8,128,256]{2,1,0:T(8,128)(2,1)S(1)} %pad_maximum_fusion.1.block0), channel_id=1, source_target_pairs={{0,1},{1,0},{2,3},{3,2},{4,5},{5,4},{6,7},{7,6},{8,9},{9,8},{10,11... | collective-permute-start | bytes 1572872 | tf_op jit(solution)/shard_map/ppermute | solution.py:440
  38.4 10.5 %collective-permute-start.5 = (bf16[8,128,256]{2,1,0:T(8,128)(2,1)S(1)}, bf16[8,128,256]{2,1,0:T(8,128)(2,1)S(1)}, u32[]{:S(2)}, u32[]{:S(2)}) collective-permute-start(bf16[8,128,256]{2,1,0:T(8,128)(2,1)S(1)} %collective-permute-done.3.block1), channel_id=1, source_target_pairs={{0,1},{1,0},{2,3},{3,2},{4,5},{5,4},{6,7},{7,6},{8,9},{9,8},{10,11... | collective-permute-start | bytes 1572872 | tf_op jit(solution)/shard_map/ppermute | solution.py:440
  64.7 2.8 %collective-permute-start.12 = (bf16[12,256,128]{2,1,0:T(8,128)(2,1)S(1)}, bf16[12,256,128]{2,1,0:T(8,128)(2,1)S(1)}, u32[]{:S(2)}, u32[]{:S(2)}) collective-permute-start(bf16[12,256,128]{2,1,0:T(8,128)(2,1)S(1)} %get-tuple-element.23), channel_id=1, source_target_pairs={{0,1},{1,0},{2,3},{3,2},{4,5},{5,4},{6,7},{7,6},{8,9},{9,8},{10,11... | collective-permute-start | bytes 2359304 | tf_op jit(solution)/shard_map/ppermute | solution.py:440

commit v5 on v4

--- a/solution.py
+++ b/solution.py
@@ -98,18 +98,47 @@
     counts,
     occupied,
     masked,
+    fetched,
     spots_s,
     sem,
+    fetch_sems,
 ):
     grp_count, blk_count, cap, rows, channels, size_x, size_y, size_z = dims
     voxels = size_x * size_y * size_z
     devices = grp_count * blk_count
     plane = size_x * size_y
     halves = voxels // LANES
-    blocks = (block0, block1, block2, block3)
+    far = (block1, block2, block3)
+    fetches = [pltpu.make_async_copy(far[k], fetched.at[k], fetch_sems.at[k]) for k in range(3)]
+    for fetch in fetches:
+        fetch.start()
+    blocks = (block0, fetched.at[0], fetched.at[1], fetched.at[2])
     each = devices // 4
     my_grp, my_blk = lax.axis_index("grp"), lax.axis_index("blk")
     me = my_grp * blk_count + my_blk
+
+    for g in range(grp_count):
+        row, col = iota((plane * TALL, voxels), 0), iota((plane * TALL, voxels), 1)
+        z = row % TALL - 1
+        inside = (z >= 0) & (z < size_z)
+        stretch[g] = one_hot(inside & (col == half_order(z, row // TALL, g, plane)))
+
+    zero_plane = jnp.zeros((1,) + padded.shape[1:], F32)
+    zero_line = jnp.zeros((padded.shape[0], 1) + padded.shape[2:], F32)
+
+    @pl.when(my_grp == 0)
+    def _():
+        padded[0:1] = zero_plane
+
+    @pl.when(my_grp == grp_count - 1)
+    def _():
+        padded[size_x + 1 : size_x + 2] = zero_plane
+
+    padded[:, 0:1] = zero_line
+    padded[:, padded.shape[1] - 1 :] = zero_line
+    for z in range(size_z):
+        tiles[z, :, 0:LANES] = jnp.zeros((LANES, LANES), BF16)
+        tiles[z, :, (blk_count + 1) * LANES :] = jnp.zeros((LANES, LANES), BF16)
 
     for k, block in enumerate(blocks):
 
@@ -122,6 +151,8 @@
             spots[pl.ds(s, 1), :] = row.astype(I32)
             return 0
 
+        if k:
+            fetches[k - 1].wait()
         lax.fori_loop(0, each, read, 0, unroll=8)
     copy = pltpu.make_async_copy(
         spots.at[pl.ds(pl.multiple_of(my_grp * blk_count, blk_count), blk_count)], spots_s, sem
@@ -134,27 +165,6 @@
         sent = counts[g * blk_count : (g + 1) * blk_count, :].T[:blk_count].astype(BF16)
         held = jnp.where(rank < mm(sent, spread), 1.0, 0.0)
         filled[g * blk_count : (g + 1) * blk_count, :] = held
-        row, col = iota((plane * TALL, voxels), 0), iota((plane * TALL, voxels), 1)
-        z = row % TALL - 1
-        inside = (z >= 0) & (z < size_z)
-        stretch[g] = one_hot(inside & (col == half_order(z, row // TALL, g, plane)))
-
-    zero_plane = jnp.zeros((1,) + padded.shape[1:], F32)
-    zero_line = jnp.zeros((padded.shape[0], 1) + padded.shape[2:], F32)
-
-    @pl.when(my_grp == 0)
-    def _():
-        padded[0:1] = zero_plane
-
-    @pl.when(my_grp == grp_count - 1)
-    def _():
-        padded[size_x + 1 : size_x + 2] = zero_plane
-
-    padded[:, 0:1] = zero_line
-    padded[:, padded.shape[1] - 1 :] = zero_line
-    for z in range(size_z):
-        tiles[z, :, 0:LANES] = jnp.zeros((LANES, LANES), BF16)
-        tiles[z, :, (blk_count + 1) * LANES :] = jnp.zeros((LANES, LANES), BF16)
 
     def occupy(r, _):
         spot = spots[pl.ds(r, 1), :]
@@ -163,7 +173,7 @@
         occupied[pl.ds(r, 1), :] = mm_t(held, rows_at(voxels, key))[0:1]
         return 0
 
-    lax.fori_loop(0, devices, occupy, 0, unroll=16)
+    lax.fori_loop(0, devices, occupy, 0, unroll=32)
 
     for k, block in enumerate(blocks):
 
@@ -225,7 +235,7 @@
             gathered[n, pl.ds(pl.multiple_of(group * TALL, TALL), TALL), :] = found[n]
         return 0
 
-    lax.fori_loop(0, rows // TALL, gather, 0)
+    lax.fori_loop(0, rows // TALL, gather, 0, unroll=2)
 
     def backward(n, total):
         windows = jnp.concatenate([gathered[n * 3 + i] for i in range(3)], axis=1).astype(BF16)
@@ -252,13 +262,19 @@
     shifted0,
     shifted1,
     acc_w,
+    fetched,
     sem,
+    fetch_sems,
 ):
     grp_count, blk_count, cap, rows, channels, size_x, size_y, size_z, scale = dims
     voxels = size_x * size_y * size_z
     devices = grp_count * blk_count
     plane = size_x * size_y
-    blocks = (block0, block1, block2, block3)
+    far = (block1, block2, block3)
+    fetches = [pltpu.make_async_copy(far[k], fetched.at[k], fetch_sems.at[k]) for k in range(3)]
+    for fetch in fetches:
+        fetch.start()
+    blocks = (block0, fetched.at[0], fetched.at[1], fetched.at[2])
     each = devices // 4
     my_grp, my_blk = lax.axis_index("grp"), lax.axis_index("blk")
     me = my_grp * blk_count + my_blk
@@ -276,6 +292,8 @@
                 slots[g * blk_count + d, place, :] = held[d * cap : (d + 1) * cap, :]
             return 0
 
+        if k:
+            fetches[k - 1].wait()
         lax.fori_loop(0, each, fill, 0, unroll=8)
 
     def place_region(r, _):
@@ -287,7 +305,7 @@
             grid[z, pl.ds(pl.multiple_of(at, plane), plane), :] = found[z * plane : (z + 1) * plane]
         return 0
 
-    lax.fori_loop(0, devices, place_region, 0, unroll=8)
+    lax.fori_loop(0, devices, place_region, 0, unroll=16)
 
     def outer(dx, dy):
         g, d = my_grp + dx, my_blk + dy
@@ -297,22 +315,16 @@
         at_y = {-1: 0, 0: 1, 1: size_y + 1}[dy]
         there = (slice(at_x, at_x + shape[0]), slice(at_y, at_y + shape[1]))
 
-        @pl.when(inside)
-        def _():
-            r = g * blk_count + d
-            spot = spots[pl.ds(r, 1), :]
-            key = spot // size_z * TALL + spot % size_z + 1
-            t = iota((shape[0] * shape[1] * TALL, voxels), 0)
-            x0, y0 = (size_x - 1 if dx < 0 else 0), (size_y - 1 if dy < 0 else 0)
-            if dy and not dx:
-                want = t // TALL * (size_y * TALL) + y0 * TALL + t % TALL
-            else:
-                want = t + (x0 * size_y + y0) * TALL
-            padded[there] = mm(one_hot(want == key), slots[r]).reshape(shape)
-
-        @pl.when(jnp.logical_not(inside))
-        def _():
-            padded[there] = jnp.zeros(shape, F32)
+        r = jnp.where(inside, g * blk_count + d, me)
+        spot = spots[pl.ds(r, 1), :]
+        key = jnp.where(inside, spot // size_z * TALL + spot % size_z + 1, -1)
+        t = iota((shape[0] * shape[1] * TALL, voxels), 0)
+        x0, y0 = (size_x - 1 if dx < 0 else 0), (size_y - 1 if dy < 0 else 0)
+        if dy and not dx:
+            want = t // TALL * (size_y * TALL) + y0 * TALL + t % TALL
+        else:
+            want = t + (x0 * size_y + y0) * TALL
+        padded[there] = mm(one_hot(want == key), slots[r]).reshape(shape)
 
     for dx in (-1, 0, 1):
         for dy in (-1, 0, 1):
@@ -489,7 +501,7 @@
             jax.ShapeDtypeStruct((devices, voxels), I32),
             jax.ShapeDtypeStruct((devices, voxels), F32),
         ),
-        in_specs=[smem] + [vmem] * 5,
+        in_specs=[smem, vmem] + [hbm] * 3 + [vmem],
         out_specs=(vmem,) * 5,
         scratch_shapes=[
             pltpu.VMEM((size_x + 2, blk_count * size_y + 2, TALL, out_channels), F32),
@@ -498,8 +510,10 @@
             pltpu.VMEM((devices, LANES), F32),
             pltpu.VMEM((devices, voxels), F32),
             pltpu.VMEM((devices, out_channels, voxels), BF16),
+            pltpu.VMEM((3,) + cotangents[0].shape, BF16),
             pltpu.SMEM((blk_count, voxels), I32),
             pltpu.SemaphoreType.DMA,
+            pltpu.SemaphoreType.DMA((3,)),
         ],
         compiler_params=pltpu.CompilerParams(vmem_limit_bytes=24 * 1024 * 1024),
         name="cotangent",
@@ -512,7 +526,7 @@
             jax.ShapeDtypeStruct((15, channels, out_channels), BF16),
             jax.ShapeDtypeStruct((12, channels, out_channels), BF16),
         ),
-        in_specs=[vmem] * 7,
+        in_specs=[vmem] + [hbm] * 3 + [vmem] * 3,
         out_specs=(vmem, vmem, hbm),
         scratch_shapes=[
             pltpu.VMEM((devices, voxels, channels), BF16),
@@ -520,7 +534,9 @@
             pltpu.VMEM((5 * out_channels, blk_count * LANES), BF16),
             pltpu.VMEM((5 * out_channels, blk_count * LANES), BF16),
             pltpu.VMEM((3, 5 * out_channels, channels), F32),
+            pltpu.VMEM((3,) + cells[0].shape, BF16),
             pltpu.SemaphoreType.DMA,
+            pltpu.SemaphoreType.DMA((3,)),
         ],
         compiler_params=pltpu.CompilerParams(vmem_limit_bytes=24 * 1024 * 1024),
         name="scene",

time: 72 us -> 71.4 us (level)
  no operation moved by 1% of the time
where the time goes in v5:
time: 71.4 us; the launch traced here: 70.2 us
  Pallas kernels  31 us (43%)
  waiting for transfers between devices  20.5 us (29%)
  starting transfers between devices  15 us (21%)
  other arithmetic  2.75 us (4%)
  between operations  0.9 us (1%)
    ppermute x13, waiting for transfers between devices, swap(): return lax.ppermute(value, ('grp', 'blk'), pairs)  20.5 us
    pallas_call x1, Pallas kernels, gathered_shards(): pl.pallas_call(functools.partial(scene_kernel, dims + (scale,)), out_shap...  15.3 us
    ppermute x13, starting transfers between devices, swap(): return lax.ppermute(value, ('grp', 'blk'), pairs)  15 us
    pallas_call x1, Pallas kernels, gathered_shards(): pl.pallas_call(functools.partial(cotangent_kernel, dims), out_shape=(jax....  10.6 us
    pallas_call x1, Pallas kernels, gathered_shards(): pl.pallas_call(functools.partial(output_kernel, sizes), out_shape=(jax.Sh...  3.12 us
    concatenate x6, other arithmetic, gather_all(): jnp.concatenate([held, swap(held, count, (even[step], odd[step]))], axis=0)  2.75 us
    pallas_call x1, Pallas kernels, gathered_shards(): pl.pallas_call(functools.partial(pack_kernel, sizes, cap), out_shape=(jax...  1.91 us
  transfers between devices with their start and end apart: 13, of which 8 were waited for; matrix products, arithmetic and copies ran while one was open for 4% of the time, Pallas kernels for 15%

profile of v5, /device:TPU:0, one launch (start us, length us, event | category | flops | bytes accessed | tf_op | source)
XLA Modules:
  0.0 70.2 jit_solution(11217912528602524360)
XLA Ops:
  0.6 1.9 %pack.1 = (bf16[272,128]{1,0:T(8,128)(2,1)}, s32[1,128]{1,0:T(1,128)}) custom-call(s32[1,128]{1,0:T(1,128)} %bitcast.12, s32[1,256]{1,0:T(1,128)} %placement.1, bf16[256,128]{1,0:T(8,128)(2,1)} %bitcast.11), custom_call_target="tpu_custom_call" | custom-call | tf_op jit(solution)/shard_map/pack/pallas_call | solution.py:482
  2.6 2.9 %collective-permute-start.6 = (bf16[1,272,128]{2,1,0:T(8,128)(2,1)}, bf16[1,272,128]{2,1,0:T(8,128)(2,1)S(1)}, u32[]{:S(2)}, u32[]{:S(2)}) collective-permute-start(bf16[1,272,128]{2,1,0:T(8,128)(2,1)} %bitcast.9), channel_id=1, source_target_pairs={{0,16},{1,9},{2,18},{3,11},{4,20},{5,13},{6,22},{7,15},{8,24},{9,1... | collective-permute-start | bytes 208904 | tf_op jit(solution)/shard_map/ppermute | solution.py:452
  5.5 2.5 %collective-permute-done.6 = bf16[1,272,128]{2,1,0:T(8,128)(2,1)S(1)} collective-permute-done((bf16[1,272,128]{2,1,0:T(8,128)(2,1)}, bf16[1,272,128]{2,1,0:T(8,128)(2,1)S(1)}, u32[]{:S(2)}, u32[]{:S(2)}) %collective-permute-start.6) | collective-permute-done | bytes 69664 | tf_op jit(solution)/shard_map/ppermute | solution.py:452
  8.0 0.9 %pad_maximum_fusion.4 = bf16[2,272,128]{2,1,0:T(8,128)(2,1)S(1)} fusion(bf16[1,272,128]{2,1,0:T(8,128)(2,1)S(1)} %collective-permute-done.6, bf16[1,272,128]{2,1,0:T(8,128)(2,1)} %bitcast.10), kind=kLoop, calls=%fused_computation.4 | loop fusion | flops 69632 | bytes 278528 | tf_op jit(solution)/shard_map/concatenate | solution.py:463
  8.9 3.2 %collective-permute-start.7 = (bf16[2,272,128]{2,1,0:T(8,128)(2,1)S(1)}, bf16[2,272,128]{2,1,0:T(8,128)(2,1)S(1)}, u32[]{:S(2)}, u32[]{:S(2)}) collective-permute-start(bf16[2,272,128]{2,1,0:T(8,128)(2,1)S(1)} %pad_maximum_fusion.4), channel_id=1, source_target_pairs={{0,8},{1,5},{2,10},{3,7},{4,12},{5,1},{6,14},{7,3},{8,0},{9,13},{1... | collective-permute-start | bytes 417800 | tf_op jit(solution)/shard_map/ppermute | solution.py:452
  12.1 0.9 %pad_maximum_fusion.5 = bf16[2,128,256]{2,1,0:T(8,128)(2,1)S(1)} fusion(bf16[1,128,256]{2,1,0:T(8,128)(2,1)S(1)} %collective-permute-done, bf16[1,128,256]{2,1,0:T(8,128)(2,1)} %bitcast.6), kind=kLoop, calls=%fused_computation.5 | loop fusion | flops 65536 | bytes 262144 | tf_op jit(solution)/shard_map/concatenate | solution.py:463
  13.0 0.5 collective-permute-start.1
  13.5 2.6 %collective-permute-done.7 = bf16[2,272,128]{2,1,0:T(8,128)(2,1)S(1)} collective-permute-done((bf16[2,272,128]{2,1,0:T(8,128)(2,1)S(1)}, bf16[2,272,128]{2,1,0:T(8,128)(2,1)S(1)}, u32[]{:S(2)}, u32[]{:S(2)}) %collective-permute-start.7) | collective-permute-done | bytes 139296 | tf_op jit(solution)/shard_map/ppermute | solution.py:452
  16.1 2.5 %collective-permute-start.8 = (bf16[4,272,128]{2,1,0:T(8,128)(2,1)S(1)}, bf16[4,272,128]{2,1,0:T(8,128)(2,1)S(1)}, u32[]{:S(2)}, u32[]{:S(2)}) collective-permute-start(bf16[4,272,128]{2,1,0:T(8,128)(2,1)S(1)} %pad_maximum_fusion.2), channel_id=1, source_target_pairs={{0,4},{1,3},{2,6},{3,1},{4,0},{5,7},{6,2},{7,5},{8,12},{9,11},{10,... | collective-permute-start | bytes 835592 | tf_op jit(solution)/shard_map/ppermute | solution.py:452
  18.6 1.1 %collective-permute-done.1 = bf16[2,128,256]{2,1,0:T(8,128)(2,1)S(1)} collective-permute-done((bf16[2,128,256]{2,1,0:T(8,128)(2,1)S(1)}, bf16[2,128,256]{2,1,0:T(8,128)(2,1)S(1)}, u32[]{:S(2)}, u32[]{:S(2)}) %collective-permute-start.1) | collective-permute-done | bytes 131104 | tf_op jit(solution)/shard_map/ppermute | solution.py:452
  19.7 0.9 %pad_maximum_fusion.3 = bf16[4,128,256]{2,1,0:T(8,128)(2,1)S(1)} fusion(bf16[2,128,256]{2,1,0:T(8,128)(2,1)S(1)} %collective-permute-done.1, bf16[1,128,256]{2,1,0:T(8,128)(2,1)S(1)} %collective-permute-done, bf16[1,128,256]{2,1,0:T(8,128)(2,1)} %bitcast.7), kind=kLoop, calls=%fused_computation.3 | loop fusion | flops 262144 | bytes 524288 | tf_op jit(solution)/shard_map/concatenate | solution.py:463
  20.6 1.6 %collective-permute-start.2 = (bf16[4,128,256]{2,1,0:T(8,128)(2,1)S(1)}, bf16[4,128,256]{2,1,0:T(8,128)(2,1)S(1)}, u32[]{:S(2)}, u32[]{:S(2)}) collective-permute-start(bf16[4,128,256]{2,1,0:T(8,128)(2,1)S(1)} %pad_maximum_fusion.3), channel_id=1, source_target_pairs={{0,4},{1,3},{2,6},{3,1},{4,0},{5,7},{6,2},{7,5},{8,12},{9,11},{10,... | collective-permute-start | bytes 786440 | tf_op jit(solution)/shard_map/ppermute | solution.py:452
  22.2 1.0 %collective-permute-done.8 = bf16[4,272,128]{2,1,0:T(8,128)(2,1)S(1)} collective-permute-done((bf16[4,272,128]{2,1,0:T(8,128)(2,1)S(1)}, bf16[4,272,128]{2,1,0:T(8,128)(2,1)S(1)}, u32[]{:S(2)}, u32[]{:S(2)}) %collective-permute-start.8) | collective-permute-done | bytes 278560 | tf_op jit(solution)/shard_map/ppermute | solution.py:452
  23.2 1.6 %collective-permute-start.9 = (bf16[8,272,128]{2,1,0:T(8,128)(2,1)S(1)}, bf16[8,272,128]{2,1,0:T(8,128)(2,1)S(1)}, u32[]{:S(2)}, u32[]{:S(2)}) collective-permute-start(bf16[8,272,128]{2,1,0:T(8,128)(2,1)S(1)} %pad_maximum_fusion.block0), channel_id=1, source_target_pairs={{0,2},{1,17},{2,0},{3,19},{4,6},{5,21},{6,4},{7,23},{8,10},{9,25},... | collective-permute-start | bytes 1671176 | tf_op jit(solution)/shard_map/ppermute | solution.py:452
  24.8 2.2 %collective-permute-done.2 = bf16[4,128,256]{2,1,0:T(8,128)(2,1)S(1)} collective-permute-done((bf16[4,128,256]{2,1,0:T(8,128)(2,1)S(1)}, bf16[4,128,256]{2,1,0:T(8,128)(2,1)S(1)}, u32[]{:S(2)}, u32[]{:S(2)}) %collective-permute-start.2) | collective-permute-done | bytes 262176 | tf_op jit(solution)/shard_map/ppermute | solution.py:452
  27.1 1.6 %collective-permute-start.3 = (bf16[8,128,256]{2,1,0:T(8,128)(2,1)S(1)}, bf16[8,128,256]{2,1,0:T(8,128)(2,1)S(1)}, u32[]{:S(2)}, u32[]{:S(2)}) collective-permute-start(bf16[8,128,256]{2,1,0:T(8,128)(2,1)S(1)} %pad_maximum_fusion.1.block0), channel_id=1, source_target_pairs={{0,2},{1,17},{2,0},{3,19},{4,6},{5,21},{6,4},{7,23},{8,10},{9,25},... | collective-permute-start | bytes 1572872 | tf_op jit(solution)/shard_map/ppermute | solution.py:452
  28.7 4.2 %collective-permute-done.9.block1 = bf16[8,272,128]{2,1,0:T(8,128)(2,1)S(1)} collective-permute-done((bf16[8,272,128]{2,1,0:T(8,128)(2,1)S(1)}, bf16[8,272,128]{2,1,0:T(8,128)(2,1)S(1)}, u32[]{:S(2)}, u32[]{:S(2)}) %collective-permute-start.9) | collective-permute-done | bytes 557088 | tf_op jit(solution)/shard_map/ppermute | solution.py:452
  32.8 0.5 collective-permute-start.4
  33.3 5.1 %collective-permute-done.3.block1 = bf16[8,128,256]{2,1,0:T(8,128)(2,1)S(1)} collective-permute-done((bf16[8,128,256]{2,1,0:T(8,128)(2,1)S(1)}, bf16[8,128,256]{2,1,0:T(8,128)(2,1)S(1)}, u32[]{:S(2)}, u32[]{:S(2)}) %collective-permute-start.3) | collective-permute-done | bytes 524320 | tf_op jit(solution)/shard_map/ppermute | solution.py:452
  38.5 10.6 %cotangent.1 = (bf16[128,256]{1,0:T(8,128)(2,1)}, bf16[4,128,2304]{2,1,0:T(8,128)(2,1)S(1)}, s32[32,128]{1,0:T(8,128)S(1)}, s32[32,256]{1,0:T(8,128)S(1)}, f32[32,256]{1,0:T(8,128)S(1)}) custom-call(s32[1,128]{1,0:T(1,128)S(1)} %copy-done.1, bf16[8,272,128]{2,1,0:T(8,128)(2,1)S(1)} %pad_maximum_fusion.block0, ...), custom_call_target="tpu_custom_call" | custom-call | tf_op jit(solution)/shard_map/cotangent/pallas_call | solution.py:495
  49.1 15.3 %scene.1 = (f32[10,10,8,256]{3,2,1,0:T(8,128)S(1)}, bf16[15,256,128]{2,1,0:T(8,128)(2,1)S(1)}, bf16[12,256,128]{2,1,0:T(8,128)(2,1)S(1)}) custom-call(bf16[8,128,256]{2,1,0:T(8,128)(2,1)S(1)} %pad_maximum_fusion.1.block0, bf16[8,128,256]{2,1,0:T(8,128)(2,1)S(1)} %collective-permute-done.3.block1, bf16[8,128,256]{2,1,0:T(8,128)(2,1)S(1)} %collective-permute-done.4.block2, ...), custom_call_target="tpu_custom_call" | custom-call | tf_op jit(solution)/shard_map/scene/pallas_call | solution.py:522
  64.4 0.6 collective-permute-start.12
  65.0 1.9 %collective-permute-done.12.received = bf16[12,256,128]{2,1,0:T(8,128)(2,1)S(1)} collective-permute-done((bf16[12,256,128]{2,1,0:T(8,128)(2,1)S(1)}, bf16[12,256,128]{2,1,0:T(8,128)(2,1)S(1)}, u32[]{:S(2)}, u32[]{:S(2)}) %collective-permute-start.12) | collective-permute-done | bytes 786464 | tf_op jit(solution)/shard_map/ppermute | solution.py:452
  66.9 3.1 %output.1 = (bf16[256,128]{1,0:T(8,128)(2,1)}, bf16[27,256,128]{2,1,0:T(8,128)(2,1)}) custom-call(f32[10,10,8,256]{3,2,1,0:T(8,128)S(1)} %get-tuple-element.20.padded, bf16[27,256,128]{2,1,0:T(8,128)(2,1)S(1)} %copy-done, s32[32,256]{1,0:T(8,128)S(1)} %get-tuple-element.19.spots, f32[32,256]{1,0:T(8,128)S(1)} %get-tuple-element.21.filled, ...), custom_call_target="tpu_custom_call" | custom-call | tf_op jit(solution)/shard_map/output/pallas_call | solution.py:545
  (18 shorter events, 0.2 us)
Async XLA Ops:
  0.6 26.4 %copy-start.2 = (bf16[128,256]{1,0:T(8,128)(2,1)S(1)}, bf16[128,256]{1,0:T(8,128)(2,1)}, u32[]{:S(2)}) copy-start(bf16[128,256]{1,0:T(8,128)(2,1)} %param.5) | copy-start | bytes 196612
  2.6 5.4 %collective-permute-start.6 = (bf16[1,272,128]{2,1,0:T(8,128)(2,1)}, bf16[1,272,128]{2,1,0:T(8,128)(2,1)S(1)}, u32[]{:S(2)}, u32[]{:S(2)}) collective-permute-start(bf16[1,272,128]{2,1,0:T(8,128)(2,1)} %bitcast.9), channel_id=1, source_target_pairs={{0,16},{1,9},{2,18},{3,11},{4,20},{5,13},{6,22},{7,15},{8,24},{9,1... | collective-permute-start | bytes 208904 | tf_op jit(solution)/shard_map/ppermute | solution.py:452
  5.5 6.6 %collective-permute-start = (bf16[1,128,256]{2,1,0:T(8,128)(2,1)}, bf16[1,128,256]{2,1,0:T(8,128)(2,1)S(1)}, u32[]{:S(2)}, u32[]{:S(2)}) collective-permute-start(bf16[1,128,256]{2,1,0:T(8,128)(2,1)} %bitcast.5), channel_id=1, source_target_pairs={{0,16},{1,9},{2,18},{3,11},{4,20},{5,13},{6,22},{7,15},{8,24},{9,1... | collective-permute-start | bytes 196616 | tf_op jit(solution)/shard_map/ppermute | solution.py:452
  8.9 29.6 %copy-start = (bf16[27,256,128]{2,1,0:T(8,128)(2,1)S(1)}, bf16[27,256,128]{2,1,0:T(8,128)(2,1)}, u32[]{:S(2)}) copy-start(bf16[27,256,128]{2,1,0:T(8,128)(2,1)} %weight.3) | copy-start | bytes 5308420
  8.9 29.6 %copy-start.1 = (s32[1,128]{1,0:T(1,128)S(1)}, s32[1,128]{1,0:T(1,128)}, u32[]{:S(2)}) copy-start(s32[1,128]{1,0:T(1,128)} %get-tuple-element.15.slot_ref) | copy-start | bytes 1540
  8.9 7.2 %collective-permute-start.7 = (bf16[2,272,128]{2,1,0:T(8,128)(2,1)S(1)}, bf16[2,272,128]{2,1,0:T(8,128)(2,1)S(1)}, u32[]{:S(2)}, u32[]{:S(2)}) collective-permute-start(bf16[2,272,128]{2,1,0:T(8,128)(2,1)S(1)} %pad_maximum_fusion.4), channel_id=1, source_target_pairs={{0,8},{1,5},{2,10},{3,7},{4,12},{5,1},{6,14},{7,3},{8,0},{9,13},{1... | collective-permute-start | bytes 417800 | tf_op jit(solution)/shard_map/ppermute | solution.py:452
  13.0 6.7 %collective-permute-start.1 = (bf16[2,128,256]{2,1,0:T(8,128)(2,1)S(1)}, bf16[2,128,256]{2,1,0:T(8,128)(2,1)S(1)}, u32[]{:S(2)}, u32[]{:S(2)}) collective-permute-start(bf16[2,128,256]{2,1,0:T(8,128)(2,1)S(1)} %pad_maximum_fusion.5), channel_id=1, source_target_pairs={{0,8},{1,5},{2,10},{3,7},{4,12},{5,1},{6,14},{7,3},{8,0},{9,13},{1... | collective-permute-start | bytes 393224 | tf_op jit(solution)/shard_map/ppermute | solution.py:452
  16.1 7.0 %collective-permute-start.8 = (bf16[4,272,128]{2,1,0:T(8,128)(2,1)S(1)}, bf16[4,272,128]{2,1,0:T(8,128)(2,1)S(1)}, u32[]{:S(2)}, u32[]{:S(2)}) collective-permute-start(bf16[4,272,128]{2,1,0:T(8,128)(2,1)S(1)} %pad_maximum_fusion.2), channel_id=1, source_target_pairs={{0,4},{1,3},{2,6},{3,1},{4,0},{5,7},{6,2},{7,5},{8,12},{9,11},{10,... | collective-permute-start | bytes 835592 | tf_op jit(solution)/shard_map/ppermute | solution.py:452
  20.6 6.4 %collective-permute-start.2 = (bf16[4,128,256]{2,1,0:T(8,128)(2,1)S(1)}, bf16[4,128,256]{2,1,0:T(8,128)(2,1)S(1)}, u32[]{:S(2)}, u32[]{:S(2)}) collective-permute-start(bf16[4,128,256]{2,1,0:T(8,128)(2,1)S(1)} %pad_maximum_fusion.3), channel_id=1, source_target_pairs={{0,4},{1,3},{2,6},{3,1},{4,0},{5,7},{6,2},{7,5},{8,12},{9,11},{10,... | collective-permute-start | bytes 786440 | tf_op jit(solution)/shard_map/ppermute | solution.py:452
  23.2 9.6 %collective-permute-start.9 = (bf16[8,272,128]{2,1,0:T(8,128)(2,1)S(1)}, bf16[8,272,128]{2,1,0:T(8,128)(2,1)S(1)}, u32[]{:S(2)}, u32[]{:S(2)}) collective-permute-start(bf16[8,272,128]{2,1,0:T(8,128)(2,1)S(1)} %pad_maximum_fusion.block0), channel_id=1, source_target_pairs={{0,2},{1,17},{2,0},{3,19},{4,6},{5,21},{6,4},{7,23},{8,10},{9,25},... | collective-permute-start | bytes 1671176 | tf_op jit(solution)/shard_map/ppermute | solution.py:452
  27.1 11.4 %collective-permute-start.3 = (bf16[8,128,256]{2,1,0:T(8,128)(2,1)S(1)}, bf16[8,128,256]{2,1,0:T(8,128)(2,1)S(1)}, u32[]{:S(2)}, u32[]{:S(2)}) collective-permute-start(bf16[8,128,256]{2,1,0:T(8,128)(2,1)S(1)} %pad_maximum_fusion.1.block0), channel_id=1, source_target_pairs={{0,2},{1,17},{2,0},{3,19},{4,6},{5,21},{6,4},{7,23},{8,10},{9,25},... | collective-permute-start | bytes 1572872 | tf_op jit(solution)/shard_map/ppermute | solution.py:452
  28.7 9.8 %collective-permute-start.10 = (bf16[8,272,128]{2,1,0:T(8,128)(2,1)S(1)}, bf16[8,272,128]{2,1,0:T(8,128)(2,1)S(1)}, u32[]{:S(2)}, u32[]{:S(2)}) collective-permute-start(bf16[8,272,128]{2,1,0:T(8,128)(2,1)S(1)} %pad_maximum_fusion.block0), channel_id=1, source_target_pairs={{0,1},{1,0},{2,3},{3,2},{4,5},{5,4},{6,7},{7,6},{8,9},{9,8},{10,11... | collective-permute-start | bytes 1671176 | tf_op jit(solution)/shard_map/ppermute | solution.py:452
  32.8 5.6 %collective-permute-start.11 = (bf16[8,272,128]{2,1,0:T(8,128)(2,1)S(1)}, bf16[8,272,128]{2,1,0:T(8,128)(2,1)S(1)}, u32[]{:S(2)}, u32[]{:S(2)}) collective-permute-start(bf16[8,272,128]{2,1,0:T(8,128)(2,1)S(1)} %collective-permute-done.9.block1), channel_id=1, source_target_pairs={{0,1},{1,0},{2,3},{3,2},{4,5},{5,4},{6,7},{7,6},{8,9},{9,8},{10,11... | collective-permute-start | bytes 1671176 | tf_op jit(solution)/shard_map/ppermute | solution.py:452
  32.8 16.3 %collective-permute-start.4 = (bf16[8,128,256]{2,1,0:T(8,128)(2,1)S(1)}, bf16[8,128,256]{2,1,0:T(8,128)(2,1)S(1)}, u32[]{:S(2)}, u32[]{:S(2)}) collective-permute-start(bf16[8,128,256]{2,1,0:T(8,128)(2,1)S(1)} %pad_maximum_fusion.1.block0), channel_id=1, source_target_pairs={{0,1},{1,0},{2,3},{3,2},{4,5},{5,4},{6,7},{7,6},{8,9},{9,8},{10,11... | collective-permute-start | bytes 1572872 | tf_op jit(solution)/shard_map/ppermute | solution.py:452
  38.4 10.7 %collective-permute-start.5 = (bf16[8,128,256]{2,1,0:T(8,128)(2,1)S(1)}, bf16[8,128,256]{2,1,0:T(8,128)(2,1)S(1)}, u32[]{:S(2)}, u32[]{:S(2)}) collective-permute-start(bf16[8,128,256]{2,1,0:T(8,128)(2,1)S(1)} %collective-permute-done.3.block1), channel_id=1, source_target_pairs={{0,1},{1,0},{2,3},{3,2},{4,5},{5,4},{6,7},{7,6},{8,9},{9,8},{10,11... | collective-permute-start | bytes 1572872 | tf_op jit(solution)/shard_map/ppermute | solution.py:452
  64.4 2.5 %collective-permute-start.12 = (bf16[12,256,128]{2,1,0:T(8,128)(2,1)S(1)}, bf16[12,256,128]{2,1,0:T(8,128)(2,1)S(1)}, u32[]{:S(2)}, u32[]{:S(2)}) collective-permute-start(bf16[12,256,128]{2,1,0:T(8,128)(2,1)S(1)} %get-tuple-element.23), channel_id=1, source_target_pairs={{0,1},{1,0},{2,3},{3,2},{4,5},{5,4},{6,7},{7,6},{8,9},{9,8},{10,11... | collective-permute-start | bytes 2359304 | tf_op jit(solution)/shard_map/ppermute | solution.py:452

commit v6 on v5

--- a/solution.py
+++ b/solution.py
@@ -443,8 +443,8 @@
 
 
 def exchange_masks(count):
-    even = [1 << i for i in range(count.bit_length() - 2, 0, -1)]
-    return even, even[1:] + even[:1]
+    far, mid, near, last = (count >> i for i in range(1, 5))
+    return (mid, far, near, last), (near, mid, last, far)
 
 
 def swap(value, count, masks):

time: 71.4 us -> 69.9 us (0.979)
  waiting for transfers between devices: 20.5 us -> 18.8 us
  starting transfers between devices: 15 us -> 15.9 us
    ppermute x13, waiting for transfers between devices: 20.5 us -> 18.8 us  [swap(): return lax.ppermute(value, ('grp', 'blk'), pairs)]
    ppermute x13, starting transfers between devices: 15 us -> 15.9 us  [swap(): return lax.ppermute(value, ('grp', 'blk'), pairs)]
  transfers between devices with their start and end apart: 13 -> 13, of which waited for: 8 -> 9; matrix products, arithmetic and copies ran while one was open for 4% -> 4% of each run, Pallas kernels for 15% -> 15%
where the time goes in v6:
time: 69.9 us; the launch traced here: 69.4 us
  Pallas kernels  30.9 us (44%)
  waiting for transfers between devices  18.8 us (27%)
  starting transfers between devices  15.9 us (23%)
  other arithmetic  2.75 us (4%)
  between operations  0.9 us (1%)
    ppermute x13, waiting for transfers between devices, swap(): return lax.ppermute(value, ('grp', 'blk'), pairs)  18.8 us
    ppermute x13, starting transfers between devices, swap(): return lax.ppermute(value, ('grp', 'blk'), pairs)  15.9 us
    pallas_call x1, Pallas kernels, gathered_shards(): pl.pallas_call(functools.partial(scene_kernel, dims + (scale,)), out_shap...  15.3 us
    pallas_call x1, Pallas kernels, gathered_shards(): pl.pallas_call(functools.partial(cotangent_kernel, dims), out_shape=(jax....  10.6 us
    pallas_call x1, Pallas kernels, gathered_shards(): pl.pallas_call(functools.partial(output_kernel, sizes), out_shape=(jax.Sh...  3.11 us
    concatenate x6, other arithmetic, gather_all(): jnp.concatenate([held, swap(held, count, (even[step], odd[step]))], axis=0)  2.75 us
    pallas_call x1, Pallas kernels, gathered_shards(): pl.pallas_call(functools.partial(pack_kernel, sizes, cap), out_shape=(jax...  1.91 us
  transfers between devices with their start and end apart: 13, of which 9 were waited for; matrix products, arithmetic and copies ran while one was open for 4% of the time, Pallas kernels for 15%

profile of v6, /device:TPU:0, one launch (start us, length us, event | category | flops | bytes accessed | tf_op | source)
XLA Modules:
  0.0 69.4 jit_solution(5144851074947712626)
XLA Ops:
  0.6 1.9 %pack.1 = (bf16[272,128]{1,0:T(8,128)(2,1)}, s32[1,128]{1,0:T(1,128)}) custom-call(s32[1,128]{1,0:T(1,128)} %bitcast.12, s32[1,256]{1,0:T(1,128)} %placement.1, bf16[256,128]{1,0:T(8,128)(2,1)} %bitcast.11), custom_call_target="tpu_custom_call" | custom-call | tf_op jit(solution)/shard_map/pack/pallas_call | solution.py:482
  2.6 4.0 %collective-permute-start.6 = (bf16[1,272,128]{2,1,0:T(8,128)(2,1)}, bf16[1,272,128]{2,1,0:T(8,128)(2,1)S(1)}, u32[]{:S(2)}, u32[]{:S(2)}) collective-permute-start(bf16[1,272,128]{2,1,0:T(8,128)(2,1)} %bitcast.9), channel_id=1, source_target_pairs={{0,8},{1,5},{2,10},{3,7},{4,12},{5,1},{6,14},{7,3},{8,0},{9,13},{1... | collective-permute-start | bytes 208904 | tf_op jit(solution)/shard_map/ppermute | solution.py:452
  6.6 2.6 %collective-permute-done.6 = bf16[1,272,128]{2,1,0:T(8,128)(2,1)S(1)} collective-permute-done((bf16[1,272,128]{2,1,0:T(8,128)(2,1)}, bf16[1,272,128]{2,1,0:T(8,128)(2,1)S(1)}, u32[]{:S(2)}, u32[]{:S(2)}) %collective-permute-start.6) | collective-permute-done | bytes 69664 | tf_op jit(solution)/shard_map/ppermute | solution.py:452
  9.2 0.9 %pad_maximum_fusion.4 = bf16[2,272,128]{2,1,0:T(8,128)(2,1)S(1)} fusion(bf16[1,272,128]{2,1,0:T(8,128)(2,1)S(1)} %collective-permute-done.6, bf16[1,272,128]{2,1,0:T(8,128)(2,1)} %bitcast.10), kind=kLoop, calls=%fused_computation.4 | loop fusion | flops 69632 | bytes 278528 | tf_op jit(solution)/shard_map/concatenate | solution.py:463
  10.1 1.8 %collective-permute-start.7 = (bf16[2,272,128]{2,1,0:T(8,128)(2,1)S(1)}, bf16[2,272,128]{2,1,0:T(8,128)(2,1)S(1)}, u32[]{:S(2)}, u32[]{:S(2)}) collective-permute-start(bf16[2,272,128]{2,1,0:T(8,128)(2,1)S(1)} %pad_maximum_fusion.4), channel_id=1, source_target_pairs={{0,16},{1,9},{2,18},{3,11},{4,20},{5,13},{6,22},{7,15},{8,24},{9,1... | collective-permute-start | bytes 417800 | tf_op jit(solution)/shard_map/ppermute | solution.py:452
  12.4 0.9 %pad_maximum_fusion.5 = bf16[2,128,256]{2,1,0:T(8,128)(2,1)S(1)} fusion(bf16[1,128,256]{2,1,0:T(8,128)(2,1)S(1)} %collective-permute-done, bf16[1,128,256]{2,1,0:T(8,128)(2,1)} %bitcast.6), kind=kLoop, calls=%fused_computation.5 | loop fusion | flops 65536 | bytes 262144 | tf_op jit(solution)/shard_map/concatenate | solution.py:463
  13.2 1.5 %collective-permute-start.1 = (bf16[2,128,256]{2,1,0:T(8,128)(2,1)S(1)}, bf16[2,128,256]{2,1,0:T(8,128)(2,1)S(1)}, u32[]{:S(2)}, u32[]{:S(2)}) collective-permute-start(bf16[2,128,256]{2,1,0:T(8,128)(2,1)S(1)} %pad_maximum_fusion.5), channel_id=1, source_target_pairs={{0,16},{1,9},{2,18},{3,11},{4,20},{5,13},{6,22},{7,15},{8,24},{9,1... | collective-permute-start | bytes 393224 | tf_op jit(solution)/shard_map/ppermute | solution.py:452
  14.7 0.5 collective-permute-done.7
  15.3 2.5 %collective-permute-start.8 = (bf16[4,272,128]{2,1,0:T(8,128)(2,1)S(1)}, bf16[4,272,128]{2,1,0:T(8,128)(2,1)S(1)}, u32[]{:S(2)}, u32[]{:S(2)}) collective-permute-start(bf16[4,272,128]{2,1,0:T(8,128)(2,1)S(1)} %pad_maximum_fusion.2), channel_id=1, source_target_pairs={{0,4},{1,3},{2,6},{3,1},{4,0},{5,7},{6,2},{7,5},{8,12},{9,11},{10,... | collective-permute-start | bytes 835592 | tf_op jit(solution)/shard_map/ppermute | solution.py:452
  17.8 0.5 collective-permute-done.1
  18.3 0.9 %pad_maximum_fusion.3 = bf16[4,128,256]{2,1,0:T(8,128)(2,1)S(1)} fusion(bf16[2,128,256]{2,1,0:T(8,128)(2,1)S(1)} %collective-permute-done.1, bf16[1,128,256]{2,1,0:T(8,128)(2,1)S(1)} %collective-permute-done, bf16[1,128,256]{2,1,0:T(8,128)(2,1)} %bitcast.7), kind=kLoop, calls=%fused_computation.3 | loop fusion | flops 262144 | bytes 524288 | tf_op jit(solution)/shard_map/concatenate | solution.py:463
  19.1 1.8 %collective-permute-start.2 = (bf16[4,128,256]{2,1,0:T(8,128)(2,1)S(1)}, bf16[4,128,256]{2,1,0:T(8,128)(2,1)S(1)}, u32[]{:S(2)}, u32[]{:S(2)}) collective-permute-start(bf16[4,128,256]{2,1,0:T(8,128)(2,1)S(1)} %pad_maximum_fusion.3), channel_id=1, source_target_pairs={{0,4},{1,3},{2,6},{3,1},{4,0},{5,7},{6,2},{7,5},{8,12},{9,11},{10,... | collective-permute-start | bytes 786440 | tf_op jit(solution)/shard_map/ppermute | solution.py:452
  21.0 1.4 %collective-permute-done.8 = bf16[4,272,128]{2,1,0:T(8,128)(2,1)S(1)} collective-permute-done((bf16[4,272,128]{2,1,0:T(8,128)(2,1)S(1)}, bf16[4,272,128]{2,1,0:T(8,128)(2,1)S(1)}, u32[]{:S(2)}, u32[]{:S(2)}) %collective-permute-start.8) | collective-permute-done | bytes 278560 | tf_op jit(solution)/shard_map/ppermute | solution.py:452
  22.4 1.6 %collective-permute-start.9 = (bf16[8,272,128]{2,1,0:T(8,128)(2,1)S(1)}, bf16[8,272,128]{2,1,0:T(8,128)(2,1)S(1)}, u32[]{:S(2)}, u32[]{:S(2)}) collective-permute-start(bf16[8,272,128]{2,1,0:T(8,128)(2,1)S(1)} %pad_maximum_fusion.block0), channel_id=1, source_target_pairs={{0,2},{1,17},{2,0},{3,19},{4,6},{5,21},{6,4},{7,23},{8,10},{9,25},... | collective-permute-start | bytes 1671176 | tf_op jit(solution)/shard_map/ppermute | solution.py:452
  24.0 1.6 %collective-permute-done.2 = bf16[4,128,256]{2,1,0:T(8,128)(2,1)S(1)} collective-permute-done((bf16[4,128,256]{2,1,0:T(8,128)(2,1)S(1)}, bf16[4,128,256]{2,1,0:T(8,128)(2,1)S(1)}, u32[]{:S(2)}, u32[]{:S(2)}) %collective-permute-start.2) | collective-permute-done | bytes 262176 | tf_op jit(solution)/shard_map/ppermute | solution.py:452
  25.6 1.5 %collective-permute-start.3 = (bf16[8,128,256]{2,1,0:T(8,128)(2,1)S(1)}, bf16[8,128,256]{2,1,0:T(8,128)(2,1)S(1)}, u32[]{:S(2)}, u32[]{:S(2)}) collective-permute-start(bf16[8,128,256]{2,1,0:T(8,128)(2,1)S(1)} %pad_maximum_fusion.1.block0), channel_id=1, source_target_pairs={{0,2},{1,17},{2,0},{3,19},{4,6},{5,21},{6,4},{7,23},{8,10},{9,25},... | collective-permute-start | bytes 1572872 | tf_op jit(solution)/shard_map/ppermute | solution.py:452
  27.2 4.8 %collective-permute-done.9.block1 = bf16[8,272,128]{2,1,0:T(8,128)(2,1)S(1)} collective-permute-done((bf16[8,272,128]{2,1,0:T(8,128)(2,1)S(1)}, bf16[8,272,128]{2,1,0:T(8,128)(2,1)S(1)}, u32[]{:S(2)}, u32[]{:S(2)}) %collective-permute-start.9) | collective-permute-done | bytes 557088 | tf_op jit(solution)/shard_map/ppermute | solution.py:452
  32.0 0.5 collective-permute-start.4
  32.5 5.1 %collective-permute-done.3.block1 = bf16[8,128,256]{2,1,0:T(8,128)(2,1)S(1)} collective-permute-done((bf16[8,128,256]{2,1,0:T(8,128)(2,1)S(1)}, bf16[8,128,256]{2,1,0:T(8,128)(2,1)S(1)}, u32[]{:S(2)}, u32[]{:S(2)}) %collective-permute-start.3) | collective-permute-done | bytes 524320 | tf_op jit(solution)/shard_map/ppermute | solution.py:452
  37.6 10.6 %cotangent.1 = (bf16[128,256]{1,0:T(8,128)(2,1)}, bf16[4,128,2304]{2,1,0:T(8,128)(2,1)S(1)}, s32[32,128]{1,0:T(8,128)S(1)}, s32[32,256]{1,0:T(8,128)S(1)}, f32[32,256]{1,0:T(8,128)S(1)}) custom-call(s32[1,128]{1,0:T(1,128)S(1)} %copy-done.1, bf16[8,272,128]{2,1,0:T(8,128)(2,1)S(1)} %pad_maximum_fusion.block0, ...), custom_call_target="tpu_custom_call" | custom-call | tf_op jit(solution)/shard_map/cotangent/pallas_call | solution.py:495
  48.3 15.3 %scene.1 = (f32[10,10,8,256]{3,2,1,0:T(8,128)S(1)}, bf16[15,256,128]{2,1,0:T(8,128)(2,1)S(1)}, bf16[12,256,128]{2,1,0:T(8,128)(2,1)S(1)}) custom-call(bf16[8,128,256]{2,1,0:T(8,128)(2,1)S(1)} %pad_maximum_fusion.1.block0, bf16[8,128,256]{2,1,0:T(8,128)(2,1)S(1)} %collective-permute-done.3.block1, bf16[8,128,256]{2,1,0:T(8,128)(2,1)S(1)} %collective-permute-done.4.block2, ...), custom_call_target="tpu_custom_call" | custom-call | tf_op jit(solution)/shard_map/scene/pallas_call | solution.py:522
  63.6 0.6 collective-permute-start.12
  64.2 1.9 %collective-permute-done.12.received = bf16[12,256,128]{2,1,0:T(8,128)(2,1)S(1)} collective-permute-done((bf16[12,256,128]{2,1,0:T(8,128)(2,1)S(1)}, bf16[12,256,128]{2,1,0:T(8,128)(2,1)S(1)}, u32[]{:S(2)}, u32[]{:S(2)}) %collective-permute-start.12) | collective-permute-done | bytes 786464 | tf_op jit(solution)/shard_map/ppermute | solution.py:452
  66.1 3.1 %output.1 = (bf16[256,128]{1,0:T(8,128)(2,1)}, bf16[27,256,128]{2,1,0:T(8,128)(2,1)}) custom-call(f32[10,10,8,256]{3,2,1,0:T(8,128)S(1)} %get-tuple-element.20.padded, bf16[27,256,128]{2,1,0:T(8,128)(2,1)S(1)} %copy-done, s32[32,256]{1,0:T(8,128)S(1)} %get-tuple-element.19.spots, f32[32,256]{1,0:T(8,128)S(1)} %get-tuple-element.21.filled, ...), custom_call_target="tpu_custom_call" | custom-call | tf_op jit(solution)/shard_map/output/pallas_call | solution.py:545
  (18 shorter events, 0.7 us)
Async XLA Ops:
  0.6 25.0 %copy-start.2 = (bf16[128,256]{1,0:T(8,128)(2,1)S(1)}, bf16[128,256]{1,0:T(8,128)(2,1)}, u32[]{:S(2)}) copy-start(bf16[128,256]{1,0:T(8,128)(2,1)} %param.5) | copy-start | bytes 196612
  2.6 6.6 %collective-permute-start.6 = (bf16[1,272,128]{2,1,0:T(8,128)(2,1)}, bf16[1,272,128]{2,1,0:T(8,128)(2,1)S(1)}, u32[]{:S(2)}, u32[]{:S(2)}) collective-permute-start(bf16[1,272,128]{2,1,0:T(8,128)(2,1)} %bitcast.9), channel_id=1, source_target_pairs={{0,8},{1,5},{2,10},{3,7},{4,12},{5,1},{6,14},{7,3},{8,0},{9,13},{1... | collective-permute-start | bytes 208904 | tf_op jit(solution)/shard_map/ppermute | solution.py:452
  6.6 5.8 %collective-permute-start = (bf16[1,128,256]{2,1,0:T(8,128)(2,1)}, bf16[1,128,256]{2,1,0:T(8,128)(2,1)S(1)}, u32[]{:S(2)}, u32[]{:S(2)}) collective-permute-start(bf16[1,128,256]{2,1,0:T(8,128)(2,1)} %bitcast.5), channel_id=1, source_target_pairs={{0,8},{1,5},{2,10},{3,7},{4,12},{5,1},{6,14},{7,3},{8,0},{9,13},{1... | collective-permute-start | bytes 196616 | tf_op jit(solution)/shard_map/ppermute | solution.py:452
  10.1 27.5 %copy-start = (bf16[27,256,128]{2,1,0:T(8,128)(2,1)S(1)}, bf16[27,256,128]{2,1,0:T(8,128)(2,1)}, u32[]{:S(2)}) copy-start(bf16[27,256,128]{2,1,0:T(8,128)(2,1)} %weight.3) | copy-start | bytes 5308420
  10.1 27.5 %copy-start.1 = (s32[1,128]{1,0:T(1,128)S(1)}, s32[1,128]{1,0:T(1,128)}, u32[]{:S(2)}) copy-start(s32[1,128]{1,0:T(1,128)} %get-tuple-element.15.slot_ref) | copy-start | bytes 1540
  10.1 5.1 %collective-permute-start.7 = (bf16[2,272,128]{2,1,0:T(8,128)(2,1)S(1)}, bf16[2,272,128]{2,1,0:T(8,128)(2,1)S(1)}, u32[]{:S(2)}, u32[]{:S(2)}) collective-permute-start(bf16[2,272,128]{2,1,0:T(8,128)(2,1)S(1)} %pad_maximum_fusion.4), channel_id=1, source_target_pairs={{0,16},{1,9},{2,18},{3,11},{4,20},{5,13},{6,22},{7,15},{8,24},{9,1... | collective-permute-start | bytes 417800 | tf_op jit(solution)/shard_map/ppermute | solution.py:452
  13.2 5.0 %collective-permute-start.1 = (bf16[2,128,256]{2,1,0:T(8,128)(2,1)S(1)}, bf16[2,128,256]{2,1,0:T(8,128)(2,1)S(1)}, u32[]{:S(2)}, u32[]{:S(2)}) collective-permute-start(bf16[2,128,256]{2,1,0:T(8,128)(2,1)S(1)} %pad_maximum_fusion.5), channel_id=1, source_target_pairs={{0,16},{1,9},{2,18},{3,11},{4,20},{5,13},{6,22},{7,15},{8,24},{9,1... | collective-permute-start | bytes 393224 | tf_op jit(solution)/shard_map/ppermute | solution.py:452
  15.3 7.0 %collective-permute-start.8 = (bf16[4,272,128]{2,1,0:T(8,128)(2,1)S(1)}, bf16[4,272,128]{2,1,0:T(8,128)(2,1)S(1)}, u32[]{:S(2)}, u32[]{:S(2)}) collective-permute-start(bf16[4,272,128]{2,1,0:T(8,128)(2,1)S(1)} %pad_maximum_fusion.2), channel_id=1, source_target_pairs={{0,4},{1,3},{2,6},{3,1},{4,0},{5,7},{6,2},{7,5},{8,12},{9,11},{10,... | collective-permute-start | bytes 835592 | tf_op jit(solution)/shard_map/ppermute | solution.py:452
  19.1 6.4 %collective-permute-start.2 = (bf16[4,128,256]{2,1,0:T(8,128)(2,1)S(1)}, bf16[4,128,256]{2,1,0:T(8,128)(2,1)S(1)}, u32[]{:S(2)}, u32[]{:S(2)}) collective-permute-start(bf16[4,128,256]{2,1,0:T(8,128)(2,1)S(1)} %pad_maximum_fusion.3), channel_id=1, source_target_pairs={{0,4},{1,3},{2,6},{3,1},{4,0},{5,7},{6,2},{7,5},{8,12},{9,11},{10,... | collective-permute-start | bytes 786440 | tf_op jit(solution)/shard_map/ppermute | solution.py:452
  22.4 9.6 %collective-permute-start.9 = (bf16[8,272,128]{2,1,0:T(8,128)(2,1)S(1)}, bf16[8,272,128]{2,1,0:T(8,128)(2,1)S(1)}, u32[]{:S(2)}, u32[]{:S(2)}) collective-permute-start(bf16[8,272,128]{2,1,0:T(8,128)(2,1)S(1)} %pad_maximum_fusion.block0), channel_id=1, source_target_pairs={{0,2},{1,17},{2,0},{3,19},{4,6},{5,21},{6,4},{7,23},{8,10},{9,25},... | collective-permute-start | bytes 1671176 | tf_op jit(solution)/shard_map/ppermute | solution.py:452
  25.6 11.9 %collective-permute-start.3 = (bf16[8,128,256]{2,1,0:T(8,128)(2,1)S(1)}, bf16[8,128,256]{2,1,0:T(8,128)(2,1)S(1)}, u32[]{:S(2)}, u32[]{:S(2)}) collective-permute-start(bf16[8,128,256]{2,1,0:T(8,128)(2,1)S(1)} %pad_maximum_fusion.1.block0), channel_id=1, source_target_pairs={{0,2},{1,17},{2,0},{3,19},{4,6},{5,21},{6,4},{7,23},{8,10},{9,25},... | collective-permute-start | bytes 1572872 | tf_op jit(solution)/shard_map/ppermute | solution.py:452
  27.2 10.4 %collective-permute-start.10 = (bf16[8,272,128]{2,1,0:T(8,128)(2,1)S(1)}, bf16[8,272,128]{2,1,0:T(8,128)(2,1)S(1)}, u32[]{:S(2)}, u32[]{:S(2)}) collective-permute-start(bf16[8,272,128]{2,1,0:T(8,128)(2,1)S(1)} %pad_maximum_fusion.block0), channel_id=1, source_target_pairs={{0,1},{1,0},{2,3},{3,2},{4,5},{5,4},{6,7},{7,6},{8,9},{9,8},{10,11... | collective-permute-start | bytes 1671176 | tf_op jit(solution)/shard_map/ppermute | solution.py:452
  32.0 5.6 %collective-permute-start.11 = (bf16[8,272,128]{2,1,0:T(8,128)(2,1)S(1)}, bf16[8,272,128]{2,1,0:T(8,128)(2,1)S(1)}, u32[]{:S(2)}, u32[]{:S(2)}) collective-permute-start(bf16[8,272,128]{2,1,0:T(8,128)(2,1)S(1)} %collective-permute-done.9.block1), channel_id=1, source_target_pairs={{0,1},{1,0},{2,3},{3,2},{4,5},{5,4},{6,7},{7,6},{8,9},{9,8},{10,11... | collective-permute-start | bytes 1671176 | tf_op jit(solution)/shard_map/ppermute | solution.py:452
  32.0 16.3 %collective-permute-start.4 = (bf16[8,128,256]{2,1,0:T(8,128)(2,1)S(1)}, bf16[8,128,256]{2,1,0:T(8,128)(2,1)S(1)}, u32[]{:S(2)}, u32[]{:S(2)}) collective-permute-start(bf16[8,128,256]{2,1,0:T(8,128)(2,1)S(1)} %pad_maximum_fusion.1.block0), channel_id=1, source_target_pairs={{0,1},{1,0},{2,3},{3,2},{4,5},{5,4},{6,7},{7,6},{8,9},{9,8},{10,11... | collective-permute-start | bytes 1572872 | tf_op jit(solution)/shard_map/ppermute | solution.py:452
  37.6 10.7 %collective-permute-start.5 = (bf16[8,128,256]{2,1,0:T(8,128)(2,1)S(1)}, bf16[8,128,256]{2,1,0:T(8,128)(2,1)S(1)}, u32[]{:S(2)}, u32[]{:S(2)}) collective-permute-start(bf16[8,128,256]{2,1,0:T(8,128)(2,1)S(1)} %collective-permute-done.3.block1), channel_id=1, source_target_pairs={{0,1},{1,0},{2,3},{3,2},{4,5},{5,4},{6,7},{7,6},{8,9},{9,8},{10,11... | collective-permute-start | bytes 1572872 | tf_op jit(solution)/shard_map/ppermute | solution.py:452
  63.6 2.5 %collective-permute-start.12 = (bf16[12,256,128]{2,1,0:T(8,128)(2,1)S(1)}, bf16[12,256,128]{2,1,0:T(8,128)(2,1)S(1)}, u32[]{:S(2)}, u32[]{:S(2)}) collective-permute-start(bf16[12,256,128]{2,1,0:T(8,128)(2,1)S(1)} %get-tuple-element.23), channel_id=1, source_target_pairs={{0,1},{1,0},{2,3},{3,2},{4,5},{5,4},{6,7},{7,6},{8,9},{9,8},{10,11... | collective-permute-start | bytes 2359304 | tf_op jit(solution)/shard_map/ppermute | solution.py:452
